TPU v7x, 32 devices: a whole 2x2x4 slice. The times are simulated.
32 devices in a mesh: gx: 2 (over x), gy: 4 (over y, core), gz: 4 (over z).
Axes of the slice: x: 2, y: 2, z: 4, core: 2. Of those that a mesh axis runs over, the one named last changes fastest.
Arguments:
- panel: float32 [64, 16, 32, 512], P(None, 'gx', 'gy', 'gz')
- potential: float32 [16, 32, 512], P('gx', 'gy', 'gz'), may hold values from -10 to 10
- atom_corner: int32 [256, 3], P(('gx', 'gy', 'gz')), may hold values from 0 to 508, as said below
- proj_index: int32 [256, 64], P(('gx', 'gy', 'gz')), may hold values from 0 to 63, each once within a row
- projectors: float32 [256, 8, 64], P(('gx', 'gy', 'gz')), may hold values from -3 to 3
- couplings: float32 [256, 8], P(('gx', 'gy', 'gz')), may hold values from 0.5 to 8
Outputs:
- filtered: float32 [64, 16, 32, 512], P(None, 'gx', 'gy', 'gz')
- gram: float32 [64, 64], P('gz')
Inputs may be any that keep to these rules, and one draw needn't show every extreme that they name: `atom_corner`: each atom's tile of 4 x 4 x 4 cells lies inside the domain of the device that holds the atom's row (rows of 8 atoms a device, devices in the order gx, gy, gz); tiles of different atoms may intersect.
All inputs are finite; a program needn't handle non-finite values.
Results may differ from a plain program's by a relative error of at most 0.0001.
Values sent between devices are 32-bit elements; how exact they have to be, the bound alone decides.
No kernel may reach another device: no remote copies, remote signals or barrier semaphores. Data moves between devices by JAX's collectives and lax.ppermute only.
A program may use at most 128 MiB of HBM per device.

v0:
```python
import jax
import jax.numpy as jnp
from jax import lax
from jax.sharding import PartitionSpec as P

DEGREE = 4


STENCIL = (
    -5369.0 / 1800.0,
    12.0 / 7.0,
    -15.0 / 56.0,
    10.0 / 189.0,
    -1.0 / 112.0,
    2.0 / 1925.0,
    -1.0 / 16632.0,
)
SPACING = 0.224
CENTER = 210.5
HALF = 209.5


def extended(array, sides, width):
    for axis, dim in sides:
        size, length = (lax.axis_size(axis), array.shape[dim])
        up = [(i, (i + 1) % size) for i in range(size)]
        down = [(j, i) for i, j in up]
        last = lax.slice_in_dim(array, length - width, length, axis=dim)
        leading = lax.slice_in_dim(array, 0, width, axis=dim)
        before = lax.ppermute(last, axis, up)
        after = lax.ppermute(leading, axis, down)
        array = jnp.concatenate([before, array, after], axis=dim)
    return array


def tile_points(corner, order, size_y, size_z):
    off_x = order // 16
    off_y = order // 4 % 4
    off_z = order % 4
    pos_x = corner[:, 0:1] + off_x
    pos_y = corner[:, 1:2] + off_y
    pos_z = corner[:, 2:3] + off_z
    return (pos_x * size_y + pos_y) * size_z + pos_z


def nonlocal_part(field, points, projectors, couplings):
    bands = field.shape[0]
    field_flat = field.reshape(bands, -1)
    taken = field_flat[:, points]
    coeffs = (
        jnp.einsum("ajp,bap->baj", projectors, taken, precision=lax.Precision.HIGHEST)
        * couplings[None]
    )
    spread = jnp.einsum("ajp,baj->bap", projectors, coeffs, precision=lax.Precision.HIGHEST)
    return jnp.zeros_like(field_flat).at[:, points].add(spread).reshape(field.shape)


def axis_terms(padded, axis_dim, length):
    total = None
    for offset in range(1, 7):
        upper = lax.slice_in_dim(padded, 6 + offset, 6 + offset + length, 1, axis_dim)
        lower = lax.slice_in_dim(padded, 6 - offset, 6 - offset + length, 1, axis_dim)
        term = STENCIL[offset] * (upper + lower)
        total = term if total is None else total + term
    return total


def laplace(field):
    size_x, size_y, size_z = (field.shape[1], field.shape[2], field.shape[3])
    slab_x = extended(field, (("gx", 1),), 6)
    slab_y = extended(field, (("gy", 2),), 6)
    slab_z = extended(field, (("gz", 3),), 6)
    summed = 3.0 * STENCIL[0] * field
    summed = summed + axis_terms(slab_x, 1, size_x)
    summed = summed + axis_terms(slab_y, 2, size_y)
    summed = summed + axis_terms(slab_z, 3, size_z)
    return summed / (SPACING * SPACING)


def hamiltonian(field, potential, points, projectors, couplings):
    kinetic = -0.5 * laplace(field)
    return kinetic + potential[None] * field + nonlocal_part(field, points, projectors, couplings)


def shards(panel, potential, atom_corner, proj_index, projectors, couplings):
    bands, size_x, size_y, size_z = panel.shape
    anchor = jnp.stack(
        [
            lax.axis_index("gx") * size_x,
            lax.axis_index("gy") * size_y,
            lax.axis_index("gz") * size_z,
        ]
    )
    local_corner = atom_corner - anchor[None, :]
    points = tile_points(local_corner, proj_index, size_y, size_z)
    previous = panel
    image = hamiltonian(panel, potential, points, projectors, couplings)
    current = (image - CENTER * panel) / HALF
    for degree_step in range(DEGREE - 1):
        image = hamiltonian(current, potential, points, projectors, couplings)
        following = 2.0 * (image - CENTER * current) / HALF - previous
        previous = current
        current = following
    field_flat = current.reshape(bands, -1)
    total_cells = (
        field_flat.shape[1] * lax.axis_size("gx") * lax.axis_size("gy") * lax.axis_size("gz")
    )
    share = lax.psum_scatter(
        jnp.einsum("bc,dc->bd", field_flat, field_flat, precision=lax.Precision.HIGHEST),
        "gz",
        scatter_dimension=0,
        tiled=True,
    )
    gram = lax.psum(share, ("gx", "gy"))
    return (current, gram / total_cells)


def solution(mesh):
    placed = (
        P(None, "gx", "gy", "gz"),
        P("gx", "gy", "gz"),
        P(("gx", "gy", "gz"), None),
        P(("gx", "gy", "gz"), None),
        P(("gx", "gy", "gz"), None, None),
        P(("gx", "gy", "gz"), None),
    )
    return jax.shard_map(
        shards,
        mesh=mesh,
        in_specs=placed,
        out_specs=(P(None, "gx", "gy", "gz"), P("gz", None)),
        check_vma=False,
    )
```

profile of v0, /device:TPU:0, one launch (start us, length us, event | category | flops | bytes accessed | tf_op | source)
XLA Modules:
  0.0 567.7 jit_solution(11324461164204223174)
XLA Ops:
  7.2 3.9 fusion.379
  24.5 3.6 collective-permute-start.4
  31.2 3.2 gather_fusion
  38.5 4.9 scatter_custom_fusion
  43.5 4.2 copy.103
  60.8 4.4 copy_dynamic-update-slice_fusion
  65.2 17.3 %collective-permute-done = f32[64,6,8,128]{3,2,1,0:T(8,128)} collective-permute-done((f32[64,6,8,128]{3,2,1,0:T(8,128)}, f32[64,6,8,128]{3,2,1,0:T(8,128)}, u32[]{:S(2)}, u32[]{:S(2)}) %collective-permute-start) | collective-permute-done | bytes 1572896 | tf_op jit(solution)/shard_map/ppermute | solution.py:31
  85.2 38.5 %broadcast_multiply_fusion = (f32[64,8,8,128]{3,2,1,0:T(8,128)}, f32[64,8,8,128]{3,2,1,0:T(8,128)}) fusion(f32[64,8,8,128]{3,2,1,0:T(8,128)S(1)} %copy-done.1, f32[64,8,8,128]{3,2,1,0:T(8,128)} %copy.103, f32[8,8,128]{2,1,0:T(8,128)S(1)} %copy-done.6, f32[64,8,8,6]{3,2,1,0:T(8,128)} %copy.98, f32[64,8,8,6]{3,2,1,0:T(8,128)} %copy.96, ...), kind=kLoop, calls=%fused_computation.606 | loop fusion | flops 41943040 | bytes 47939584 | tf_op jit(solution)/shard_map/div | solution.py:98
  136.9 3.2 gather_fusion.1
  145.8 3.9 collective-permute-start.10
  155.8 4.6 scatter_custom_fusion.1
  160.4 4.2 copy.116
  170.5 3.2 copy.105
  176.9 26.2 %collective-permute-done.7 = f32[64,6,8,128]{3,2,1,0:T(8,128)} collective-permute-done((f32[64,6,8,128]{3,2,1,0:T(8,128)}, f32[64,6,8,128]{3,2,1,0:T(8,128)}, u32[]{:S(2)}, u32[]{:S(2)}) %collective-permute-start.7) | collective-permute-done | bytes 1572896 | tf_op jit(solution)/shard_map/ppermute | solution.py:30
  203.1 62.4 %fusion.81 = f32[64,8,8,128]{3,2,1,0:T(8,128)S(1)} fusion(f32[64,8,8,128]{3,2,1,0:T(8,128)} %param.6, f32[64,8,8,128]{3,2,1,0:T(8,128)} %copy.116, f32[64,8,8,128]{3,2,1,0:T(8,128)} %get-tuple-element.4, f32[64,6,8,128]{3,2,1,0:T(8,128)} %collective-permute-done.7, f32[64,6,8,128]{3,2,1,0:T(8,128)} %collective-permute-done.6, f32[64,8,8,6]{3,2,1,0:T(8,128)} %copy.111, ...), kind=kLoop, calls=%fused_computation.299 | loop fusion | flops 51904512 | bytes 17006592 | tf_op jit(solution)/shard_map/sub | solution.py:101
  285.5 4.0 collective-permute-start.16
  295.9 4.6 scatter_custom_fusion.2
  300.4 4.2 copy.129
  310.4 3.2 copy.118
  316.9 25.9 %collective-permute-done.13 = f32[64,6,8,128]{3,2,1,0:T(8,128)} collective-permute-done((f32[64,6,8,128]{3,2,1,0:T(8,128)}, f32[64,6,8,128]{3,2,1,0:T(8,128)}, u32[]{:S(2)}, u32[]{:S(2)}) %collective-permute-start.13) | collective-permute-done | bytes 1572896 | tf_op jit(solution)/shard_map/ppermute | solution.py:30
  342.7 34.4 %fusion.47 = f32[64,8,8,128]{3,2,1,0:T(8,128)} fusion(f32[64,8,8,128]{3,2,1,0:T(8,128)} %copy.129, f32[64,8,8,128]{3,2,1,0:T(8,128)S(1)} %fusion.81, f32[64,6,8,128]{3,2,1,0:T(8,128)} %collective-permute-done.13, f32[64,6,8,128]{3,2,1,0:T(8,128)} %collective-permute-done.12, f32[64,8,8,6]{3,2,1,0:T(8,128)} %copy.124, f32[64,8,8,6]{3,2,1,0:T(8,128)} %copy.122, ...), kind=kLoop, calls=%fused_computation.265 | loop fusion | flops 52428800 | bytes 14909440 | tf_op jit(solution)/shard_map/sub | solution.py:101
  387.9 3.8 copy.138
  395.1 5.0 fusion.371
  402.7 4.1 collective-permute-start.22
  413.1 4.4 scatter_custom_fusion.3
  417.6 4.2 copy.142
  427.6 3.2 copy.131
  434.0 22.9 %collective-permute-done.19 = f32[64,6,8,128]{3,2,1,0:T(8,128)} collective-permute-done((f32[64,6,8,128]{3,2,1,0:T(8,128)}, f32[64,6,8,128]{3,2,1,0:T(8,128)}, u32[]{:S(2)}, u32[]{:S(2)}) %collective-permute-start.19) | collective-permute-done | bytes 1572896 | tf_op jit(solution)/shard_map/ppermute | solution.py:30
  456.9 63.8 %fusion.13 = f32[64,8,8,128]{3,2,1,0:T(8,128)} fusion(f32[64,8,8,128]{3,2,1,0:T(8,128)S(1)} %fusion.81, f32[64,8,8,128]{3,2,1,0:T(8,128)} %copy.142, f32[64,8,8,128]{3,2,1,0:T(8,128)} %fusion.47, f32[64,6,8,128]{3,2,1,0:T(8,128)} %collective-permute-done.19, f32[64,6,8,128]{3,2,1,0:T(8,128)} %collective-permute-done.18, f32[64,8,8,6]{3,2,1,0:T(8,128)} %copy.137, ...), kind=kLoop, calls=%fused_computation.231 | loop fusion | flops 51904512 | bytes 14909440 | tf_op jit(solution)/shard_map/sub | solution.py:101
  520.6 6.9 %fusion.347 = f32[64,64]{1,0:T(8,128)} fusion(f32[64,8,8,128]{3,2,1,0:T(8,128)} %fusion.13), kind=kOutput, calls=%fused_computation.597 | convolution fusion | flops 402653184 | bytes 2113536 | tf_op jit(solution)/shard_map/bc,dc->bd/dot_general | solution.py:109
  527.5 20.1 %reduce-scatter.2.cloned.1.call-done = f32[16,64]{1,0:T(8,128)} async-done(((f32[64,64]{1,0:T(8,128)}), f32[16,64]{1,0:T(8,128)}) %reduce-scatter.2.cloned.1.call-update) | async-done | bytes 4112 | tf_op jit(solution)/shard_map/reduce_scatter | solution.py:108
  547.6 12.2 %psum.7 = f32[16,64]{1,0:T(8,128)S(1)} all-reduce(f32[16,64]{1,0:T(8,128)} %reduce-scatter.2.cloned.1.call-done), channel_id=1, replica_groups=mesh['gx'=2,'gy'=4,'gz'=4] {'gx','gy'}, use_global_device_ids=true, to_apply=%region_5.6 | all-reduce | flops 1024 | bytes 8192 | tf_op jit(solution)/shard_map/psum | solution.py:114
  (132 shorter events, 138.5 us)
Async XLA Ops:
  7.2 27.4 %copy-start = (f32[8,8,64]{2,1,0:T(8,128)S(1)}, f32[8,8,64]{2,1,0:T(8,128)}, u32[]{:S(2)}) copy-start(f32[8,8,64]{2,1,0:T(8,128)} %param.10) | copy-start | bytes 49156
  7.2 6.9 %copy-start.1 = (f32[64,8,8,128]{3,2,1,0:T(8,128)S(1)}, f32[64,8,8,128]{3,2,1,0:T(8,128)}, u32[]{:S(2)}) copy-start(f32[64,8,8,128]{3,2,1,0:T(8,128)} %param.6) | copy-start | bytes 6291460
  7.2 540.4 %reduce-scatter.2.cloned.1.call-start = ((), (), s32[]{:S(2)}) async-start(), calls=%async_computation.1 | async-start | bytes 40960 | tf_op jit(solution)/shard_map/reduce_scatter | solution.py:108
  11.2 45.4 %collective-permute-start.1 = (f32[64,6,8,128]{3,2,1,0:T(8,128)}, f32[64,6,8,128]{3,2,1,0:T(8,128)}, u32[]{:S(2)}, u32[]{:S(2)}) collective-permute-start(f32[64,6,8,128]{3,2,1,0:T(8,128)} %get-tuple-element.25), channel_id=1, source_target_pairs={{0,16},{16,0},{1,17},{17,1},{2,18},{18,2},{3,19},{19,3},{4,20},{20... | collective-permute-start | bytes 4718600 | tf_op jit(solution)/shard_map/ppermute | solution.py:30
  16.3 44.5 %collective-permute-start.2 = (f32[64,8,6,128]{3,1,2,0:T(8,128)}, f32[64,8,6,128]{3,1,2,0:T(8,128)}, u32[]{:S(2)}, u32[]{:S(2)}) collective-permute-start(f32[64,8,6,128]{3,1,2,0:T(8,128)} %copy.154), channel_id=1, source_target_pairs={{4,0},{8,4},{12,8},{0,12},{5,1},{9,5},{13,9},{1,13},{6,2},{10,6},{... | collective-permute-start | bytes 4718600 | tf_op jit(solution)/shard_map/ppermute | solution.py:31
  17.0 65.6 %collective-permute-start = (f32[64,6,8,128]{3,2,1,0:T(8,128)}, f32[64,6,8,128]{3,2,1,0:T(8,128)}, u32[]{:S(2)}, u32[]{:S(2)}) collective-permute-start(f32[64,6,8,128]{3,2,1,0:T(8,128)} %get-tuple-element.24), channel_id=1, source_target_pairs={{16,0},{0,16},{17,1},{1,17},{18,2},{2,18},{19,3},{3,19},{20,4},{4,... | collective-permute-start | bytes 4718600 | tf_op jit(solution)/shard_map/ppermute | solution.py:31
  19.0 34.4 %collective-permute-start.3 = (f32[64,8,6,128]{3,1,2,0:T(8,128)}, f32[64,8,6,128]{3,1,2,0:T(8,128)}, u32[]{:S(2)}, u32[]{:S(2)}) collective-permute-start(f32[64,8,6,128]{3,1,2,0:T(8,128)} %copy.155), channel_id=1, source_target_pairs={{0,4},{4,8},{8,12},{12,0},{1,5},{5,9},{9,13},{13,1},{2,6},{6,10},{... | collective-permute-start | bytes 4718600 | tf_op jit(solution)/shard_map/ppermute | solution.py:30
  21.8 6.4 %copy-start.9 = (s32[8,3]{0,1:T(4,128)S(1)}, s32[8,3]{0,1:T(4,128)}, u32[]{:S(2)}) copy-start(s32[8,3]{0,1:T(4,128)} %param.8) | copy-start | bytes 292
  24.5 13.3 %collective-permute-start.4 = (f32[64,8,8,6]{0,2,3,1:T(8,128)S(1)}, f32[64,8,8,6]{0,2,3,1:T(8,128)S(1)}, u32[]{:S(2)}, u32[]{:S(2)}) collective-permute-start(f32[64,8,8,6]{0,2,3,1:T(8,128)S(1)} %copy.156), channel_id=1, source_target_pairs={{1,0},{2,1},{3,2},{0,3},{5,4},{6,5},{7,6},{4,7},{9,8},{10,9},{11,1... | collective-permute-start | bytes 294920 | tf_op jit(solution)/shard_map/ppermute | solution.py:31
  31.0 3.5 copy-start.7
  37.7 12.8 %collective-permute-start.5 = (f32[64,8,8,6]{0,2,3,1:T(8,128)S(1)}, f32[64,8,8,6]{0,2,3,1:T(8,128)S(1)}, u32[]{:S(2)}, u32[]{:S(2)}) collective-permute-start(f32[64,8,8,6]{0,2,3,1:T(8,128)S(1)} %copy.157), channel_id=1, source_target_pairs={{0,1},{1,2},{2,3},{3,0},{4,5},{5,6},{6,7},{7,4},{8,9},{9,10},{10,1... | collective-permute-start | bytes 294920 | tf_op jit(solution)/shard_map/ppermute | solution.py:30
  60.8 24.4 %copy-start.4 = (f32[64,14,8,128]{3,2,1,0:T(8,128)}, f32[64,14,8,128]{3,2,1,0:T(8,128)S(1)}, u32[]{:S(2)}) copy-start(f32[64,14,8,128]{3,2,1,0:T(8,128)S(1)} %get-tuple-element.28) | copy-start | bytes 11010052
  65.2 20.0 %copy-start.6 = (f32[8,8,128]{2,1,0:T(8,128)S(1)}, f32[8,8,128]{2,1,0:T(8,128)}, u32[]{:S(2)}) copy-start(f32[8,8,128]{2,1,0:T(8,128)} %param.7) | copy-start | bytes 98308
  129.9 40.5 %collective-permute-start.8 = (f32[64,8,6,128]{3,1,2,0:T(8,128)}, f32[64,8,6,128]{3,1,2,0:T(8,128)}, u32[]{:S(2)}, u32[]{:S(2)}) collective-permute-start(f32[64,8,6,128]{3,1,2,0:T(8,128)} %copy.104), channel_id=1, source_target_pairs={{4,0},{8,4},{12,8},{0,12},{5,1},{9,5},{13,9},{1,13},{6,2},{10,6},{... | collective-permute-start | bytes 4718600 | tf_op jit(solution)/shard_map/ppermute | solution.py:31
  131.8 41.9 %collective-permute-start.9 = (f32[64,8,6,128]{3,1,2,0:T(8,128)}, f32[64,8,6,128]{3,1,2,0:T(8,128)}, u32[]{:S(2)}, u32[]{:S(2)}) collective-permute-start(f32[64,8,6,128]{3,1,2,0:T(8,128)} %copy.106), channel_id=1, source_target_pairs={{0,4},{4,8},{8,12},{12,0},{1,5},{5,9},{9,13},{13,1},{2,6},{6,10},{... | collective-permute-start | bytes 4718600 | tf_op jit(solution)/shard_map/ppermute | solution.py:30
  132.1 44.8 %collective-permute-start.6 = (f32[64,6,8,128]{3,2,1,0:T(8,128)}, f32[64,6,8,128]{3,2,1,0:T(8,128)}, u32[]{:S(2)}, u32[]{:S(2)}) collective-permute-start(f32[64,6,8,128]{3,2,1,0:T(8,128)} %get-tuple-element.22), channel_id=1, source_target_pairs={{16,0},{0,16},{17,1},{1,17},{18,2},{2,18},{19,3},{3,19},{20,4},{4,... | collective-permute-start | bytes 4718600 | tf_op jit(solution)/shard_map/ppermute | solution.py:31
  133.9 69.2 %collective-permute-start.7 = (f32[64,6,8,128]{3,2,1,0:T(8,128)}, f32[64,6,8,128]{3,2,1,0:T(8,128)}, u32[]{:S(2)}, u32[]{:S(2)}) collective-permute-start(f32[64,6,8,128]{3,2,1,0:T(8,128)} %get-tuple-element.23), channel_id=1, source_target_pairs={{0,16},{16,0},{1,17},{17,1},{2,18},{18,2},{3,19},{19,3},{4,20},{20... | collective-permute-start | bytes 4718600 | tf_op jit(solution)/shard_map/ppermute | solution.py:30
  143.0 7.2 %copy-start.5 = (f32[64,8,8,6]{3,2,1,0:T(8,128)S(1)}, f32[64,8,8,6]{3,2,1,0:T(8,128)}, u32[]{:S(2)}) copy-start(f32[64,8,8,6]{3,2,1,0:T(8,128)} %get-tuple-element.21) | copy-start | bytes 294916
  145.8 8.8 %collective-permute-start.10 = (f32[64,8,8,6]{0,2,3,1:T(8,128)S(1)}, f32[64,8,8,6]{0,2,3,1:T(8,128)S(1)}, u32[]{:S(2)}, u32[]{:S(2)}) collective-permute-start(f32[64,8,8,6]{0,2,3,1:T(8,128)S(1)} %copy.108), channel_id=1, source_target_pairs={{1,0},{2,1},{3,2},{0,3},{5,4},{6,5},{7,6},{4,7},{9,8},{10,9},{11,1... | collective-permute-start | bytes 294920 | tf_op jit(solution)/shard_map/ppermute | solution.py:31
  154.6 12.9 %collective-permute-start.11 = (f32[64,8,8,6]{0,2,3,1:T(8,128)S(1)}, f32[64,8,8,6]{0,2,3,1:T(8,128)S(1)}, u32[]{:S(2)}, u32[]{:S(2)}) collective-permute-start(f32[64,8,8,6]{0,2,3,1:T(8,128)S(1)} %copy.110), channel_id=1, source_target_pairs={{0,1},{1,2},{2,3},{3,0},{4,5},{5,6},{6,7},{7,4},{8,9},{9,10},{10,1... | collective-permute-start | bytes 294920 | tf_op jit(solution)/shard_map/ppermute | solution.py:30
  269.5 40.9 %collective-permute-start.14 = (f32[64,8,6,128]{3,1,2,0:T(8,128)}, f32[64,8,6,128]{3,1,2,0:T(8,128)}, u32[]{:S(2)}, u32[]{:S(2)}) collective-permute-start(f32[64,8,6,128]{3,1,2,0:T(8,128)} %copy.117), channel_id=1, source_target_pairs={{4,0},{8,4},{12,8},{0,12},{5,1},{9,5},{13,9},{1,13},{6,2},{10,6},{... | collective-permute-start | bytes 4718600 | tf_op jit(solution)/shard_map/ppermute | solution.py:31
  271.4 42.3 %collective-permute-start.15 = (f32[64,8,6,128]{3,1,2,0:T(8,128)}, f32[64,8,6,128]{3,1,2,0:T(8,128)}, u32[]{:S(2)}, u32[]{:S(2)}) collective-permute-start(f32[64,8,6,128]{3,1,2,0:T(8,128)} %copy.119), channel_id=1, source_target_pairs={{0,4},{4,8},{8,12},{12,0},{1,5},{5,9},{9,13},{13,1},{2,6},{6,10},{... | collective-permute-start | bytes 4718600 | tf_op jit(solution)/shard_map/ppermute | solution.py:30
  271.9 45.0 %collective-permute-start.12 = (f32[64,6,8,128]{3,2,1,0:T(8,128)}, f32[64,6,8,128]{3,2,1,0:T(8,128)}, u32[]{:S(2)}, u32[]{:S(2)}) collective-permute-start(f32[64,6,8,128]{3,2,1,0:T(8,128)} %get-tuple-element.16), channel_id=1, source_target_pairs={{16,0},{0,16},{17,1},{1,17},{18,2},{2,18},{19,3},{3,19},{20,4},{4,... | collective-permute-start | bytes 4718600 | tf_op jit(solution)/shard_map/ppermute | solution.py:31
  273.9 68.9 %collective-permute-start.13 = (f32[64,6,8,128]{3,2,1,0:T(8,128)}, f32[64,6,8,128]{3,2,1,0:T(8,128)}, u32[]{:S(2)}, u32[]{:S(2)}) collective-permute-start(f32[64,6,8,128]{3,2,1,0:T(8,128)} %get-tuple-element.17), channel_id=1, source_target_pairs={{0,16},{16,0},{1,17},{17,1},{2,18},{18,2},{3,19},{19,3},{4,20},{20... | collective-permute-start | bytes 4718600 | tf_op jit(solution)/shard_map/ppermute | solution.py:30
  285.5 9.2 %collective-permute-start.16 = (f32[64,8,8,6]{0,2,3,1:T(8,128)S(1)}, f32[64,8,8,6]{0,2,3,1:T(8,128)S(1)}, u32[]{:S(2)}, u32[]{:S(2)}) collective-permute-start(f32[64,8,8,6]{0,2,3,1:T(8,128)S(1)} %copy.121), channel_id=1, source_target_pairs={{1,0},{2,1},{3,2},{0,3},{5,4},{6,5},{7,6},{4,7},{9,8},{10,9},{11,1... | collective-permute-start | bytes 294920 | tf_op jit(solution)/shard_map/ppermute | solution.py:31
  294.7 12.9 %collective-permute-start.17 = (f32[64,8,8,6]{0,2,3,1:T(8,128)S(1)}, f32[64,8,8,6]{0,2,3,1:T(8,128)S(1)}, u32[]{:S(2)}, u32[]{:S(2)}) collective-permute-start(f32[64,8,8,6]{0,2,3,1:T(8,128)S(1)} %copy.123), channel_id=1, source_target_pairs={{0,1},{1,2},{2,3},{3,0},{4,5},{5,6},{6,7},{7,4},{8,9},{9,10},{10,1... | collective-permute-start | bytes 294920 | tf_op jit(solution)/shard_map/ppermute | solution.py:30
  383.5 44.1 %collective-permute-start.20 = (f32[64,8,6,128]{3,1,2,0:T(8,128)}, f32[64,8,6,128]{3,1,2,0:T(8,128)}, u32[]{:S(2)}, u32[]{:S(2)}) collective-permute-start(f32[64,8,6,128]{3,1,2,0:T(8,128)} %copy.130), channel_id=1, source_target_pairs={{4,0},{8,4},{12,8},{0,12},{5,1},{9,5},{13,9},{1,13},{6,2},{10,6},{... | collective-permute-start | bytes 4718600 | tf_op jit(solution)/shard_map/ppermute | solution.py:31
  385.9 44.9 %collective-permute-start.21 = (f32[64,8,6,128]{3,1,2,0:T(8,128)}, f32[64,8,6,128]{3,1,2,0:T(8,128)}, u32[]{:S(2)}, u32[]{:S(2)}) collective-permute-start(f32[64,8,6,128]{3,1,2,0:T(8,128)} %copy.132), channel_id=1, source_target_pairs={{0,4},{4,8},{8,12},{12,0},{1,5},{5,9},{9,13},{13,1},{2,6},{6,10},{... | collective-permute-start | bytes 4718600 | tf_op jit(solution)/shard_map/ppermute | solution.py:30
  385.9 48.1 %collective-permute-start.18 = (f32[64,6,8,128]{3,2,1,0:T(8,128)}, f32[64,6,8,128]{3,2,1,0:T(8,128)}, u32[]{:S(2)}, u32[]{:S(2)}) collective-permute-start(f32[64,6,8,128]{3,2,1,0:T(8,128)} %get-tuple-element.10), channel_id=1, source_target_pairs={{16,0},{0,16},{17,1},{1,17},{18,2},{2,18},{19,3},{3,19},{20,4},{4,... | collective-permute-start | bytes 4718600 | tf_op jit(solution)/shard_map/ppermute | solution.py:31
  387.6 69.3 %collective-permute-start.19 = (f32[64,6,8,128]{3,2,1,0:T(8,128)}, f32[64,6,8,128]{3,2,1,0:T(8,128)}, u32[]{:S(2)}, u32[]{:S(2)}) collective-permute-start(f32[64,6,8,128]{3,2,1,0:T(8,128)} %get-tuple-element.11), channel_id=1, source_target_pairs={{0,16},{16,0},{1,17},{17,1},{2,18},{18,2},{3,19},{19,3},{4,20},{20... | collective-permute-start | bytes 4718600 | tf_op jit(solution)/shard_map/ppermute | solution.py:30
  402.7 9.2 %collective-permute-start.22 = (f32[64,8,8,6]{0,2,3,1:T(8,128)S(1)}, f32[64,8,8,6]{0,2,3,1:T(8,128)S(1)}, u32[]{:S(2)}, u32[]{:S(2)}) collective-permute-start(f32[64,8,8,6]{0,2,3,1:T(8,128)S(1)} %copy.134), channel_id=1, source_target_pairs={{1,0},{2,1},{3,2},{0,3},{5,4},{6,5},{7,6},{4,7},{9,8},{10,9},{11,1... | collective-permute-start | bytes 294920 | tf_op jit(solution)/shard_map/ppermute | solution.py:31
  411.9 12.7 %collective-permute-start.23 = (f32[64,8,8,6]{0,2,3,1:T(8,128)S(1)}, f32[64,8,8,6]{0,2,3,1:T(8,128)S(1)}, u32[]{:S(2)}, u32[]{:S(2)}) collective-permute-start(f32[64,8,8,6]{0,2,3,1:T(8,128)S(1)} %copy.136), channel_id=1, source_target_pairs={{0,1},{1,2},{2,3},{3,0},{4,5},{5,6},{6,7},{7,4},{8,9},{9,10},{10,1... | collective-permute-start | bytes 294920 | tf_op jit(solution)/shard_map/ppermute | solution.py:30
  (3 other events, 8.5 us)
Sparse Core Ops, SparseCore 0:
  527.7 19.9 reduce-scatter.1
where the time goes:
time: 575 us; the launch traced here: 568 us
  other arithmetic  218 us (38%)
  local copies, waits for them, and re-layouts  162 us (28%)
  waiting for transfers between devices  119 us (21%)
  starting transfers between devices  29.7 us (5%)
  between operations  14.8 us (3%)
  blocking collectives  12.2 us (2%)
  matrix products  11.3 us (2%)
    sub x3, other arithmetic, shards(): following = 2.0 * (image - CENTER * current) / HALF - previous  160 us
    ppermute x12, waiting for transfers between devices, extended(): before = lax.ppermute(last, axis, up)  74.9 us
    slice x18, local copies, waits for them, and re-layouts, extended(): leading = lax.slice_in_dim(array, 0, width, axis=dim)  42.6 us
    div x1, other arithmetic, shards(): current = (image - CENTER * panel) / HALF  38.5 us
    ppermute x8, local copies, waits for them, and re-layouts, extended(): before = lax.ppermute(last, axis, up)  24.5 us
    ppermute x12, waiting for transfers between devices, extended(): after = lax.ppermute(leading, axis, down)  24.4 us
    ppermute x12, starting transfers between devices, extended(): after = lax.ppermute(leading, axis, down)  23.7 us
    ppermute x7, local copies, waits for them, and re-layouts, extended(): after = lax.ppermute(leading, axis, down)  21.3 us
  transfers between devices with their start and end apart: 25, of which 8 were waited for; matrix products, arithmetic and copies ran while one was open for 29% of the time, Pallas kernels for 0%

commit v1 on v0

v1 whole, which is shorter than its diff:
```python
import functools
import math

import jax
import jax.numpy as jnp
import ml_dtypes
import numpy as np
from jax import lax
from jax.experimental import pallas as pl
from jax.experimental.pallas import tpu as pltpu
from jax.sharding import PartitionSpec as P

DEGREE = 4
CHUNKS = 2

STENCIL = (
    -5369.0 / 1800.0,
    12.0 / 7.0,
    -15.0 / 56.0,
    10.0 / 189.0,
    -1.0 / 112.0,
    2.0 / 1925.0,
    -1.0 / 16632.0,
)
SPACING = 0.224
CENTER = 210.5
HALF = 209.5
REACH = 6
TILE = 64
LANES = 128
SUBS = 8
KINETIC = -0.5 / (SPACING * SPACING) / HALF
TAPS = tuple(KINETIC * c for c in STENCIL)
DIAGONAL = 3.0 * TAPS[0] - CENTER / HALF

F32 = jnp.float32
BF16 = jnp.bfloat16
VMEM = pl.BlockSpec(memory_space=pltpu.VMEM)
SMEM = pl.BlockSpec(memory_space=pltpu.SMEM)
ANY = pl.BlockSpec(memory_space=pl.ANY)


def split_halves(matrix):
    high = matrix.astype(ml_dtypes.bfloat16)
    low = (matrix - high.astype(np.float64)).astype(ml_dtypes.bfloat16)
    wide = np.concatenate([high, low], axis=1)
    return np.concatenate([wide, wide], axis=0)


def line_weights():
    own = np.zeros((LANES, LANES))
    halo = np.zeros((LANES, LANES))
    for k in range(1, REACH + 1):
        for z in range(LANES):
            if z + k < LANES:
                own[z + k, z] = TAPS[k]
            else:
                halo[8 + z + k - LANES, z] = TAPS[k]
            if z - k >= 0:
                own[z - k, z] = TAPS[k]
            else:
                halo[REACH + z - k, z] = TAPS[k]
    return np.concatenate([split_halves(own), split_halves(halo)], axis=0)


def halves(value):
    high = value.astype(BF16)
    low = (value - high.astype(F32)).astype(BF16)
    return high, low


def parts_kernel(count, index_ref, proj_ref, root_ref, pot_ref, meta_ref, out_ref):
    out_ref[0:64, :] = pot_ref[...]
    point = lax.broadcasted_iota(jnp.int32, (TILE, TILE), 0)
    for pair in range(count // 2):
        both = []
        for atom in (2 * pair, 2 * pair + 1):
            order = index_ref[atom : atom + 1, :]
            hot = (point == order).astype(F32)
            both.append(
                lax.dot_general(
                    proj_ref[atom],
                    hot,
                    (((1,), (1,)), ((), ())),
                    precision=lax.Precision.HIGHEST,
                    preferred_element_type=F32,
                )
                * root_ref[:, atom : atom + 1]
            )
        out_ref[64 + 8 * pair : 72 + 8 * pair, :] = jnp.concatenate(both, axis=1)
    out_ref[64 + 4 * count : 72 + 4 * count, :] = meta_ref[...]


def setup_kernel(gx, gy, nb, count, me_ref, *refs):
    group = gx * gy
    blocks = refs[:group]
    diag_ref, q_ref, meta_ref, pots, roots, raw, sem = refs[group:]
    rows = 4 * count
    copies = []
    for d in range(group):
        slot = me_ref[0] ^ d
        i, j = slot // gy, slot % gy
        for b in range(nb):
            copies.append(
                pltpu.make_async_copy(
                    blocks[d].at[pl.ds(0, 64)],
                    pots.at[pl.ds(pl.multiple_of(((j * gx + i) * nb + b) * 64, 64), 64)],
                    sem.at[0],
                )
            )
        copies.append(
            pltpu.make_async_copy(
                blocks[d].at[pl.ds(64, rows)],
                roots.at[pl.ds(pl.multiple_of(slot * rows, 8), rows)],
                sem.at[0],
            )
        )
        copies.append(
            pltpu.make_async_copy(
                blocks[d].at[pl.ds(64 + rows, 8)],
                raw.at[pl.ds(pl.multiple_of(slot * 8, 8), 8)],
                sem.at[0],
            )
        )
    for copy in copies:
        copy.start()
    for copy in copies:
        copy.wait()

    def corner(n, carry):
        slot = n // count
        atom = n % count
        base = raw[slot * 8, atom].astype(jnp.int32)
        meta_ref[2 * n] = base + (slot % gy) * 64
        meta_ref[2 * n + 1] = raw[slot * 8, count + atom].astype(jnp.int32)
        return carry

    lax.fori_loop(0, group * count, corner, 0)

    def line(y, carry):
        for x in range(8):
            start = (y // 8) * 512 + y % 8 + x * 8
            value = pots[pl.ds(start, SUBS, stride=64), :]
            diag_ref[y * 8 + x] = value * (1.0 / HALF) + DIAGONAL
        return carry

    lax.fori_loop(0, gy * 8, line, 0)
    same = lax.broadcasted_iota(jnp.int32, (LANES, LANES), 0) // TILE == (
        lax.broadcasted_iota(jnp.int32, (LANES, LANES), 1) // TILE
    )

    def pair(p, carry):
        root = roots[pl.ds(pl.multiple_of(p * 8, 8), 8), :]
        full = lax.dot_general(
            root,
            root,
            (((0,), (0,)), ((), ())),
            precision=lax.Precision.HIGHEST,
            preferred_element_type=F32,
        )
        high, low = halves(jnp.where(same, full, 0.0))
        q_ref[p] = jnp.concatenate([high, low], axis=1)
        return carry

    lax.fori_loop(0, group * count // 2, pair, 0)


def pack_edges(values, lane):
    low = high = None
    for slot, value in enumerate(values):
        here = (lane >> 3) == slot
        to_low = pltpu.roll(value, 8 * slot, 1) if slot else value
        to_high = pltpu.roll(value, (8 * slot - (LANES - REACH)) % LANES, 1)
        low = to_low if low is None else jnp.where(here, to_low, low)
        high = to_high if high is None else jnp.where(here, to_high, high)
    return low, high


def unpack_kernel(gx, gy, nb, me_ref, *refs):
    group = gx * gy
    blocks = refs[:group]
    z_ref, low_ref, high_ref, staged, sem = refs[group:]
    size = nb * 64
    copies = []
    for d in range(group):
        slot = me_ref[0] ^ d
        i, j = slot // gy, slot % gy
        copies.append(
            pltpu.make_async_copy(
                blocks[d],
                staged.at[pl.ds(pl.multiple_of((j * gx + i) * size, 64), size)],
                sem.at[0],
            )
        )
    for copy in copies:
        copy.start()
    for copy in copies:
        copy.wait()
    lane = lax.broadcasted_iota(jnp.int32, (SUBS, LANES), 1)

    def lines(pair, carry):
        values = []
        for q in range(2):
            y = 2 * pair + q
            for x in range(8):
                start = (y // 8) * 512 + y % 8 + x * 8
                value = staged[pl.ds(start, SUBS, stride=64), :]
                z_ref[y * 8 + x] = value
                values.append(value)
        low, high = pack_edges(values, lane)
        low_ref[pair] = low
        high_ref[pair] = high
        return carry

    lax.fori_loop(0, gy * 4, lines, 0)


def step_kernel(gx, gy, nb, count, first, last, me_ref, meta_ref, *refs):
    group = gx * gy
    if first:
        z_ref, diag_ref, q_ref, below_ref, above_ref, w_ref = refs[:6]
        refs = refs[6:]
    else:
        z_ref, prev_ref, diag_ref, q_ref, below_ref, above_ref, w_ref = refs[:7]
        refs = refs[7:]
    if last:
        blocks = refs[:group]
        acc, out_ref, sem = refs[group:]
    else:
        out_ref, low_ref, high_ref, acc = refs
    ny = gy * 8
    lane = lax.broadcasted_iota(jnp.int32, (SUBS, LANES), 1)
    row_part = lax.broadcasted_iota(jnp.int32, (SUBS, LANES), 0) // nb

    def second_dim(x, carry):
        values = [z_ref[y * 8 + x] for y in range(ny)]
        for y in range(ny):
            total = None
            for k in range(1, REACH + 1):
                term = TAPS[k] * (values[(y + k) % ny] + values[(y - k) % ny])
                total = term if total is None else total + term
            acc[y * 8 + x] = total
        return carry

    lax.fori_loop(0, 8, second_dim, 0)

    def atoms(slot, carry):
        part = slot // gy
        places = []
        tiles = []
        for p in range(count // 2):
            tile = jnp.zeros((SUBS, LANES), F32)
            for q in range(2):
                n = slot * count + 2 * p + q
                base = meta_ref[2 * n]
                z0 = meta_ref[2 * n + 1]
                places.append((base, z0))
                for t in range(16):
                    value = z_ref[base + (t % 4) * 8 + t // 4]
                    shifted = pltpu.roll(value, (4 * t + TILE * q - z0 + LANES) & (LANES - 1), 1)
                    tile = jnp.where((lane >> 2) == t + 16 * q, shifted, tile)
            tiles.append(tile)
        spreads = []
        for p in range(count // 2):
            high, low = halves(tiles[p])
            product = jnp.dot(
                jnp.concatenate([high, low], axis=0),
                q_ref[slot * (count // 2) + p],
                preferred_element_type=F32,
            )
            spreads.append(
                product[:SUBS, :LANES]
                + product[:SUBS, LANES:]
                + product[SUBS:, :LANES]
                + product[SUBS:, LANES:]
            )
        for n in range(count):
            base, z0 = places[n]
            inside = (row_part == part) & (lane >= z0) & (lane < z0 + 4)
            for t in range(16):
                shifted = pltpu.roll(
                    spreads[n // 2], (z0 - 4 * t - TILE * (n % 2) + LANES) & (LANES - 1), 1
                )
                row = base + (t % 4) * 8 + t // 4
                acc[row] = acc[row] + jnp.where(inside, shifted, 0.0)
        return carry

    lax.fori_loop(0, group, atoms, 0)

    def rest(four, carry):
        tiles = z_ref[pl.ds(four * 32, 32)]
        own = tiles.reshape(32 * SUBS, LANES)
        joined = []
        for q in range(2):
            below = below_ref[2 * four + q]
            above = above_ref[2 * four + q]
            for slot in range(16):
                left = pltpu.roll(below, (-8 * slot) % LANES, 1)
                right = pltpu.roll(above, (8 - 8 * slot) % LANES, 1)
                joined.append(jnp.where(lane < 8, left, right))
        halo = jnp.concatenate(joined, axis=0)
        operand = jnp.concatenate([*halves(own), *halves(halo)], axis=1)
        product = jnp.dot(operand, w_ref[...], preferred_element_type=F32)
        third = (product[:, :LANES] + product[:, LANES:]).reshape(32, SUBS, LANES)
        results = []
        for q in range(4):
            values = [tiles[8 * q + x] for x in range(8)]
            after = [pltpu.roll(value, SUBS - nb, 0) for value in values]
            before = after if gx == 2 else [pltpu.roll(value, nb, 0) for value in values]
            wide = before + values + after
            for x in range(8):
                total = acc[four * 32 + 8 * q + x] + third[8 * q + x]
                total = total + diag_ref[four * 32 + 8 * q + x] * values[x]
                for k in range(1, REACH + 1):
                    total = total + TAPS[k] * (wide[8 + x + k] + wide[8 + x - k])
                if not first:
                    total = 2.0 * total - prev_ref[four * 32 + 8 * q + x]
                results.append(total)
                if last:
                    y = four * 4 + q
                    start = (y // 8) * 512 + y % 8 + x * 8
                    out_ref[pl.ds(start, SUBS, stride=64), :] = total
                else:
                    out_ref[four * 32 + 8 * q + x] = total
        if not last:
            for q in range(2):
                low, high = pack_edges(results[16 * q : 16 * q + 16], lane)
                low_ref[2 * four + q] = low
                high_ref[2 * four + q] = high
        return carry

    lax.fori_loop(0, gy * 2, rest, 0)
    if last:
        size = nb * 64
        copies = []
        for d in range(group):
            slot = me_ref[0] ^ d
            i, j = slot // gy, slot % gy
            copies.append(
                pltpu.make_async_copy(
                    out_ref.at[pl.ds(pl.multiple_of((j * gx + i) * size, 64), size)],
                    blocks[d],
                    sem.at[0],
                )
            )
        for copy in copies:
            copy.start()
        for copy in copies:
            copy.wait()


def gather_kernel(group, nb, bands, me_ref, *refs):
    blocks = refs[: CHUNKS * group]
    out_ref, gram_ref, field, sem = refs[CHUNKS * group :]
    size = nb * 64
    copies = []
    for chunk in range(CHUNKS):
        for d in range(group):
            slot = me_ref[0] ^ d
            row = (chunk * group + slot) * size
            copies.append(
                pltpu.make_async_copy(
                    blocks[chunk * group + d],
                    field.at[pl.ds(pl.multiple_of(row, 64), size)],
                    sem.at[0],
                )
            )
    for copy in copies:
        copy.start()
    for copy in copies:
        copy.wait()
    store = pltpu.make_async_copy(field, out_ref, sem.at[0])
    store.start()
    gram_ref[...] = jnp.zeros_like(gram_ref)

    def cells(n, carry):
        total = None
        for m in range(4):
            pieces = []
            for c in range(2):
                cell = n * 8 + m * 2 + c
                pieces.append(
                    jnp.concatenate(
                        [
                            field[pl.ds(g * SUBS * 64 + cell, SUBS, stride=64), :]
                            for g in range(bands // SUBS)
                        ],
                        axis=0,
                    )
                )
            value = jnp.concatenate(pieces, axis=1)
            high, low = halves(value)
            both = jnp.concatenate([high, low], axis=0)
            product = lax.dot_general(
                both, both, (((1,), (1,)), ((), ())), preferred_element_type=F32
            )
            total = product if total is None else total + product
        gram_ref[...] += (
            total[:bands, :bands]
            + total[bands:, :bands]
            + total[:bands, bands:]
            + total[bands:, bands:]
        )
        return carry

    lax.fori_loop(0, 8, cells, 0)
    store.wait()


def shape(*dims, dtype=F32):
    return jax.ShapeDtypeStruct(dims, dtype)


def shards(panel, potential, atom_corner, proj_index, projectors, couplings):
    bands, size_x, size_y, size_z = panel.shape
    count, nproj = couplings.shape
    gx, gy, gz = lax.axis_size("gx"), lax.axis_size("gy"), lax.axis_size("gz")
    group = gx * gy
    nb = bands // (CHUNKS * group)
    column = ("gx", "gy")
    me = lax.axis_index("gx") * gy + lax.axis_index("gy")
    me_arr = me.reshape(1)
    rows = gy * 64
    pairs = gy * 4

    def swap(block, d):
        return lax.ppermute(block, column, [(s, s ^ d) for s in range(group)])

    anchor = jnp.stack(
        [
            lax.axis_index("gx") * size_x,
            lax.axis_index("gy") * size_y,
            lax.axis_index("gz") * size_z,
        ]
    )
    local = atom_corner - anchor[None, :]
    meta = jnp.concatenate([local[:, 1] * 8 + local[:, 0], local[:, 2]]).astype(F32)
    meta = jnp.broadcast_to(jnp.pad(meta, (0, LANES - 2 * count))[None], (8, LANES))
    part_rows = 64 + 4 * count + 8
    parts = pl.pallas_call(
        functools.partial(parts_kernel, count),
        out_shape=shape(part_rows, LANES),
        in_specs=[VMEM] * 5,
        out_specs=VMEM,
        name="parts",
    )(
        proj_index,
        projectors,
        jnp.sqrt(couplings * (1.0 / HALF)).T,
        potential.reshape(64, LANES),
        meta,
    )
    others = [parts] + [swap(parts, d) for d in range(1, group)]

    field = panel.reshape(bands * 64, LANES)
    size = nb * 64
    forward = []
    for chunk in range(CHUNKS):
        own = [
            lax.dynamic_slice_in_dim(field, (chunk * group + (me ^ d)) * size, size, 0)
            for d in range(group)
        ]
        forward.append([own[0]] + [swap(own[d], d) for d in range(1, group)])

    diag, q_mat, places = pl.pallas_call(
        functools.partial(setup_kernel, gx, gy, nb, count),
        out_shape=[
            shape(rows, SUBS, LANES),
            shape(group * count // 2, LANES, 2 * LANES, dtype=BF16),
            shape(2 * group * count, dtype=jnp.int32),
        ],
        in_specs=[SMEM] + [ANY] * group,
        out_specs=[VMEM, VMEM, SMEM],
        scratch_shapes=[
            pltpu.VMEM((rows * SUBS, LANES), F32),
            pltpu.VMEM((group * 4 * count, LANES), F32),
            pltpu.SMEM((group * 8, LANES), F32),
            pltpu.SemaphoreType.DMA((1,)),
        ],
        name="setup",
    )(me_arr, *others)

    weights = jnp.asarray(line_weights())
    up = [(s, (s + 1) % gz) for s in range(gz)]
    down = [(s, (s - 1) % gz) for s in range(gz)]

    def halos(low, high):
        return lax.ppermute(high, "gz", up), lax.ppermute(low, "gz", down)

    tile_shape = shape(rows, SUBS, LANES)
    edge_shape = shape(pairs, SUBS, LANES)
    states = []
    for chunk in range(CHUNKS):
        tiles, low, high = pl.pallas_call(
            functools.partial(unpack_kernel, gx, gy, nb),
            out_shape=[tile_shape, edge_shape, edge_shape],
            in_specs=[SMEM] + [ANY] * group,
            out_specs=[VMEM] * 3,
            scratch_shapes=[
                pltpu.VMEM((rows * SUBS, LANES), F32),
                pltpu.SemaphoreType.DMA((1,)),
            ],
            name="unpack",
        )(me_arr, *forward[chunk])
        states.append((None, tiles, low, high))

    cost = pl.CostEstimate(flops=rows * SUBS * LANES * 2000, bytes_accessed=8 << 20, transcendentals=0)
    results = [None] * CHUNKS
    for degree_step in range(DEGREE):
        first, last = degree_step == 0, degree_step == DEGREE - 1
        for chunk in range(CHUNKS):
            prev, tiles, low, high = states[chunk]
            below, above = halos(low, high)
            operands = [me_arr, places, tiles]
            if not first:
                operands.append(prev)
            operands += [diag, q_mat, below, above, weights]
            scratch = [pltpu.VMEM((rows, SUBS, LANES), F32)]
            if last:
                out_shape = [shape(size, LANES)] * group
                out_specs = [ANY] * group
                scratch += [
                    pltpu.VMEM((rows * SUBS, LANES), F32),
                    pltpu.SemaphoreType.DMA((1,)),
                ]
            else:
                out_shape = [tile_shape, edge_shape, edge_shape]
                out_specs = [VMEM] * 3
            outs = pl.pallas_call(
                functools.partial(step_kernel, gx, gy, nb, count, first, last),
                out_shape=out_shape,
                in_specs=[SMEM, SMEM] + [VMEM] * (len(operands) - 2),
                out_specs=out_specs,
                scratch_shapes=scratch,
                compiler_params=pltpu.CompilerParams(vmem_limit_bytes=24 << 20),
                cost_estimate=cost,
                name="step",
            )(*operands)
            if last:
                results[chunk] = [outs[0]] + [swap(outs[d], d) for d in range(1, group)]
            else:
                states[chunk] = (tiles, *outs)

    filtered, gram = pl.pallas_call(
        functools.partial(gather_kernel, group, nb, bands),
        out_shape=[shape(bands * 64, LANES), shape(bands, bands)],
        in_specs=[SMEM] + [ANY] * (CHUNKS * group),
        out_specs=[ANY, VMEM],
        scratch_shapes=[
            pltpu.VMEM((bands * 64, LANES), F32),
            pltpu.SemaphoreType.DMA((1,)),
        ],
        name="gather",
    )(me_arr, *[block for chunk in results for block in chunk])

    d = 1
    while d < group:
        gram = gram + swap(gram, d)
        d *= 2
    d = 1
    while d < gz:
        gram = gram + lax.ppermute(gram, "gz", [(s, s ^ d) for s in range(gz)])
        d *= 2
    total_cells = size_x * size_y * size_z * group * gz
    share = bands // gz
    gram = lax.dynamic_slice_in_dim(gram, lax.axis_index("gz") * share, share, 0)
    return filtered.reshape(panel.shape), gram * (1.0 / total_cells)


def solution(mesh):
    placed = (
        P(None, "gx", "gy", "gz"),
        P("gx", "gy", "gz"),
        P(("gx", "gy", "gz"), None),
        P(("gx", "gy", "gz"), None),
        P(("gx", "gy", "gz"), None, None),
        P(("gx", "gy", "gz"), None),
    )
    return jax.shard_map(
        shards,
        mesh=mesh,
        in_specs=placed,
        out_specs=(P(None, "gx", "gy", "gz"), P("gz", None)),
        check_vma=False,
    )
```

time: 575 us -> 219 us (0.38); the launches traced: 568 us -> 219 us
  other arithmetic: 218 us -> 2.9 us
  local copies, waits for them, and re-layouts: 162 us -> 10.4 us
  Pallas kernels: 0 us -> 94.6 us
  waiting for transfers between devices: 119 us -> 36 us
  starting transfers between devices: 29.7 us -> 73.6 us
  between operations: 14.8 us -> 1.15 us
  blocking collectives: 12.2 us -> 0 us
  matrix products: 11.3 us -> 0 us
    sub x4 -> x1, other arithmetic: 161 us -> 0.75 us  [shards(): local = atom_corner - anchor[None, :]]
    pallas_call x0 -> x13, Pallas kernels: none -> 94.6 us  [the longest x8 65.4 us: shards(): pl.pallas_call(functools.partial(step_kernel, gx, gy, nb, count, first, l...]
    ppermute x24 -> x56, waiting for transfers between devices: 99.3 us -> 36 us  [the longest x38 28.1 us: swap(): return lax.ppermute(block, column, [(s, s ^ d) for s in range(group)])]
    slice x24 -> x0, local copies, waits for them, and re-layouts: 53.7 us -> none  [the longest x18 42.6 us: extended(): leading = lax.slice_in_dim(array, 0, width, axis=dim)]
    ppermute x15 -> x0, local copies, waits for them, and re-layouts: 45.8 us -> none  [the longest x8 24.5 us: extended(): before = lax.ppermute(last, axis, up)]
    ppermute x24 -> x56, starting transfers between devices: 29.7 us -> 73.6 us  [the longest x38 39.5 us: swap(): return lax.ppermute(block, column, [(s, s ^ d) for s in range(group)])]
    div x2 -> x0, other arithmetic: 39.1 us -> none  [the longest x1 38.5 us: shards(): current = (image - CENTER * panel) / HALF]
    reduce_scatter x1 -> x0, waiting for transfers between devices: 20.1 us -> none  [shards(): lax.psum_scatter(jnp.einsum('bc,dc->bd', field_flat, field_flat, precisio...]
  transfers between devices with their start and end apart: 25 -> 56, of which waited for: 8 -> 19; matrix products, arithmetic and copies ran while one was open for 29% -> 1% of each run, Pallas kernels for 0% -> 40%
where the time goes in v1:
time: 219 us
  Pallas kernels  94.6 us (43%)
  starting transfers between devices  73.6 us (34%)
  waiting for transfers between devices  36 us (16%)
  local copies, waits for them, and re-layouts  10.4 us (5%)
  other arithmetic  2.9 us (1%)
    pallas_call x8, Pallas kernels, shards(): pl.pallas_call(functools.partial(step_kernel, gx, gy, nb, count, first, l...  65.4 us
    ppermute x38, starting transfers between devices, swap(): return lax.ppermute(block, column, [(s, s ^ d) for s in range(group)])  39.5 us
    ppermute x16, starting transfers between devices, halos(): return (lax.ppermute(high, 'gz', up), lax.ppermute(low, 'gz', down))  31.3 us
    ppermute x38, waiting for transfers between devices, swap(): return lax.ppermute(block, column, [(s, s ^ d) for s in range(group)])  28.1 us
    pallas_call x1, Pallas kernels, shards(): pl.pallas_call(functools.partial(setup_kernel, gx, gy, nb, count), out_sh...  13.6 us
    pallas_call x2, Pallas kernels, shards(): pl.pallas_call(functools.partial(unpack_kernel, gx, gy, nb), out_shape=[t...  8.09 us
    unnamed x85, local copies, waits for them, and re-layouts  7.31 us
    ppermute x2, waiting for transfers between devices, shards(): gram = gram + lax.ppermute(gram, 'gz', [(s, s ^ d) for s in range(gz)])  5.9 us
  transfers between devices with their start and end apart: 56, of which 19 were waited for; matrix products, arithmetic and copies ran while one was open for 1% of the time, Pallas kernels for 40%

profile of v1, /device:TPU:0, one launch (start us, length us, event | category | flops | bytes accessed | tf_op | source)
XLA Modules:
  0.0 218.5 jit_solution(6840562824204974717)
XLA Ops:
  6.0 2.5 %collective-permute-start.1 = (f32[104,128]{1,0:T(8,128)}, f32[104,128]{1,0:T(8,128)S(1)}, u32[]{:S(2)}, u32[]{:S(2)}) collective-permute-start(f32[104,128]{1,0:T(8,128)} %parts.1.refs_0_), channel_id=1, source_target_pairs={{0,8},{4,12},{8,0},{12,4},{16,24},{20,28},{24,16},{28,20},{1,9},{5... | collective-permute-start | bytes 159752 | tf_op jit(solution)/shard_map/ppermute | solution.py:427
  8.5 2.4 %constant_dynamic-slice_fusion = (f32[256,128]{1,0:T(8,128)S(1)}, f32[256,128]{1,0:T(8,128)S(1)}, f32[256,128]{1,0:T(8,128)S(1)}, f32[256,128]{1,0:T(8,128)S(1)}...) fusion(f32[4096,128]{1,0:T(8,128)} %bitcast.13, ...), kind=kLoop, calls=%fused_computation.2 | loop fusion | bytes 4194368 | tf_op jit(solution)/shard_map/dynamic_slice | solution.py:460
  13.1 2.5 %collective-permute-start.5 = (f32[104,128]{1,0:T(8,128)S(1)}, f32[104,128]{1,0:T(8,128)S(1)}, u32[]{:S(2)}, u32[]{:S(2)}) collective-permute-start(f32[104,128]{1,0:T(8,128)S(1)} %copy-done.8), channel_id=1, source_target_pairs={{0,24},{4,28},{8,16},{12,20},{16,8},{20,12},{24,0},{28,4},{1,25},{... | collective-permute-start | bytes 159752 | tf_op jit(solution)/shard_map/ppermute | solution.py:427
  20.2 4.3 %collective-permute-done.6.refs_7_ = f32[104,128]{1,0:T(8,128)S(1)} collective-permute-done((f32[104,128]{1,0:T(8,128)S(1)}, f32[104,128]{1,0:T(8,128)S(1)}, u32[]{:S(2)}, u32[]{:S(2)}) %collective-permute-start.6) | collective-permute-done | bytes 53280 | tf_op jit(solution)/shard_map/ppermute | solution.py:427
  32.0 2.5 %collective-permute-done.34.refs_6_ = f32[256,128]{1,0:T(8,128)S(1)} collective-permute-done((f32[256,128]{1,0:T(8,128)S(1)}, f32[256,128]{1,0:T(8,128)S(1)}, u32[]{:S(2)}, u32[]{:S(2)}) %collective-permute-start.34) | collective-permute-done | bytes 131104 | tf_op jit(solution)/shard_map/ppermute | solution.py:427
  37.1 2.0 collective-permute-done.10.refs_4_
  41.2 2.0 collective-permute-start.9
  43.2 4.1 %unpack.3 = (f32[256,8,128]{2,1,0:T(8,128)}, f32[16,8,128]{2,1,0:T(8,128)}, f32[16,8,128]{2,1,0:T(8,128)}) custom-call(s32[1]{0:T(128)} %bitcast.me_ref, f32[256,128]{1,0:T(8,128)} %get-tuple-element.99.refs_0_, f32[256,128]{1,0:T(8,128)} %copy-done.23, f32[256,128]{1,0:T(8,128)} %copy-done.24, f32[256,128]{1,0:T(8,128)} %copy-done.26, ...), custom_call_target="tpu_custom_call" | custom-call | tf_op jit(solution)/shard_map/unpack/pallas_call | solution.py:494
  49.0 2.6 %collective-permute-start.37 = (f32[16,8,128]{2,1,0:T(8,128)}, f32[16,8,128]{2,1,0:T(8,128)S(1)}, u32[]{:S(2)}, u32[]{:S(2)}) collective-permute-start(f32[16,8,128]{2,1,0:T(8,128)} %get-tuple-element.72), channel_id=1, source_target_pairs={{0,3},{1,0},{2,1},{3,2},{4,7},{5,4},{6,5},{7,6},{8,11},{9,8},{10,9... | collective-permute-start | bytes 196616 | tf_op jit(solution)/shard_map/ppermute | solution.py:488
  51.6 13.6 %setup.1 = (f32[256,8,128]{2,1,0:T(8,128)}, bf16[32,128,256]{2,1,0:T(8,128)(2,1)}, s32[128]{0:T(128)}) custom-call(s32[1]{0:T(128)} %bitcast.me_ref, f32[104,128]{1,0:T(8,128)} %parts.1.refs_0_, f32[104,128]{1,0:T(8,128)} %copy-done.35, f32[104,128]{1,0:T(8,128)} %copy-done.36, f32[104,128]{1,0:T(8,128)} %copy-done.37, f32[104,128]{1,0:T(8,128)} %copy-done.38, ...), custom_call_target="tpu_custom_call" | custom-call | tf_op jit(solution)/shard_map/setup/pallas_call | solution.py:465
  65.9 4.0 %unpack.2 = (f32[256,8,128]{2,1,0:T(8,128)}, f32[16,8,128]{2,1,0:T(8,128)}, f32[16,8,128]{2,1,0:T(8,128)}) custom-call(s32[1]{0:T(128)} %bitcast.me_ref, f32[256,128]{1,0:T(8,128)} %get-tuple-element.107.refs_0_, f32[256,128]{1,0:T(8,128)} %copy-done.32, f32[256,128]{1,0:T(8,128)} %collective-permute-done.8.refs_2_, ...), custom_call_target="tpu_custom_call" | custom-call | tf_op jit(solution)/shard_map/unpack/pallas_call | solution.py:494
  70.0 3.8 %collective-permute-start.15 = (f32[16,8,128]{2,1,0:T(8,128)}, f32[16,8,128]{2,1,0:T(8,128)S(1)}, u32[]{:S(2)}, u32[]{:S(2)}) collective-permute-start(f32[16,8,128]{2,1,0:T(8,128)} %get-tuple-element.52), channel_id=1, source_target_pairs={{0,3},{1,0},{2,1},{3,2},{4,7},{5,4},{6,5},{7,6},{8,11},{9,8},{10,9... | collective-permute-start | bytes 196616 | tf_op jit(solution)/shard_map/ppermute | solution.py:488
  77.3 7.7 %step.12 = (f32[256,8,128]{2,1,0:T(8,128)S(1)}, f32[16,8,128]{2,1,0:T(8,128)S(1)}, f32[16,8,128]{2,1,0:T(8,128)S(1)}) custom-call(s32[1]{0:T(128)} %bitcast.me_ref, s32[128]{0:T(128)S(1)} %copy-done.7, f32[256,8,128]{2,1,0:T(8,128)S(1)} %copy-done.3, f32[256,8,128]{2,1,0:T(8,128)S(1)} %copy-done.1, bf16[32,128,256]{2,1,0:T(8,128)(2,1)S(1)} %copy-done, ...), custom_call_target="tpu_custom_call" | custom-call | flops 524288000 | bytes 8388608 | tf_op jit(solution)/shard_map/step/pallas_call | solution.py:529
  85.0 3.8 %collective-permute-start.39 = (f32[16,8,128]{2,1,0:T(8,128)S(1)}, f32[16,8,128]{2,1,0:T(8,128)S(1)}, u32[]{:S(2)}, u32[]{:S(2)}) collective-permute-start(f32[16,8,128]{2,1,0:T(8,128)S(1)} %get-tuple-element.75), channel_id=1, source_target_pairs={{0,3},{1,0},{2,1},{3,2},{4,7},{5,4},{6,5},{7,6},{8,11},{9,8},{10,9... | collective-permute-start | bytes 196616 | tf_op jit(solution)/shard_map/ppermute | solution.py:488
  88.9 7.7 %step.8 = (f32[256,8,128]{2,1,0:T(8,128)S(1)}, f32[16,8,128]{2,1,0:T(8,128)S(1)}, f32[16,8,128]{2,1,0:T(8,128)S(1)}) custom-call(s32[1]{0:T(128)} %bitcast.me_ref, s32[128]{0:T(128)S(1)} %copy-done.7, f32[256,8,128]{2,1,0:T(8,128)S(1)} %copy-done.4, f32[256,8,128]{2,1,0:T(8,128)S(1)} %copy-done.1, bf16[32,128,256]{2,1,0:T(8,128)(2,1)S(1)} %copy-done, ...), custom_call_target="tpu_custom_call" | custom-call | flops 524288000 | bytes 8388608 | tf_op jit(solution)/shard_map/step/pallas_call | solution.py:529
  96.6 3.8 %collective-permute-start.17 = (f32[16,8,128]{2,1,0:T(8,128)S(1)}, f32[16,8,128]{2,1,0:T(8,128)S(1)}, u32[]{:S(2)}, u32[]{:S(2)}) collective-permute-start(f32[16,8,128]{2,1,0:T(8,128)S(1)} %get-tuple-element.55), channel_id=1, source_target_pairs={{0,3},{1,0},{2,1},{3,2},{4,7},{5,4},{6,5},{7,6},{8,11},{9,8},{10,9... | collective-permute-start | bytes 196616 | tf_op jit(solution)/shard_map/ppermute | solution.py:488
  100.4 7.8 %step.13 = (f32[256,8,128]{2,1,0:T(8,128)S(1)}, f32[16,8,128]{2,1,0:T(8,128)S(1)}, f32[16,8,128]{2,1,0:T(8,128)S(1)}) custom-call(s32[1]{0:T(128)} %bitcast.me_ref, s32[128]{0:T(128)S(1)} %copy-done.7, f32[256,8,128]{2,1,0:T(8,128)S(1)} %get-tuple-element.73.refs_0_.refs_1_, f32[256,8,128]{2,1,0:T(8,128)S(1)} %copy-done.3, f32[256,8,128]{2,1,0:T(8,128)S(1)} %copy-done.1, ...), custom_call_target="tpu_custom_call" | custom-call | flops 524288000 | bytes 8388608 | tf_op jit(solution)/shard_map/step/pallas_call | solution.py:529
  108.2 3.8 %collective-permute-start.41 = (f32[16,8,128]{2,1,0:T(8,128)S(1)}, f32[16,8,128]{2,1,0:T(8,128)S(1)}, u32[]{:S(2)}, u32[]{:S(2)}) collective-permute-start(f32[16,8,128]{2,1,0:T(8,128)S(1)} %get-tuple-element.78), channel_id=1, source_target_pairs={{0,3},{1,0},{2,1},{3,2},{4,7},{5,4},{6,5},{7,6},{8,11},{9,8},{10,9... | collective-permute-start | bytes 196616 | tf_op jit(solution)/shard_map/ppermute | solution.py:488
  112.1 7.7 %step.9 = (f32[256,8,128]{2,1,0:T(8,128)S(1)}, f32[16,8,128]{2,1,0:T(8,128)S(1)}, f32[16,8,128]{2,1,0:T(8,128)S(1)}) custom-call(s32[1]{0:T(128)} %bitcast.me_ref, s32[128]{0:T(128)S(1)} %copy-done.7, f32[256,8,128]{2,1,0:T(8,128)S(1)} %get-tuple-element.53.refs_0_.refs_1_, f32[256,8,128]{2,1,0:T(8,128)S(1)} %copy-done.4, f32[256,8,128]{2,1,0:T(8,128)S(1)} %copy-done.1, ...), custom_call_target="tpu_custom_call" | custom-call | flops 524288000 | bytes 8388608 | tf_op jit(solution)/shard_map/step/pallas_call | solution.py:529
  119.9 3.8 %collective-permute-start.19 = (f32[16,8,128]{2,1,0:T(8,128)S(1)}, f32[16,8,128]{2,1,0:T(8,128)S(1)}, u32[]{:S(2)}, u32[]{:S(2)}) collective-permute-start(f32[16,8,128]{2,1,0:T(8,128)S(1)} %get-tuple-element.58), channel_id=1, source_target_pairs={{0,3},{1,0},{2,1},{3,2},{4,7},{5,4},{6,5},{7,6},{8,11},{9,8},{10,9... | collective-permute-start | bytes 196616 | tf_op jit(solution)/shard_map/ppermute | solution.py:488
  123.7 7.7 %step.14 = (f32[256,8,128]{2,1,0:T(8,128)S(1)}, f32[16,8,128]{2,1,0:T(8,128)S(1)}, f32[16,8,128]{2,1,0:T(8,128)S(1)}) custom-call(s32[1]{0:T(128)} %bitcast.me_ref, s32[128]{0:T(128)S(1)} %copy-done.7, f32[256,8,128]{2,1,0:T(8,128)S(1)} %get-tuple-element.76.refs_0_.refs_1_, f32[256,8,128]{2,1,0:T(8,128)S(1)} %get-tuple-element.73.refs_0_.refs_1_, ...), custom_call_target="tpu_custom_call" | custom-call | flops 524288000 | bytes 8388608 | tf_op jit(solution)/shard_map/step/pallas_call | solution.py:529
  131.5 3.8 %collective-permute-start.43 = (f32[16,8,128]{2,1,0:T(8,128)S(1)}, f32[16,8,128]{2,1,0:T(8,128)S(1)}, u32[]{:S(2)}, u32[]{:S(2)}) collective-permute-start(f32[16,8,128]{2,1,0:T(8,128)S(1)} %get-tuple-element.81), channel_id=1, source_target_pairs={{0,3},{1,0},{2,1},{3,2},{4,7},{5,4},{6,5},{7,6},{8,11},{9,8},{10,9... | collective-permute-start | bytes 196616 | tf_op jit(solution)/shard_map/ppermute | solution.py:488
  135.3 7.7 %step.10 = (f32[256,8,128]{2,1,0:T(8,128)S(1)}, f32[16,8,128]{2,1,0:T(8,128)S(1)}, f32[16,8,128]{2,1,0:T(8,128)S(1)}) custom-call(s32[1]{0:T(128)} %bitcast.me_ref, s32[128]{0:T(128)S(1)} %copy-done.7, f32[256,8,128]{2,1,0:T(8,128)S(1)} %get-tuple-element.56.refs_0_.refs_1_, f32[256,8,128]{2,1,0:T(8,128)S(1)} %get-tuple-element.53.refs_0_.refs_1_, ...), custom_call_target="tpu_custom_call" | custom-call | flops 524288000 | bytes 8388608 | tf_op jit(solution)/shard_map/step/pallas_call | solution.py:529
  143.1 9.5 %step.15 = (f32[256,128]{1,0:T(8,128)S(1)}, f32[256,128]{1,0:T(8,128)S(1)}, f32[256,128]{1,0:T(8,128)S(1)}, f32[256,128]{1,0:T(8,128)S(1)}, f32[256,128]{1,0:T(8...) custom-call(s32[1]{0:T(128)} %bitcast.me_ref, s32[128]{0:T(128)S(1)} %copy-done.7, ...), custom_call_target="tpu_custom_call" | custom-call | flops 524288000 | bytes 8388608 | tf_op jit(solution)/shard_map/step/pallas_call | solution.py:529
  156.1 3.8 %collective-permute-start.21 = (f32[16,8,128]{2,1,0:T(8,128)S(1)}, f32[16,8,128]{2,1,0:T(8,128)S(1)}, u32[]{:S(2)}, u32[]{:S(2)}) collective-permute-start(f32[16,8,128]{2,1,0:T(8,128)S(1)} %get-tuple-element.61), channel_id=1, source_target_pairs={{0,3},{1,0},{2,1},{3,2},{4,7},{5,4},{6,5},{7,6},{8,11},{9,8},{10,9... | collective-permute-start | bytes 196616 | tf_op jit(solution)/shard_map/ppermute | solution.py:488
  161.8 9.5 %step.11 = (f32[256,128]{1,0:T(8,128)S(1)}, f32[256,128]{1,0:T(8,128)S(1)}, f32[256,128]{1,0:T(8,128)S(1)}, f32[256,128]{1,0:T(8,128)S(1)}, f32[256,128]{1,0:T(8...) custom-call(s32[1]{0:T(128)} %bitcast.me_ref, s32[128]{0:T(128)S(1)} %copy-done.7, ...), custom_call_target="tpu_custom_call" | custom-call | flops 524288000 | bytes 8388608 | tf_op jit(solution)/shard_map/step/pallas_call | solution.py:529
  187.9 2.9 %collective-permute-done.27.refs_6_ = f32[256,128]{1,0:T(8,128)S(1)} collective-permute-done((f32[256,128]{1,0:T(8,128)S(1)}, f32[256,128]{1,0:T(8,128)S(1)}, u32[]{:S(2)}, u32[]{:S(2)}) %collective-permute-start.27) | collective-permute-done | bytes 131104 | tf_op jit(solution)/shard_map/ppermute | solution.py:427
  190.9 2.1 collective-permute-done.28.refs_7_
  193.6 5.4 %gather.1 = (f32[4096,128]{1,0:T(8,128)}, f32[64,64]{1,0:T(8,128)}) custom-call(s32[1]{0:T(128)} %bitcast.me_ref, f32[256,128]{1,0:T(8,128)} %copy-done.6, f32[256,128]{1,0:T(8,128)} %copy-done.16, f32[256,128]{1,0:T(8,128)} %copy-done.17, f32[256,128]{1,0:T(8,128)} %copy-done.18, f32[256,128]{1,0:T(8,128)} %copy-done.19, f32[256,128]{1,0:T(8,128)} %copy-done.20, ...), custom_call_target="tpu_custom_call" | custom-call | tf_op jit(solution)/shard_map/gather/pallas_call | solution.py:544
  201.4 2.0 collective-permute-start.52
  209.2 3.9 %collective-permute-done.54 = f32[64,64]{1,0:T(8,128)S(1)} collective-permute-done((f32[64,64]{1,0:T(8,128)S(1)}, f32[64,64]{1,0:T(8,128)S(1)}, u32[]{:S(2)}, u32[]{:S(2)}) %collective-permute-start.54) | collective-permute-done | bytes 16416 | tf_op jit(solution)/shard_map/ppermute | solution.py:562
  213.1 2.8 %collective-permute-start.55 = (f32[64,64]{1,0:T(8,128)S(1)}, f32[64,64]{1,0:T(8,128)S(1)}, u32[]{:S(2)}, u32[]{:S(2)}) collective-permute-start(f32[64,64]{1,0:T(8,128)S(1)} %add.131), channel_id=1, source_target_pairs={{0,2},{1,3},{2,0},{3,1},{4,6},{5,7},{6,4},{7,5},{8,10},{9,11},{10,... | collective-permute-start | bytes 49160 | tf_op jit(solution)/shard_map/ppermute | solution.py:562
  (191 shorter events, 63.4 us)
Async XLA Ops:
  10.9 14.9 %collective-permute-start.29 = (f32[256,128]{1,0:T(8,128)S(1)}, f32[256,128]{1,0:T(8,128)S(1)}, u32[]{:S(2)}, u32[]{:S(2)}) collective-permute-start(f32[256,128]{1,0:T(8,128)S(1)} %get-tuple-element.98), channel_id=1, source_target_pairs={{0,4},{4,0},{8,12},{12,8},{16,20},{20,16},{24,28},{28,24},{1,5},{5... | collective-permute-start | bytes 393224 | tf_op jit(solution)/shard_map/ppermute | solution.py:427
  16.3 11.2 %collective-permute-start.30 = (f32[256,128]{1,0:T(8,128)S(1)}, f32[256,128]{1,0:T(8,128)S(1)}, u32[]{:S(2)}, u32[]{:S(2)}) collective-permute-start(f32[256,128]{1,0:T(8,128)S(1)} %get-tuple-element.97), channel_id=1, source_target_pairs={{0,8},{4,12},{8,0},{12,4},{16,24},{20,28},{24,16},{28,20},{1,9},{5... | collective-permute-start | bytes 393224 | tf_op jit(solution)/shard_map/ppermute | solution.py:427
  16.8 11.8 %collective-permute-start.31 = (f32[256,128]{1,0:T(8,128)S(1)}, f32[256,128]{1,0:T(8,128)S(1)}, u32[]{:S(2)}, u32[]{:S(2)}) collective-permute-start(f32[256,128]{1,0:T(8,128)S(1)} %get-tuple-element.96), channel_id=1, source_target_pairs={{0,12},{4,8},{8,4},{12,0},{16,28},{20,24},{24,20},{28,16},{1,13},{... | collective-permute-start | bytes 393224 | tf_op jit(solution)/shard_map/ppermute | solution.py:427
  17.9 11.1 %collective-permute-start.32 = (f32[256,128]{1,0:T(8,128)S(1)}, f32[256,128]{1,0:T(8,128)S(1)}, u32[]{:S(2)}, u32[]{:S(2)}) collective-permute-start(f32[256,128]{1,0:T(8,128)S(1)} %get-tuple-element.95), channel_id=1, source_target_pairs={{0,16},{4,20},{8,24},{12,28},{16,0},{20,4},{24,8},{28,12},{1,17},{... | collective-permute-start | bytes 393224 | tf_op jit(solution)/shard_map/ppermute | solution.py:427
  28.6 10.6 %collective-permute-start.10 = (f32[256,128]{1,0:T(8,128)S(1)}, f32[256,128]{1,0:T(8,128)S(1)}, u32[]{:S(2)}, u32[]{:S(2)}) collective-permute-start(f32[256,128]{1,0:T(8,128)S(1)} %get-tuple-element.103), channel_id=1, source_target_pairs={{0,16},{4,20},{8,24},{12,28},{16,0},{20,4},{24,8},{28,12},{1,17},{... | collective-permute-start | bytes 393224 | tf_op jit(solution)/shard_map/ppermute | solution.py:427
  29.0 12.1 %collective-permute-start.11 = (f32[256,128]{1,0:T(8,128)S(1)}, f32[256,128]{1,0:T(8,128)S(1)}, u32[]{:S(2)}, u32[]{:S(2)}) collective-permute-start(f32[256,128]{1,0:T(8,128)S(1)} %get-tuple-element.102), channel_id=1, source_target_pairs={{0,20},{4,16},{8,28},{12,24},{16,4},{20,0},{24,12},{28,8},{1,21},{... | collective-permute-start | bytes 393224 | tf_op jit(solution)/shard_map/ppermute | solution.py:427
  30.4 17.0 %collective-permute-start.12 = (f32[256,128]{1,0:T(8,128)S(1)}, f32[256,128]{1,0:T(8,128)S(1)}, u32[]{:S(2)}, u32[]{:S(2)}) collective-permute-start(f32[256,128]{1,0:T(8,128)S(1)} %get-tuple-element.101), channel_id=1, source_target_pairs={{0,24},{4,28},{8,16},{12,20},{16,8},{20,12},{24,0},{28,4},{1,25},{... | collective-permute-start | bytes 393224 | tf_op jit(solution)/shard_map/ppermute | solution.py:427
  34.5 14.5 %collective-permute-start.13 = (f32[256,128]{1,0:T(8,128)S(1)}, f32[256,128]{1,0:T(8,128)S(1)}, u32[]{:S(2)}, u32[]{:S(2)}) collective-permute-start(f32[256,128]{1,0:T(8,128)S(1)} %get-tuple-element.100), channel_id=1, source_target_pairs={{0,28},{4,24},{8,20},{12,16},{16,12},{20,8},{24,4},{28,0},{1,29},{... | collective-permute-start | bytes 393224 | tf_op jit(solution)/shard_map/ppermute | solution.py:427
  36.7 28.6 %collective-permute-start.7 = (f32[256,128]{1,0:T(8,128)S(1)}, f32[256,128]{1,0:T(8,128)S(1)}, u32[]{:S(2)}, u32[]{:S(2)}) collective-permute-start(f32[256,128]{1,0:T(8,128)S(1)} %get-tuple-element.106), channel_id=1, source_target_pairs={{0,4},{4,0},{8,12},{12,8},{16,20},{20,16},{24,28},{28,24},{1,5},{5... | collective-permute-start | bytes 393224 | tf_op jit(solution)/shard_map/ppermute | solution.py:427
  39.2 26.1 %collective-permute-start.8 = (f32[256,128]{1,0:T(8,128)S(1)}, f32[256,128]{1,0:T(8,128)}, u32[]{:S(2)}, u32[]{:S(2)}) collective-permute-start(f32[256,128]{1,0:T(8,128)S(1)} %get-tuple-element.105), channel_id=1, source_target_pairs={{0,8},{4,12},{8,0},{12,4},{16,24},{20,28},{24,16},{28,20},{1,9},{5... | collective-permute-start | bytes 393224 | tf_op jit(solution)/shard_map/ppermute | solution.py:427
  41.2 24.1 %collective-permute-start.9 = (f32[256,128]{1,0:T(8,128)S(1)}, f32[256,128]{1,0:T(8,128)}, u32[]{:S(2)}, u32[]{:S(2)}) collective-permute-start(f32[256,128]{1,0:T(8,128)S(1)} %get-tuple-element.104), channel_id=1, source_target_pairs={{0,12},{4,8},{8,4},{12,0},{16,28},{20,24},{24,20},{28,16},{1,13},{... | collective-permute-start | bytes 393224 | tf_op jit(solution)/shard_map/ppermute | solution.py:427
  47.4 26.5 %collective-permute-start.36 = (f32[16,8,128]{2,1,0:T(8,128)}, f32[16,8,128]{2,1,0:T(8,128)S(1)}, u32[]{:S(2)}, u32[]{:S(2)}) collective-permute-start(f32[16,8,128]{2,1,0:T(8,128)} %get-tuple-element.71), channel_id=1, source_target_pairs={{0,1},{1,2},{2,3},{3,0},{4,5},{5,6},{6,7},{7,4},{8,9},{9,10},{10,1... | collective-permute-start | bytes 196616 | tf_op jit(solution)/shard_map/ppermute | solution.py:488
  49.0 24.8 %collective-permute-start.37 = (f32[16,8,128]{2,1,0:T(8,128)}, f32[16,8,128]{2,1,0:T(8,128)S(1)}, u32[]{:S(2)}, u32[]{:S(2)}) collective-permute-start(f32[16,8,128]{2,1,0:T(8,128)} %get-tuple-element.72), channel_id=1, source_target_pairs={{0,3},{1,0},{2,1},{3,2},{4,7},{5,4},{6,5},{7,6},{8,11},{9,8},{10,9... | collective-permute-start | bytes 196616 | tf_op jit(solution)/shard_map/ppermute | solution.py:488
  69.9 18.9 %collective-permute-start.14 = (f32[16,8,128]{2,1,0:T(8,128)}, f32[16,8,128]{2,1,0:T(8,128)S(1)}, u32[]{:S(2)}, u32[]{:S(2)}) collective-permute-start(f32[16,8,128]{2,1,0:T(8,128)} %get-tuple-element.51), channel_id=1, source_target_pairs={{0,1},{1,2},{2,3},{3,0},{4,5},{5,6},{6,7},{7,4},{8,9},{9,10},{10,1... | collective-permute-start | bytes 196616 | tf_op jit(solution)/shard_map/ppermute | solution.py:488
  70.0 18.8 %collective-permute-start.15 = (f32[16,8,128]{2,1,0:T(8,128)}, f32[16,8,128]{2,1,0:T(8,128)S(1)}, u32[]{:S(2)}, u32[]{:S(2)}) collective-permute-start(f32[16,8,128]{2,1,0:T(8,128)} %get-tuple-element.52), channel_id=1, source_target_pairs={{0,3},{1,0},{2,1},{3,2},{4,7},{5,4},{6,5},{7,6},{8,11},{9,8},{10,9... | collective-permute-start | bytes 196616 | tf_op jit(solution)/shard_map/ppermute | solution.py:488
  85.0 15.4 %collective-permute-start.38 = (f32[16,8,128]{2,1,0:T(8,128)S(1)}, f32[16,8,128]{2,1,0:T(8,128)S(1)}, u32[]{:S(2)}, u32[]{:S(2)}) collective-permute-start(f32[16,8,128]{2,1,0:T(8,128)S(1)} %get-tuple-element.74), channel_id=1, source_target_pairs={{0,1},{1,2},{2,3},{3,0},{4,5},{5,6},{6,7},{7,4},{8,9},{9,10},{10,1... | collective-permute-start | bytes 196616 | tf_op jit(solution)/shard_map/ppermute | solution.py:488
  85.0 15.4 %collective-permute-start.39 = (f32[16,8,128]{2,1,0:T(8,128)S(1)}, f32[16,8,128]{2,1,0:T(8,128)S(1)}, u32[]{:S(2)}, u32[]{:S(2)}) collective-permute-start(f32[16,8,128]{2,1,0:T(8,128)S(1)} %get-tuple-element.75), channel_id=1, source_target_pairs={{0,3},{1,0},{2,1},{3,2},{4,7},{5,4},{6,5},{7,6},{8,11},{9,8},{10,9... | collective-permute-start | bytes 196616 | tf_op jit(solution)/shard_map/ppermute | solution.py:488
  96.5 15.5 %collective-permute-start.16 = (f32[16,8,128]{2,1,0:T(8,128)S(1)}, f32[16,8,128]{2,1,0:T(8,128)S(1)}, u32[]{:S(2)}, u32[]{:S(2)}) collective-permute-start(f32[16,8,128]{2,1,0:T(8,128)S(1)} %get-tuple-element.54), channel_id=1, source_target_pairs={{0,1},{1,2},{2,3},{3,0},{4,5},{5,6},{6,7},{7,4},{8,9},{9,10},{10,1... | collective-permute-start | bytes 196616 | tf_op jit(solution)/shard_map/ppermute | solution.py:488
  96.6 15.5 %collective-permute-start.17 = (f32[16,8,128]{2,1,0:T(8,128)S(1)}, f32[16,8,128]{2,1,0:T(8,128)S(1)}, u32[]{:S(2)}, u32[]{:S(2)}) collective-permute-start(f32[16,8,128]{2,1,0:T(8,128)S(1)} %get-tuple-element.55), channel_id=1, source_target_pairs={{0,3},{1,0},{2,1},{3,2},{4,7},{5,4},{6,5},{7,6},{8,11},{9,8},{10,9... | collective-permute-start | bytes 196616 | tf_op jit(solution)/shard_map/ppermute | solution.py:488
  108.2 15.5 %collective-permute-start.40 = (f32[16,8,128]{2,1,0:T(8,128)S(1)}, f32[16,8,128]{2,1,0:T(8,128)S(1)}, u32[]{:S(2)}, u32[]{:S(2)}) collective-permute-start(f32[16,8,128]{2,1,0:T(8,128)S(1)} %get-tuple-element.77), channel_id=1, source_target_pairs={{0,1},{1,2},{2,3},{3,0},{4,5},{5,6},{6,7},{7,4},{8,9},{9,10},{10,1... | collective-permute-start | bytes 196616 | tf_op jit(solution)/shard_map/ppermute | solution.py:488
  108.2 15.4 %collective-permute-start.41 = (f32[16,8,128]{2,1,0:T(8,128)S(1)}, f32[16,8,128]{2,1,0:T(8,128)S(1)}, u32[]{:S(2)}, u32[]{:S(2)}) collective-permute-start(f32[16,8,128]{2,1,0:T(8,128)S(1)} %get-tuple-element.78), channel_id=1, source_target_pairs={{0,3},{1,0},{2,1},{3,2},{4,7},{5,4},{6,5},{7,6},{8,11},{9,8},{10,9... | collective-permute-start | bytes 196616 | tf_op jit(solution)/shard_map/ppermute | solution.py:488
  119.8 15.5 %collective-permute-start.18 = (f32[16,8,128]{2,1,0:T(8,128)S(1)}, f32[16,8,128]{2,1,0:T(8,128)S(1)}, u32[]{:S(2)}, u32[]{:S(2)}) collective-permute-start(f32[16,8,128]{2,1,0:T(8,128)S(1)} %get-tuple-element.57), channel_id=1, source_target_pairs={{0,1},{1,2},{2,3},{3,0},{4,5},{5,6},{6,7},{7,4},{8,9},{9,10},{10,1... | collective-permute-start | bytes 196616 | tf_op jit(solution)/shard_map/ppermute | solution.py:488
  119.9 15.4 %collective-permute-start.19 = (f32[16,8,128]{2,1,0:T(8,128)S(1)}, f32[16,8,128]{2,1,0:T(8,128)S(1)}, u32[]{:S(2)}, u32[]{:S(2)}) collective-permute-start(f32[16,8,128]{2,1,0:T(8,128)S(1)} %get-tuple-element.58), channel_id=1, source_target_pairs={{0,3},{1,0},{2,1},{3,2},{4,7},{5,4},{6,5},{7,6},{8,11},{9,8},{10,9... | collective-permute-start | bytes 196616 | tf_op jit(solution)/shard_map/ppermute | solution.py:488
  131.4 11.7 %collective-permute-start.42 = (f32[16,8,128]{2,1,0:T(8,128)S(1)}, f32[16,8,128]{2,1,0:T(8,128)S(1)}, u32[]{:S(2)}, u32[]{:S(2)}) collective-permute-start(f32[16,8,128]{2,1,0:T(8,128)S(1)} %get-tuple-element.80), channel_id=1, source_target_pairs={{0,1},{1,2},{2,3},{3,0},{4,5},{5,6},{6,7},{7,4},{8,9},{9,10},{10,1... | collective-permute-start | bytes 196616 | tf_op jit(solution)/shard_map/ppermute | solution.py:488
  131.5 11.6 %collective-permute-start.43 = (f32[16,8,128]{2,1,0:T(8,128)S(1)}, f32[16,8,128]{2,1,0:T(8,128)S(1)}, u32[]{:S(2)}, u32[]{:S(2)}) collective-permute-start(f32[16,8,128]{2,1,0:T(8,128)S(1)} %get-tuple-element.81), channel_id=1, source_target_pairs={{0,3},{1,0},{2,1},{3,2},{4,7},{5,4},{6,5},{7,6},{8,11},{9,8},{10,9... | collective-permute-start | bytes 196616 | tf_op jit(solution)/shard_map/ppermute | solution.py:488
  143.0 13.1 %collective-permute-start.20 = (f32[16,8,128]{2,1,0:T(8,128)S(1)}, f32[16,8,128]{2,1,0:T(8,128)S(1)}, u32[]{:S(2)}, u32[]{:S(2)}) collective-permute-start(f32[16,8,128]{2,1,0:T(8,128)S(1)} %get-tuple-element.60), channel_id=1, source_target_pairs={{0,1},{1,2},{2,3},{3,0},{4,5},{5,6},{6,7},{7,4},{8,9},{9,10},{10,1... | collective-permute-start | bytes 196616 | tf_op jit(solution)/shard_map/ppermute | solution.py:488
  153.3 18.7 %collective-permute-start.44 = (f32[256,128]{1,0:T(8,128)S(1)}, f32[256,128]{1,0:T(8,128)S(1)}, u32[]{:S(2)}, u32[]{:S(2)}) collective-permute-start(f32[256,128]{1,0:T(8,128)S(1)} %get-tuple-element.83), channel_id=1, source_target_pairs={{0,4},{4,0},{8,12},{12,8},{16,20},{20,16},{24,28},{28,24},{1,5},{5... | collective-permute-start | bytes 393224 | tf_op jit(solution)/shard_map/ppermute | solution.py:427
  153.3 20.1 %collective-permute-start.45 = (f32[256,128]{1,0:T(8,128)S(1)}, f32[256,128]{1,0:T(8,128)S(1)}, u32[]{:S(2)}, u32[]{:S(2)}) collective-permute-start(f32[256,128]{1,0:T(8,128)S(1)} %get-tuple-element.84), channel_id=1, source_target_pairs={{0,8},{4,12},{8,0},{12,4},{16,24},{20,28},{24,16},{28,20},{1,9},{5... | collective-permute-start | bytes 393224 | tf_op jit(solution)/shard_map/ppermute | solution.py:427
  153.7 21.8 %collective-permute-start.46 = (f32[256,128]{1,0:T(8,128)S(1)}, f32[256,128]{1,0:T(8,128)S(1)}, u32[]{:S(2)}, u32[]{:S(2)}) collective-permute-start(f32[256,128]{1,0:T(8,128)S(1)} %get-tuple-element.85), channel_id=1, source_target_pairs={{0,12},{4,8},{8,4},{12,0},{16,28},{20,24},{24,20},{28,16},{1,13},{... | collective-permute-start | bytes 393224 | tf_op jit(solution)/shard_map/ppermute | solution.py:427
  155.2 20.3 %collective-permute-start.47 = (f32[256,128]{1,0:T(8,128)S(1)}, f32[256,128]{1,0:T(8,128)S(1)}, u32[]{:S(2)}, u32[]{:S(2)}) collective-permute-start(f32[256,128]{1,0:T(8,128)S(1)} %get-tuple-element.86), channel_id=1, source_target_pairs={{0,16},{4,20},{8,24},{12,28},{16,0},{20,4},{24,8},{28,12},{1,17},{... | collective-permute-start | bytes 393224 | tf_op jit(solution)/shard_map/ppermute | solution.py:427
  161.8 14.5 %collective-permute-start.48 = (f32[256,128]{1,0:T(8,128)S(1)}, f32[256,128]{1,0:T(8,128)S(1)}, u32[]{:S(2)}, u32[]{:S(2)}) collective-permute-start(f32[256,128]{1,0:T(8,128)S(1)} %get-tuple-element.87), channel_id=1, source_target_pairs={{0,20},{4,16},{8,28},{12,24},{16,4},{20,0},{24,12},{28,8},{1,21},{... | collective-permute-start | bytes 393224 | tf_op jit(solution)/shard_map/ppermute | solution.py:427
  176.3 11.6 %collective-permute-start.24 = (f32[256,128]{1,0:T(8,128)S(1)}, f32[256,128]{1,0:T(8,128)S(1)}, u32[]{:S(2)}, u32[]{:S(2)}) collective-permute-start(f32[256,128]{1,0:T(8,128)S(1)} %get-tuple-element.65), channel_id=1, source_target_pairs={{0,12},{4,8},{8,4},{12,0},{16,28},{20,24},{24,20},{28,16},{1,13},{... | collective-permute-start | bytes 393224 | tf_op jit(solution)/shard_map/ppermute | solution.py:427
  (66 other events, 668.2 us)

commit v2 on v1

v2 whole, which is shorter than its diff:
```python
import functools
import math

import jax
import jax.numpy as jnp
import ml_dtypes
import numpy as np
from jax import lax
from jax.experimental import pallas as pl
from jax.experimental.pallas import tpu as pltpu
from jax.sharding import PartitionSpec as P

DEGREE = 4
CHUNKS = 2

STENCIL = (
    -5369.0 / 1800.0,
    12.0 / 7.0,
    -15.0 / 56.0,
    10.0 / 189.0,
    -1.0 / 112.0,
    2.0 / 1925.0,
    -1.0 / 16632.0,
)
SPACING = 0.224
CENTER = 210.5
HALF = 209.5
REACH = 6
TILE = 64
LANES = 128
SUBS = 8
KINETIC = -0.5 / (SPACING * SPACING) / HALF
TAPS = tuple(KINETIC * c for c in STENCIL)
DIAGONAL = 3.0 * TAPS[0] - CENTER / HALF

F32 = jnp.float32
BF16 = jnp.bfloat16
VMEM = pl.BlockSpec(memory_space=pltpu.VMEM)
SMEM = pl.BlockSpec(memory_space=pltpu.SMEM)
ANY = pl.BlockSpec(memory_space=pl.ANY)


def split_halves(matrix):
    high = matrix.astype(ml_dtypes.bfloat16)
    low = (matrix - high.astype(np.float64)).astype(ml_dtypes.bfloat16)
    wide = np.concatenate([high, low], axis=1)
    return np.concatenate([wide, wide], axis=0)


def line_weights():
    own = np.zeros((LANES, LANES))
    halo = np.zeros((LANES, LANES))
    for k in range(1, REACH + 1):
        for z in range(LANES):
            if z + k < LANES:
                own[z + k, z] = TAPS[k]
            else:
                halo[8 + z + k - LANES, z] = TAPS[k]
            if z - k >= 0:
                own[z - k, z] = TAPS[k]
            else:
                halo[REACH + z - k, z] = TAPS[k]
    return np.concatenate([split_halves(own), split_halves(halo)], axis=0)


def halves(value):
    high = value.astype(BF16)
    low = (value - high.astype(F32)).astype(BF16)
    return high, low


def parts_kernel(count, fold, index_ref, proj_ref, root_ref, pot_ref, meta_ref, out_ref):
    out_ref[0:64, :] = pot_ref[...]
    point = lax.broadcasted_iota(jnp.int32, (TILE, TILE), 0)
    width = TILE // fold
    sorted_rows = []
    for atom in range(count):
        order = index_ref[atom : atom + 1, :]
        if fold == 2:
            order = ((order >> 4) & 1) * width + (order >> 5) * 16 + (order & 15)
        hot = (point == order).astype(F32)
        sorted_rows.append(
            lax.dot_general(
                proj_ref[atom],
                hot,
                (((1,), (1,)), ((), ())),
                precision=lax.Precision.HIGHEST,
                preferred_element_type=F32,
            )
            * root_ref[:, atom : atom + 1]
        )
    row = 64
    for first in range(0, count, 2 * fold):
        for f in range(fold):
            out_ref[row : row + 8, :] = jnp.concatenate(
                [sorted_rows[first + q][:, f * width : (f + 1) * width] for q in range(2 * fold)],
                axis=1,
            )
            row += 8
    out_ref[row : row + 8, :] = meta_ref[...]


def setup_kernel(gx, gy, nb, count, fold, me_ref, *refs):
    group = gx * gy
    blocks = refs[:group]
    diag_ref, roots_ref, meta_ref, pots, roots, raw, sem = refs[group:]
    rows = 4 * count
    copies = []
    for d in range(group):
        slot = me_ref[0] ^ d
        i, j = slot // gy, slot % gy
        for b in range(nb):
            copies.append(
                pltpu.make_async_copy(
                    blocks[d].at[pl.ds(0, 64)],
                    pots.at[pl.ds(pl.multiple_of(((j * gx + i) * nb + b) * 64, 64), 64)],
                    sem.at[0],
                )
            )
        copies.append(
            pltpu.make_async_copy(
                blocks[d].at[pl.ds(64, rows)],
                roots.at[pl.ds(pl.multiple_of(slot * rows, 8), rows)],
                sem.at[0],
            )
        )
        copies.append(
            pltpu.make_async_copy(
                blocks[d].at[pl.ds(64 + rows, 8)],
                raw.at[pl.ds(pl.multiple_of(slot * 8, 8), 8)],
                sem.at[0],
            )
        )
    for copy in copies:
        copy.start()
    for copy in copies:
        copy.wait()

    def corners(slot, carry):
        for atom in range(count):
            n = slot * count + atom
            meta_ref[2 * n] = raw[slot * 8, atom].astype(jnp.int32) + (slot % gy) * 64
            meta_ref[2 * n + 1] = raw[slot * 8, count + atom].astype(jnp.int32)
        return carry

    lax.fori_loop(0, group, corners, 0)

    def lines(j, carry):
        for y in range(8):
            for x in range(8):
                value = pots[pl.ds(j * 512 + x * 8 + y, SUBS, stride=64), :]
                diag_ref[(j * 8 + y) * 8 + x] = value * (1.0 / HALF) + DIAGONAL
        return carry

    lax.fori_loop(0, gy, lines, 0)
    sub = lax.broadcasted_iota(jnp.int32, (SUBS, LANES), 0)

    def spread(m, carry):
        for k in range(8):
            parts = [
                jnp.broadcast_to(roots[pl.ds(m * 8 * fold + f * 8 + k, 1), :], (SUBS, LANES))
                for f in range(fold)
            ]
            value = parts[0] if fold == 1 else jnp.where(sub < SUBS // 2, parts[0], parts[1])
            roots_ref[m * 8 + k] = value
        return carry

    lax.fori_loop(0, group * count // (2 * fold), spread, 0)


def pack_edges(values, lane):
    low = high = None
    for slot, value in enumerate(values):
        here = (lane >> 3) == slot
        to_low = pltpu.roll(value, 8 * slot, 1) if slot else value
        to_high = pltpu.roll(value, (8 * slot - (LANES - REACH)) % LANES, 1)
        low = to_low if low is None else jnp.where(here, to_low, low)
        high = to_high if high is None else jnp.where(here, to_high, high)
    return low, high


def send_edges(even, low, high):
    return jnp.where(even, high, low), jnp.where(even, low, high)


def unpack_kernel(gx, gy, nb, me_ref, places_ref, *refs):
    group = gx * gy
    blocks = refs[:group]
    z_ref, one_ref, two_ref, staged, sem = refs[group:]
    size = nb * 64
    copies = []
    for d in range(group):
        slot = me_ref[0] ^ d
        i, j = slot // gy, slot % gy
        copies.append(
            pltpu.make_async_copy(
                blocks[d],
                staged.at[pl.ds(pl.multiple_of((j * gx + i) * size, 64), size)],
                sem.at[0],
            )
        )
    for copy in copies:
        copy.start()
    for copy in copies:
        copy.wait()
    lane = lax.broadcasted_iota(jnp.int32, (SUBS, LANES), 1)
    even = me_ref[1] == 0

    def lines(j, carry):
        for pair in range(4):
            values = []
            for q in range(2):
                y = 2 * pair + q
                for x in range(8):
                    value = staged[pl.ds(j * 512 + x * 8 + y, SUBS, stride=64), :]
                    z_ref[pl.ds(((j * 8 + y) * 8 + x) * SUBS, SUBS)] = value
                    values.append(value)
            low, high = pack_edges(values, lane)
            one_ref[j * 4 + pair], two_ref[j * 4 + pair] = send_edges(even, low, high)
        return carry

    lax.fori_loop(0, gy, lines, 0)


def step_kernel(gx, gy, nb, count, fold, first, last, me_ref, meta_ref, *refs):
    group = gx * gy
    if first:
        z_ref, diag_ref, roots_ref, one_in, two_in, w_ref, sum_ref = refs[:7]
        refs = refs[7:]
    else:
        z_ref, prev_ref, diag_ref, roots_ref, one_in, two_in, w_ref, sum_ref = refs[:8]
        refs = refs[8:]
    if last:
        blocks = refs[:group]
        acc, out_ref, sem = refs[group:]
    else:
        out_ref, one_ref, two_ref, acc = refs
    ny = gy * 8
    lane = lax.broadcasted_iota(jnp.int32, (SUBS, LANES), 1)
    sub = lax.broadcasted_iota(jnp.int32, (SUBS, LANES), 0)
    even = me_ref[1] == 0

    def tile_rows(row):
        return pl.ds(pl.multiple_of(row * SUBS, SUBS), SUBS)

    def second_dim(x, carry):
        values = [z_ref[tile_rows(y * 8 + x)] for y in range(ny)]
        for y in range(ny):
            total = None
            for k in range(1, REACH + 1):
                term = TAPS[k] * (values[(y + k) % ny] + values[(y - k) % ny])
                total = term if total is None else total + term
            acc[tile_rows(y * 8 + x)] = total
        return carry

    lax.fori_loop(0, 8, second_dim, 0)

    width = TILE // fold
    per_tile = 2 * fold

    def atoms(i, carry):
        places = []
        tiles = []
        for j in range(gy):
            for m in range(count // per_tile):
                tile = jnp.zeros((SUBS, LANES), F32)
                for q in range(per_tile):
                    n = (i * gy + j) * count + per_tile * m + q
                    base = meta_ref[2 * n]
                    z0 = meta_ref[2 * n + 1]
                    places.append((base, z0))
                    for t in range(16 // fold):
                        row = base + (t % 4) * 8 + (t // 4) * fold
                        if fold == 1:
                            value = z_ref[tile_rows(row)]
                        else:
                            start = row * SUBS + i * nb
                            value = jnp.where(
                                sub < nb,
                                z_ref[pl.ds(start, SUBS)],
                                z_ref[pl.ds(start + nb, SUBS)],
                            )
                        value = pltpu.roll(
                            value, (4 * t + width * q - z0 + LANES) & (LANES - 1), 1
                        )
                        tile = jnp.where((lane >> 2) == t + q * (width // 4), value, tile)
                tiles.append(tile)
        n_tiles = len(tiles)
        products = []
        for m in range(n_tiles):
            for k in range(8):
                products.append(tiles[m] * roots_ref[(i * n_tiles + m) * 8 + k])
        stacked = jnp.concatenate(products, axis=0)
        sums = jnp.dot(
            jnp.concatenate(halves(stacked), axis=1), sum_ref[...], preferred_element_type=F32
        )
        for m in range(n_tiles):
            spread = None
            for k in range(8):
                at = (m * 8 + k) * SUBS
                coeff = sums[at : at + SUBS]
                if fold == 2:
                    coeff = coeff + pltpu.roll(coeff, nb, 0)
                term = coeff * roots_ref[(i * n_tiles + m) * 8 + k]
                spread = term if spread is None else spread + term
            for q in range(per_tile):
                base, z0 = places[m * per_tile + q]
                inside = (lane >= z0) & (lane < z0 + 4)
                if fold == 1:
                    inside = inside & (sub // nb == i)
                for t in range(16 // fold):
                    row = base + (t % 4) * 8 + (t // 4) * fold
                    value = pltpu.roll(
                        spread, (z0 - 4 * t - width * q + LANES) & (LANES - 1), 1
                    )
                    value = jnp.where(inside, value, 0.0)
                    if fold == 1:
                        acc[tile_rows(row)] += value
                    else:
                        start = row * SUBS + i * nb
                        acc[pl.ds(start, SUBS)] += jnp.where(sub < nb, value, 0.0)
                        acc[pl.ds(start + nb, SUBS)] += jnp.where(sub < nb, 0.0, value)
        return carry

    lax.fori_loop(0, gx, atoms, 0)

    def rest(four, carry):
        own = z_ref[pl.ds(pl.multiple_of(four * 32 * SUBS, 32 * SUBS), 32 * SUBS)]
        joined = []
        for q in range(2):
            one = one_in[2 * four + q]
            two = two_in[2 * four + q]
            below = jnp.where(even, two, one)
            above = jnp.where(even, one, two)
            for slot in range(16):
                left = pltpu.roll(below, (-8 * slot) % LANES, 1)
                right = pltpu.roll(above, (8 - 8 * slot) % LANES, 1)
                joined.append(jnp.where(lane < 8, left, right))
        halo = jnp.concatenate(joined, axis=0)
        operand = jnp.concatenate([*halves(own), *halves(halo)], axis=1)
        product = jnp.dot(operand, w_ref[...], preferred_element_type=F32)
        third = product[:, :LANES] + product[:, LANES:]
        results = []
        for q in range(4):
            values = [own[(8 * q + x) * SUBS : (8 * q + x + 1) * SUBS] for x in range(8)]
            after = [pltpu.roll(value, SUBS - nb, 0) for value in values]
            before = after if gx == 2 else [pltpu.roll(value, nb, 0) for value in values]
            wide = before + values + after
            for x in range(8):
                at = 8 * q + x
                here = tile_rows(four * 32 + at)
                total = acc[here] + third[at * SUBS : (at + 1) * SUBS]
                total = total + diag_ref[four * 32 + at] * values[x]
                for k in range(1, REACH + 1):
                    total = total + TAPS[k] * (wide[8 + x + k] + wide[8 + x - k])
                if not first:
                    total = 2.0 * total - prev_ref[here]
                results.append(total)
                if last:
                    y = four * 4 + q
                    start = (y // 8) * 512 + y % 8 + x * 8
                    out_ref[pl.ds(start, SUBS, stride=64), :] = total
                else:
                    out_ref[here] = total
        if not last:
            for q in range(2):
                low, high = pack_edges(results[16 * q : 16 * q + 16], lane)
                one_ref[2 * four + q], two_ref[2 * four + q] = send_edges(even, low, high)
        return carry

    lax.fori_loop(0, gy * 2, rest, 0, unroll=2)
    if last:
        size = nb * 64
        copies = []
        for d in range(group):
            slot = me_ref[0] ^ d
            i, j = slot // gy, slot % gy
            copies.append(
                pltpu.make_async_copy(
                    out_ref.at[pl.ds(pl.multiple_of((j * gx + i) * size, 64), size)],
                    blocks[d],
                    sem.at[0],
                )
            )
        for copy in copies:
            copy.start()
        for copy in copies:
            copy.wait()


def gather_kernel(group, nb, bands, me_ref, *refs):
    blocks = refs[: CHUNKS * group]
    out_ref, gram_ref, field, sem = refs[CHUNKS * group :]
    size = nb * 64
    copies = []
    for chunk in range(CHUNKS):
        for d in range(group):
            slot = me_ref[0] ^ d
            row = (chunk * group + slot) * size
            copies.append(
                pltpu.make_async_copy(
                    blocks[chunk * group + d],
                    field.at[pl.ds(pl.multiple_of(row, 64), size)],
                    sem.at[0],
                )
            )
    for copy in copies:
        copy.start()
    for copy in copies:
        copy.wait()
    store = pltpu.make_async_copy(field, out_ref, sem.at[0])
    store.start()
    gram_ref[...] = jnp.zeros_like(gram_ref)

    def cells(n, carry):
        total = None
        for m in range(4):
            pieces = []
            for c in range(2):
                cell = n * 8 + m * 2 + c
                pieces.append(
                    jnp.concatenate(
                        [
                            field[pl.ds(g * SUBS * 64 + cell, SUBS, stride=64), :]
                            for g in range(bands // SUBS)
                        ],
                        axis=0,
                    )
                )
            value = jnp.concatenate(pieces, axis=1)
            high, low = halves(value)
            both = jnp.concatenate([high, low], axis=0)
            product = lax.dot_general(
                both, both, (((1,), (1,)), ((), ())), preferred_element_type=F32
            )
            total = product if total is None else total + product
        gram_ref[...] += (
            total[:bands, :bands]
            + total[bands:, :bands]
            + total[:bands, bands:]
            + total[bands:, bands:]
        )
        return carry

    lax.fori_loop(0, 8, cells, 0)
    store.wait()


def shape(*dims, dtype=F32):
    return jax.ShapeDtypeStruct(dims, dtype)


def cost(microseconds):
    return pl.CostEstimate(
        flops=int(microseconds * 1e9), bytes_accessed=int(microseconds * 3e6), transcendentals=0
    )


def shards(panel, potential, atom_corner, proj_index, projectors, couplings):
    bands, size_x, size_y, size_z = panel.shape
    count, nproj = couplings.shape
    gx, gy, gz = lax.axis_size("gx"), lax.axis_size("gy"), lax.axis_size("gz")
    group = gx * gy
    nb = bands // (CHUNKS * group)
    fold = 2 if gx == 2 else 1
    column = ("gx", "gy")
    me = lax.axis_index("gx") * gy + lax.axis_index("gy")
    me_z = lax.axis_index("gz")
    me_arr = jnp.stack([me, me_z % 2])
    rows = gy * 64
    pairs = gy * 4

    def swap(block, d):
        return lax.ppermute(block, column, [(s, s ^ d) for s in range(group)])

    def swap_z(block, d):
        return lax.ppermute(block, "gz", [(s, s ^ d) for s in range(gz)])

    anchor = jnp.stack(
        [
            lax.axis_index("gx") * size_x,
            lax.axis_index("gy") * size_y,
            me_z * size_z,
        ]
    )
    local = atom_corner - anchor[None, :]
    meta = jnp.concatenate([local[:, 1] * 8 + local[:, 0], local[:, 2]]).astype(F32)
    meta = jnp.broadcast_to(jnp.pad(meta, (0, LANES - 2 * count))[None], (8, LANES))
    part_rows = 64 + 4 * count + 8
    parts = pl.pallas_call(
        functools.partial(parts_kernel, count, fold),
        out_shape=shape(part_rows, LANES),
        in_specs=[VMEM] * 5,
        out_specs=VMEM,
        cost_estimate=cost(2),
        name="parts",
    )(
        proj_index,
        projectors,
        jnp.sqrt(couplings * (1.0 / HALF)).T,
        potential.reshape(64, LANES),
        meta,
    )
    others = [parts] + [swap(parts, d) for d in range(1, group)]

    field = panel.reshape(bands * 64, LANES)
    size = nb * 64
    forward = []
    for chunk in range(CHUNKS):
        own = [
            lax.dynamic_slice_in_dim(field, (chunk * group + (me ^ d)) * size, size, 0)
            for d in range(group)
        ]
        forward.append([own[0]] + [swap(own[d], d) for d in range(1, group)])

    root_tiles = group * count * 8 // (2 * fold)
    diag, roots, places = pl.pallas_call(
        functools.partial(setup_kernel, gx, gy, nb, count, fold),
        out_shape=[
            shape(rows, SUBS, LANES),
            shape(root_tiles, SUBS, LANES),
            shape(2 * group * count, dtype=jnp.int32),
        ],
        in_specs=[SMEM] + [ANY] * group,
        out_specs=[VMEM, VMEM, SMEM],
        scratch_shapes=[
            pltpu.VMEM((rows * SUBS, LANES), F32),
            pltpu.VMEM((group * 4 * count, LANES), F32),
            pltpu.SMEM((group * 8, LANES), F32),
            pltpu.SemaphoreType.DMA((1,)),
        ],
        cost_estimate=cost(4),
        name="setup",
    )(me_arr, *others)

    weights = jnp.asarray(line_weights())
    summing = np.kron(np.eye(2 * fold), np.ones((TILE // fold, TILE // fold)))
    summing = jnp.asarray(np.concatenate([summing, summing], axis=0).astype(ml_dtypes.bfloat16))
    pair_one = [(s, s ^ 1) for s in range(gz)]
    pair_two = [(s, (s + (1 if s % 2 else -1)) % gz) for s in range(gz)]

    tile_shape = shape(rows * SUBS, LANES)
    edge_shape = shape(pairs, SUBS, LANES)
    states = []
    for chunk in range(CHUNKS):
        tiles, one, two = pl.pallas_call(
            functools.partial(unpack_kernel, gx, gy, nb),
            out_shape=[tile_shape, edge_shape, edge_shape],
            in_specs=[SMEM, SMEM] + [ANY] * group,
            out_specs=[VMEM] * 3,
            scratch_shapes=[
                pltpu.VMEM((rows * SUBS, LANES), F32),
                pltpu.SemaphoreType.DMA((1,)),
            ],
            cost_estimate=cost(3),
            name="unpack",
        )(me_arr, places, *forward[chunk])
        states.append((None, tiles, one, two))

    results = [None] * CHUNKS
    for degree_step in range(DEGREE):
        first, last = degree_step == 0, degree_step == DEGREE - 1
        for chunk in range(CHUNKS):
            prev, tiles, one, two = states[chunk]
            one = lax.ppermute(one, "gz", pair_one)
            two = lax.ppermute(two, "gz", pair_two)
            operands = [me_arr, places, tiles]
            if not first:
                operands.append(prev)
            operands += [diag, roots, one, two, weights, summing]
            scratch = [pltpu.VMEM((rows * SUBS, LANES), F32)]
            if last:
                out_shape = [shape(size, LANES)] * group
                out_specs = [ANY] * group
                scratch += [
                    pltpu.VMEM((rows * SUBS, LANES), F32),
                    pltpu.SemaphoreType.DMA((1,)),
                ]
            else:
                out_shape = [tile_shape, edge_shape, edge_shape]
                out_specs = [VMEM] * 3
            outs = pl.pallas_call(
                functools.partial(step_kernel, gx, gy, nb, count, fold, first, last),
                out_shape=out_shape,
                in_specs=[SMEM, SMEM] + [VMEM] * (len(operands) - 2),
                out_specs=out_specs,
                scratch_shapes=scratch,
                compiler_params=pltpu.CompilerParams(vmem_limit_bytes=24 << 20),
                cost_estimate=cost(5),
                name="step",
            )(*operands)
            if last:
                results[chunk] = [outs[0]] + [swap(outs[d], d) for d in range(1, group)]
            else:
                states[chunk] = (tiles, *outs)

    filtered, gram = pl.pallas_call(
        functools.partial(gather_kernel, group, nb, bands),
        out_shape=[shape(bands * 64, LANES), shape(bands, bands)],
        in_specs=[SMEM] + [ANY] * (CHUNKS * group),
        out_specs=[ANY, VMEM],
        scratch_shapes=[
            pltpu.VMEM((bands * 64, LANES), F32),
            pltpu.SemaphoreType.DMA((1,)),
        ],
        cost_estimate=cost(5),
        name="gather",
    )(me_arr, *[block for chunk in results for block in chunk])

    total_cells = size_x * size_y * size_z * group * gz
    gram = gram * (1.0 / total_cells)
    gram = gram + swap(gram, 1)
    d = 2
    while d < group:
        if 2 * d < group:
            gram = gram + (swap(gram, d) + swap(gram, 2 * d) + swap(gram, 3 * d))
        else:
            gram = gram + swap(gram, d)
        d *= 4
    share = bands // gz
    terms = []
    for d in range(gz):
        term = lax.dynamic_slice_in_dim(gram, (me_z ^ d) * share, share, 0)
        terms.append(swap_z(term, d) if d else term)
    return filtered.reshape(panel.shape), sum(terms[1:], terms[0])


def solution(mesh):
    placed = (
        P(None, "gx", "gy", "gz"),
        P("gx", "gy", "gz"),
        P(("gx", "gy", "gz"), None),
        P(("gx", "gy", "gz"), None),
        P(("gx", "gy", "gz"), None, None),
        P(("gx", "gy", "gz"), None),
    )
    return jax.shard_map(
        shards,
        mesh=mesh,
        in_specs=placed,
        out_specs=(P(None, "gx", "gy", "gz"), P("gz", None)),
        check_vma=False,
    )
```

time: 219 us -> 168 us (0.77)
  Pallas kernels: 94.6 us -> 65 us
  waiting for transfers between devices: 36 us -> 24.5 us
  starting transfers between devices: 73.6 us -> 68 us
  local copies, waits for them, and re-layouts: 10.4 us -> 4.94 us
    pallas_call x10, Pallas kernels: 81 us -> 51.1 us  [the longest x8 44.3 us: shards(): pl.pallas_call(functools.partial(step_kernel, gx, gy, nb, count, fold, fi...]
    ppermute x38 -> x39, waiting for transfers between devices: 28.1 us -> 21.5 us  [swap(): return lax.ppermute(block, column, [(s, s ^ d) for s in range(group)])]
    ppermute x18 -> x19, starting transfers between devices: 34.1 us -> 27.7 us  [the longest x8 15.5 us: shards(): two = lax.ppermute(two, 'gz', pair_two)]
    ppermute x18 -> x19, waiting for transfers between devices: 7.84 us -> 3.03 us  [the longest x3 2.99 us: swap_z(): return lax.ppermute(block, 'gz', [(s, s ^ d) for s in range(gz)])]
    unnamed x85 -> x83, local copies, waits for them, and re-layouts: 7.31 us -> 3.4 us
    ppermute x38 -> x39, starting transfers between devices: 39.5 us -> 40.3 us  [swap(): return lax.ppermute(block, column, [(s, s ^ d) for s in range(group)])]
  transfers between devices with their start and end apart: 56 -> 58, of which waited for: 19 -> 16; matrix products, arithmetic and copies ran while one was open for 1% -> 1% of each run, Pallas kernels for 40% -> 34%
where the time goes in v2:
time: 168 us
  starting transfers between devices  68 us (40%)
  Pallas kernels  65 us (39%)
  waiting for transfers between devices  24.5 us (15%)
  local copies, waits for them, and re-layouts  4.94 us (3%)
  other arithmetic  4.3 us (3%)
    pallas_call x8, Pallas kernels, shards(): pl.pallas_call(functools.partial(step_kernel, gx, gy, nb, count, fold, fi...  44.3 us
    ppermute x39, starting transfers between devices, swap(): return lax.ppermute(block, column, [(s, s ^ d) for s in range(group)])  40.3 us
    ppermute x39, waiting for transfers between devices, swap(): return lax.ppermute(block, column, [(s, s ^ d) for s in range(group)])  21.5 us
    ppermute x8, starting transfers between devices, shards(): two = lax.ppermute(two, 'gz', pair_two)  15.5 us
    pallas_call x2, Pallas kernels, shards(): pl.pallas_call(functools.partial(unpack_kernel, gx, gy, nb), out_shape=[t...  7.83 us
    ppermute x8, starting transfers between devices, shards(): one = lax.ppermute(one, 'gz', pair_one)  7.73 us
    pallas_call x1, Pallas kernels, shards(): pl.pallas_call(functools.partial(gather_kernel, group, nb, bands), out_sh...  6.12 us
    pallas_call x1, Pallas kernels, shards(): pl.pallas_call(functools.partial(setup_kernel, gx, gy, nb, count, fold),...  4.59 us
  transfers between devices with their start and end apart: 58, of which 16 were waited for; matrix products, arithmetic and copies ran while one was open for 1% of the time, Pallas kernels for 34%

profile of v2, /device:TPU:0, one launch (start us, length us, event | category | flops | bytes accessed | tf_op | source)
XLA Modules:
  0.0 167.9 jit_solution(9702739985167258332)
XLA Ops:
  3.5 2.1 %parts.1.refs_0_ = f32[104,128]{1,0:T(8,128)} custom-call(s32[8,64]{1,0:T(8,128)} %index_ref.1, f32[8,8,64]{2,1,0:T(8,128)} %proj_ref.1, f32[8,8]{1,0:T(8,128)} %sqrt_bitcast_fusion.root_ref, f32[64,128]{1,0:T(8,128)} %bitcast.15, f32[8,128]{1,0:T(8,128)} %broadcast_in_dim.2.meta_ref), custom_call_target="tpu_custom_call" | custom-call | flops 2000000000 | bytes 6000000 | tf_op jit(solution)/shard_map/parts/pallas_call | solution.py:490
  6.1 2.5 %collective-permute-start.1 = (f32[104,128]{1,0:T(8,128)}, f32[104,128]{1,0:T(8,128)}, u32[]{:S(2)}, u32[]{:S(2)}) collective-permute-start(f32[104,128]{1,0:T(8,128)} %parts.1.refs_0_), channel_id=1, source_target_pairs={{0,8},{4,12},{8,0},{12,4},{16,24},{20,28},{24,16},{28,20},{1,9},{5... | collective-permute-start | bytes 159752 | tf_op jit(solution)/shard_map/ppermute | solution.py:474
  10.5 2.6 %collective-permute-start.5 = (f32[104,128]{1,0:T(8,128)}, f32[104,128]{1,0:T(8,128)}, u32[]{:S(2)}, u32[]{:S(2)}) collective-permute-start(f32[104,128]{1,0:T(8,128)} %parts.1.refs_0_), channel_id=1, source_target_pairs={{0,24},{4,28},{8,16},{12,20},{16,8},{20,12},{24,0},{28,4},{1,25},{... | collective-permute-start | bytes 159752 | tf_op jit(solution)/shard_map/ppermute | solution.py:474
  18.5 4.1 %collective-permute-done.6.refs_7_ = f32[104,128]{1,0:T(8,128)S(1)} collective-permute-done((f32[104,128]{1,0:T(8,128)}, f32[104,128]{1,0:T(8,128)S(1)}, u32[]{:S(2)}, u32[]{:S(2)}) %collective-permute-start.6) | collective-permute-done | bytes 53280 | tf_op jit(solution)/shard_map/ppermute | solution.py:474
  23.4 2.0 %collective-permute-start.34 = (f32[256,128]{1,0:T(8,128)S(1)}, f32[256,128]{1,0:T(8,128)S(1)}, u32[]{:S(2)}, u32[]{:S(2)}) collective-permute-start(f32[256,128]{1,0:T(8,128)S(1)} %get-tuple-element.93), channel_id=1, source_target_pairs={{0,24},{4,28},{8,16},{12,20},{16,8},{20,12},{24,0},{28,4},{1,25},{... | collective-permute-start | bytes 393224 | tf_op jit(solution)/shard_map/ppermute | solution.py:474
  27.9 4.6 %setup.1 = (f32[256,8,128]{2,1,0:T(8,128)}, f32[128,8,128]{2,1,0:T(8,128)}, s32[128]{0:T(128)}) custom-call(s32[2]{0:T(128)} %pad_add_fusion.me_ref, f32[104,128]{1,0:T(8,128)} %parts.1.refs_0_, f32[104,128]{1,0:T(8,128)} %copy-done.39, f32[104,128]{1,0:T(8,128)} %collective-permute-done.1.refs_2_, f32[104,128]{1,0:T(8,128)} %collective-permute-done.2.refs_3_, ...), custom_call_target="tpu_custom_call" | custom-call | flops 4000000000 | bytes 12000000 | tf_op jit(solution)/shard_map/setup/pallas_call | solution.py:517
  32.5 2.0 %collective-permute-start.12 = (f32[256,128]{1,0:T(8,128)S(1)}, f32[256,128]{1,0:T(8,128)S(1)}, u32[]{:S(2)}, u32[]{:S(2)}) collective-permute-start(f32[256,128]{1,0:T(8,128)S(1)} %get-tuple-element.101), channel_id=1, source_target_pairs={{0,24},{4,28},{8,16},{12,20},{16,8},{20,12},{24,0},{28,4},{1,25},{... | collective-permute-start | bytes 393224 | tf_op jit(solution)/shard_map/ppermute | solution.py:474
  41.2 3.9 %unpack.3 = (f32[2048,128]{1,0:T(8,128)}, f32[16,8,128]{2,1,0:T(8,128)}, f32[16,8,128]{2,1,0:T(8,128)}) custom-call(s32[2]{0:T(128)} %pad_add_fusion.me_ref, s32[128]{0:T(128)} %get-tuple-element.47.places_ref.meta_ref, f32[256,128]{1,0:T(8,128)} %get-tuple-element.99.refs_0_, f32[256,128]{1,0:T(8,128)} %copy-done.11, f32[256,128]{1,0:T(8,128)} %copy-done.12, ...), custom_call_target="tpu_custom_call" | custom-call | flops 3000000000 | bytes 9000000 | tf_op jit(solution)/shard_map/unpack/pallas_call | solution.py:546
  46.7 2.9 %collective-permute-start.37 = (f32[16,8,128]{2,1,0:T(8,128)}, f32[16,8,128]{2,1,0:T(8,128)S(1)}, u32[]{:S(2)}, u32[]{:S(2)}) collective-permute-start(f32[16,8,128]{2,1,0:T(8,128)} %get-tuple-element.72), channel_id=1, source_target_pairs={{0,3},{1,2},{2,1},{3,0},{4,7},{5,6},{6,5},{7,4},{8,11},{9,10},{10,... | collective-permute-start | bytes 196616 | tf_op jit(solution)/shard_map/ppermute | solution.py:566
  51.0 4.0 %unpack.2 = (f32[2048,128]{1,0:T(8,128)}, f32[16,8,128]{2,1,0:T(8,128)}, f32[16,8,128]{2,1,0:T(8,128)}) custom-call(s32[2]{0:T(128)} %pad_add_fusion.me_ref, s32[128]{0:T(128)} %get-tuple-element.47.places_ref.meta_ref, f32[256,128]{1,0:T(8,128)} %get-tuple-element.107.refs_0_, f32[256,128]{1,0:T(8,128)} %copy-done.32, f32[256,128]{1,0:T(8,128)} %copy-done.34, ...), custom_call_target="tpu_custom_call" | custom-call | flops 3000000000 | bytes 9000000 | tf_op jit(solution)/shard_map/unpack/pallas_call | solution.py:546
  55.9 2.5 %collective-permute-start.15 = (f32[16,8,128]{2,1,0:T(8,128)}, f32[16,8,128]{2,1,0:T(8,128)S(1)}, u32[]{:S(2)}, u32[]{:S(2)}) collective-permute-start(f32[16,8,128]{2,1,0:T(8,128)} %get-tuple-element.52), channel_id=1, source_target_pairs={{0,3},{1,2},{2,1},{3,0},{4,7},{5,6},{6,5},{7,4},{8,11},{9,10},{10,... | collective-permute-start | bytes 196616 | tf_op jit(solution)/shard_map/ppermute | solution.py:566
  58.5 5.0 %step.12 = (f32[2048,128]{1,0:T(8,128)S(1)}, f32[16,8,128]{2,1,0:T(8,128)S(1)}, f32[16,8,128]{2,1,0:T(8,128)S(1)}) custom-call(s32[2]{0:T(128)S(1)} %copy-done.2, s32[128]{0:T(128)S(1)} %copy-done.9, f32[2048,128]{1,0:T(8,128)S(1)} %copy-done.3, f32[256,8,128]{2,1,0:T(8,128)S(1)} %copy-done.5, f32[128,8,128]{2,1,0:T(8,128)S(1)} %copy-done.6, ...), custom_call_target="tpu_custom_call" | custom-call | flops 5000000000 | bytes 15000000 | tf_op jit(solution)/shard_map/step/pallas_call | solution.py:582
  65.2 5.0 %step.8 = (f32[2048,128]{1,0:T(8,128)S(1)}, f32[16,8,128]{2,1,0:T(8,128)S(1)}, f32[16,8,128]{2,1,0:T(8,128)S(1)}) custom-call(s32[2]{0:T(128)S(1)} %copy-done.2, s32[128]{0:T(128)S(1)} %copy-done.9, f32[2048,128]{1,0:T(8,128)S(1)} %copy-done.4, f32[256,8,128]{2,1,0:T(8,128)S(1)} %copy-done.5, f32[128,8,128]{2,1,0:T(8,128)S(1)} %copy-done.6, ...), custom_call_target="tpu_custom_call" | custom-call | flops 5000000000 | bytes 15000000 | tf_op jit(solution)/shard_map/step/pallas_call | solution.py:582
  71.2 2.5 %collective-permute-start.17 = (f32[16,8,128]{2,1,0:T(8,128)S(1)}, f32[16,8,128]{2,1,0:T(8,128)S(1)}, u32[]{:S(2)}, u32[]{:S(2)}) collective-permute-start(f32[16,8,128]{2,1,0:T(8,128)S(1)} %get-tuple-element.55), channel_id=1, source_target_pairs={{0,3},{1,2},{2,1},{3,0},{4,7},{5,6},{6,5},{7,4},{8,11},{9,10},{10,... | collective-permute-start | bytes 196616 | tf_op jit(solution)/shard_map/ppermute | solution.py:566
  73.7 5.1 %step.13 = (f32[2048,128]{1,0:T(8,128)S(1)}, f32[16,8,128]{2,1,0:T(8,128)S(1)}, f32[16,8,128]{2,1,0:T(8,128)S(1)}) custom-call(s32[2]{0:T(128)S(1)} %copy-done.2, s32[128]{0:T(128)S(1)} %copy-done.9, f32[2048,128]{1,0:T(8,128)S(1)} %get-tuple-element.73.refs_0_.refs_1_, f32[2048,128]{1,0:T(8,128)S(1)} %copy-done.3, f32[256,8,128]{2,1,0:T(8,128)S(1)} %copy-done.5, ...), custom_call_target="tpu_custom_call" | custom-call | flops 5000000000 | bytes 15000000 | tf_op jit(solution)/shard_map/step/pallas_call | solution.py:582
  80.5 5.1 %step.9 = (f32[2048,128]{1,0:T(8,128)S(1)}, f32[16,8,128]{2,1,0:T(8,128)S(1)}, f32[16,8,128]{2,1,0:T(8,128)S(1)}) custom-call(s32[2]{0:T(128)S(1)} %copy-done.2, s32[128]{0:T(128)S(1)} %copy-done.9, f32[2048,128]{1,0:T(8,128)S(1)} %get-tuple-element.53.refs_0_.refs_1_, f32[2048,128]{1,0:T(8,128)S(1)} %copy-done.4, f32[256,8,128]{2,1,0:T(8,128)S(1)} %copy-done.5, ...), custom_call_target="tpu_custom_call" | custom-call | flops 5000000000 | bytes 15000000 | tf_op jit(solution)/shard_map/step/pallas_call | solution.py:582
  86.5 2.5 %collective-permute-start.19 = (f32[16,8,128]{2,1,0:T(8,128)S(1)}, f32[16,8,128]{2,1,0:T(8,128)S(1)}, u32[]{:S(2)}, u32[]{:S(2)}) collective-permute-start(f32[16,8,128]{2,1,0:T(8,128)S(1)} %get-tuple-element.58), channel_id=1, source_target_pairs={{0,3},{1,2},{2,1},{3,0},{4,7},{5,6},{6,5},{7,4},{8,11},{9,10},{10,... | collective-permute-start | bytes 196616 | tf_op jit(solution)/shard_map/ppermute | solution.py:566
  89.0 5.1 %step.14 = (f32[2048,128]{1,0:T(8,128)S(1)}, f32[16,8,128]{2,1,0:T(8,128)S(1)}, f32[16,8,128]{2,1,0:T(8,128)S(1)}) custom-call(s32[2]{0:T(128)S(1)} %copy-done.2, s32[128]{0:T(128)S(1)} %copy-done.9, f32[2048,128]{1,0:T(8,128)S(1)} %get-tuple-element.76.refs_0_.refs_1_, f32[2048,128]{1,0:T(8,128)S(1)} %get-tuple-element.73.refs_0_.refs_1_, ...), custom_call_target="tpu_custom_call" | custom-call | flops 5000000000 | bytes 15000000 | tf_op jit(solution)/shard_map/step/pallas_call | solution.py:582
  95.8 5.1 %step.10 = (f32[2048,128]{1,0:T(8,128)S(1)}, f32[16,8,128]{2,1,0:T(8,128)S(1)}, f32[16,8,128]{2,1,0:T(8,128)S(1)}) custom-call(s32[2]{0:T(128)S(1)} %copy-done.2, s32[128]{0:T(128)S(1)} %copy-done.9, f32[2048,128]{1,0:T(8,128)S(1)} %get-tuple-element.56.refs_0_.refs_1_, f32[2048,128]{1,0:T(8,128)S(1)} %get-tuple-element.53.refs_0_.refs_1_, ...), custom_call_target="tpu_custom_call" | custom-call | flops 5000000000 | bytes 15000000 | tf_op jit(solution)/shard_map/step/pallas_call | solution.py:582
  101.8 2.5 %collective-permute-start.21 = (f32[16,8,128]{2,1,0:T(8,128)S(1)}, f32[16,8,128]{2,1,0:T(8,128)S(1)}, u32[]{:S(2)}, u32[]{:S(2)}) collective-permute-start(f32[16,8,128]{2,1,0:T(8,128)S(1)} %get-tuple-element.61), channel_id=1, source_target_pairs={{0,3},{1,2},{2,1},{3,0},{4,7},{5,6},{6,5},{7,4},{8,11},{9,10},{10,... | collective-permute-start | bytes 196616 | tf_op jit(solution)/shard_map/ppermute | solution.py:566
  104.3 7.0 %step.15 = (f32[256,128]{1,0:T(8,128)S(1)}, f32[256,128]{1,0:T(8,128)S(1)}, f32[256,128]{1,0:T(8,128)S(1)}, f32[256,128]{1,0:T(8,128)S(1)}, f32[256,128]{1,0:T(8...) custom-call(s32[2]{0:T(128)S(1)} %copy-done.2, s32[128]{0:T(128)S(1)} %copy-done.9, ...), custom_call_target="tpu_custom_call" | custom-call | flops 5000000000 | bytes 15000000 | tf_op jit(solution)/shard_map/step/pallas_call | solution.py:582
  111.4 1.9 %collective-permute-start.45 = (f32[256,128]{1,0:T(8,128)S(1)}, f32[256,128]{1,0:T(8,128)S(1)}, u32[]{:S(2)}, u32[]{:S(2)}) collective-permute-start(f32[256,128]{1,0:T(8,128)S(1)} %get-tuple-element.84), channel_id=1, source_target_pairs={{0,8},{4,12},{8,0},{12,4},{16,24},{20,28},{24,16},{28,20},{1,9},{5... | collective-permute-start | bytes 393224 | tf_op jit(solution)/shard_map/ppermute | solution.py:474
  115.0 6.9 %step.11 = (f32[256,128]{1,0:T(8,128)S(1)}, f32[256,128]{1,0:T(8,128)S(1)}, f32[256,128]{1,0:T(8,128)S(1)}, f32[256,128]{1,0:T(8,128)S(1)}, f32[256,128]{1,0:T(8...) custom-call(s32[2]{0:T(128)S(1)} %copy-done.2, s32[128]{0:T(128)S(1)} %copy-done.9, ...), custom_call_target="tpu_custom_call" | custom-call | flops 5000000000 | bytes 15000000 | tf_op jit(solution)/shard_map/step/pallas_call | solution.py:582
  122.5 1.9 %collective-permute-start.49 = (f32[256,128]{1,0:T(8,128)S(1)}, f32[256,128]{1,0:T(8,128)S(1)}, u32[]{:S(2)}, u32[]{:S(2)}) collective-permute-start(f32[256,128]{1,0:T(8,128)S(1)} %get-tuple-element.88), channel_id=1, source_target_pairs={{0,24},{4,28},{8,16},{12,20},{16,8},{20,12},{24,0},{28,4},{1,25},{... | collective-permute-start | bytes 393224 | tf_op jit(solution)/shard_map/ppermute | solution.py:474
  125.6 1.9 %collective-permute-start.23 = (f32[256,128]{1,0:T(8,128)S(1)}, f32[256,128]{1,0:T(8,128)S(1)}, u32[]{:S(2)}, u32[]{:S(2)}) collective-permute-start(f32[256,128]{1,0:T(8,128)S(1)} %get-tuple-element.64), channel_id=1, source_target_pairs={{0,8},{4,12},{8,0},{12,4},{16,24},{20,28},{24,16},{28,20},{1,9},{5... | collective-permute-start | bytes 393224 | tf_op jit(solution)/shard_map/ppermute | solution.py:474
  127.5 2.3 %collective-permute-done.49.refs_14_ = f32[256,128]{1,0:T(8,128)S(1)} collective-permute-done((f32[256,128]{1,0:T(8,128)S(1)}, f32[256,128]{1,0:T(8,128)S(1)}, u32[]{:S(2)}, u32[]{:S(2)}) %collective-permute-start.49) | collective-permute-done | bytes 131104 | tf_op jit(solution)/shard_map/ppermute | solution.py:474
  132.6 2.7 %collective-permute-start.27 = (f32[256,128]{1,0:T(8,128)S(1)}, f32[256,128]{1,0:T(8,128)S(1)}, u32[]{:S(2)}, u32[]{:S(2)}) collective-permute-start(f32[256,128]{1,0:T(8,128)S(1)} %get-tuple-element.68), channel_id=1, source_target_pairs={{0,24},{4,28},{8,16},{12,20},{16,8},{20,12},{24,0},{28,4},{1,25},{... | collective-permute-start | bytes 393224 | tf_op jit(solution)/shard_map/ppermute | solution.py:474
  137.9 4.6 %collective-permute-done.27.refs_6_ = f32[256,128]{1,0:T(8,128)S(1)} collective-permute-done((f32[256,128]{1,0:T(8,128)S(1)}, f32[256,128]{1,0:T(8,128)S(1)}, u32[]{:S(2)}, u32[]{:S(2)}) %collective-permute-start.27) | collective-permute-done | bytes 131104 | tf_op jit(solution)/shard_map/ppermute | solution.py:474
  144.4 6.1 %gather.1 = (f32[4096,128]{1,0:T(8,128)}, f32[64,64]{1,0:T(8,128)}) custom-call(s32[2]{0:T(128)} %pad_add_fusion.me_ref, f32[256,128]{1,0:T(8,128)} %copy-done.8, f32[256,128]{1,0:T(8,128)} %copy-done.26, f32[256,128]{1,0:T(8,128)} %copy-done.29, f32[256,128]{1,0:T(8,128)} %copy-done.31, f32[256,128]{1,0:T(8,128)} %copy-done.33, f32[256,128]{1,0:T(8,128)} %copy-done.35, ...), custom_call_target="tpu_custom_call" | custom-call | flops 5000000000 | bytes 15000000 | tf_op jit(solution)/shard_map/gather/pallas_call | solution.py:597
  155.0 2.0 %collective-permute-start.54 = (f32[64,64]{1,0:T(8,128)S(1)}, f32[64,64]{1,0:T(8,128)S(1)}, u32[]{:S(2)}, u32[]{:S(2)}) collective-permute-start(f32[64,64]{1,0:T(8,128)S(1)} %fusion), channel_id=1, source_target_pairs={{0,24},{4,28},{8,16},{12,20},{16,8},{20,12},{24,0},{28,4},{1,25},{... | collective-permute-start | bytes 49160 | tf_op jit(solution)/shard_map/ppermute | solution.py:474
  161.9 2.5 %collective-permute-start.57 = (f32[16,64]{1,0:T(8,128)S(1)}, f32[16,64]{1,0:T(8,128)S(1)}, u32[]{:S(2)}, u32[]{:S(2)}) collective-permute-start(f32[16,64]{1,0:T(8,128)S(1)} %get-tuple-element.109), channel_id=1, source_target_pairs={{0,3},{1,2},{2,1},{3,0},{4,7},{5,6},{6,5},{7,4},{8,11},{9,10},{10,... | collective-permute-start | bytes 12296 | tf_op jit(solution)/shard_map/ppermute | solution.py:477
  165.1 2.2 %collective-permute-done.57 = f32[16,64]{1,0:T(8,128)S(1)} collective-permute-done((f32[16,64]{1,0:T(8,128)S(1)}, f32[16,64]{1,0:T(8,128)S(1)}, u32[]{:S(2)}, u32[]{:S(2)}) %collective-permute-start.57) | collective-permute-done | bytes 4128 | tf_op jit(solution)/shard_map/ppermute | solution.py:477
  (194 shorter events, 54.0 us)
Async XLA Ops:
  14.0 9.4 %collective-permute-start.29 = (f32[256,128]{1,0:T(8,128)}, f32[256,128]{1,0:T(8,128)S(1)}, u32[]{:S(2)}, u32[]{:S(2)}) collective-permute-start(f32[256,128]{1,0:T(8,128)} %get-tuple-element.98), channel_id=1, source_target_pairs={{0,4},{4,0},{8,12},{12,8},{16,20},{20,16},{24,28},{28,24},{1,5},{5... | collective-permute-start | bytes 393224 | tf_op jit(solution)/shard_map/ppermute | solution.py:474
  14.2 11.2 %collective-permute-start.30 = (f32[256,128]{1,0:T(8,128)}, f32[256,128]{1,0:T(8,128)S(1)}, u32[]{:S(2)}, u32[]{:S(2)}) collective-permute-start(f32[256,128]{1,0:T(8,128)} %get-tuple-element.97), channel_id=1, source_target_pairs={{0,8},{4,12},{8,0},{12,4},{16,24},{20,28},{24,16},{28,20},{1,9},{5... | collective-permute-start | bytes 393224 | tf_op jit(solution)/shard_map/ppermute | solution.py:474
  14.7 11.3 %collective-permute-start.31 = (f32[256,128]{1,0:T(8,128)}, f32[256,128]{1,0:T(8,128)S(1)}, u32[]{:S(2)}, u32[]{:S(2)}) collective-permute-start(f32[256,128]{1,0:T(8,128)} %get-tuple-element.96), channel_id=1, source_target_pairs={{0,12},{4,8},{8,4},{12,0},{16,28},{20,24},{24,20},{28,16},{1,13},{... | collective-permute-start | bytes 393224 | tf_op jit(solution)/shard_map/ppermute | solution.py:474
  15.9 11.1 %collective-permute-start.32 = (f32[256,128]{1,0:T(8,128)S(1)}, f32[256,128]{1,0:T(8,128)S(1)}, u32[]{:S(2)}, u32[]{:S(2)}) collective-permute-start(f32[256,128]{1,0:T(8,128)S(1)} %get-tuple-element.95), channel_id=1, source_target_pairs={{0,16},{4,20},{8,24},{12,28},{16,0},{20,4},{24,8},{28,12},{1,17},{... | collective-permute-start | bytes 393224 | tf_op jit(solution)/shard_map/ppermute | solution.py:474
  22.6 9.9 %collective-permute-start.33 = (f32[256,128]{1,0:T(8,128)S(1)}, f32[256,128]{1,0:T(8,128)S(1)}, u32[]{:S(2)}, u32[]{:S(2)}) collective-permute-start(f32[256,128]{1,0:T(8,128)S(1)} %get-tuple-element.94), channel_id=1, source_target_pairs={{0,20},{4,16},{8,28},{12,24},{16,4},{20,0},{24,12},{28,8},{1,21},{... | collective-permute-start | bytes 393224 | tf_op jit(solution)/shard_map/ppermute | solution.py:474
  23.4 11.1 %collective-permute-start.34 = (f32[256,128]{1,0:T(8,128)S(1)}, f32[256,128]{1,0:T(8,128)S(1)}, u32[]{:S(2)}, u32[]{:S(2)}) collective-permute-start(f32[256,128]{1,0:T(8,128)S(1)} %get-tuple-element.93), channel_id=1, source_target_pairs={{0,24},{4,28},{8,16},{12,20},{16,8},{20,12},{24,0},{28,4},{1,25},{... | collective-permute-start | bytes 393224 | tf_op jit(solution)/shard_map/ppermute | solution.py:474
  25.4 9.8 %collective-permute-start.35 = (f32[256,128]{1,0:T(8,128)S(1)}, f32[256,128]{1,0:T(8,128)S(1)}, u32[]{:S(2)}, u32[]{:S(2)}) collective-permute-start(f32[256,128]{1,0:T(8,128)S(1)} %get-tuple-element.92), channel_id=1, source_target_pairs={{0,28},{4,24},{8,20},{12,16},{16,12},{20,8},{24,4},{28,0},{1,29},{... | collective-permute-start | bytes 393224 | tf_op jit(solution)/shard_map/ppermute | solution.py:474
  26.1 11.0 %collective-permute-start.10 = (f32[256,128]{1,0:T(8,128)S(1)}, f32[256,128]{1,0:T(8,128)S(1)}, u32[]{:S(2)}, u32[]{:S(2)}) collective-permute-start(f32[256,128]{1,0:T(8,128)S(1)} %get-tuple-element.103), channel_id=1, source_target_pairs={{0,16},{4,20},{8,24},{12,28},{16,0},{20,4},{24,8},{28,12},{1,17},{... | collective-permute-start | bytes 393224 | tf_op jit(solution)/shard_map/ppermute | solution.py:474
  27.0 12.3 %collective-permute-start.11 = (f32[256,128]{1,0:T(8,128)S(1)}, f32[256,128]{1,0:T(8,128)S(1)}, u32[]{:S(2)}, u32[]{:S(2)}) collective-permute-start(f32[256,128]{1,0:T(8,128)S(1)} %get-tuple-element.102), channel_id=1, source_target_pairs={{0,20},{4,16},{8,28},{12,24},{16,4},{20,0},{24,12},{28,8},{1,21},{... | collective-permute-start | bytes 393224 | tf_op jit(solution)/shard_map/ppermute | solution.py:474
  32.5 12.5 %collective-permute-start.12 = (f32[256,128]{1,0:T(8,128)S(1)}, f32[256,128]{1,0:T(8,128)S(1)}, u32[]{:S(2)}, u32[]{:S(2)}) collective-permute-start(f32[256,128]{1,0:T(8,128)S(1)} %get-tuple-element.101), channel_id=1, source_target_pairs={{0,24},{4,28},{8,16},{12,20},{16,8},{20,12},{24,0},{28,4},{1,25},{... | collective-permute-start | bytes 393224 | tf_op jit(solution)/shard_map/ppermute | solution.py:474
  34.5 12.2 %collective-permute-start.13 = (f32[256,128]{1,0:T(8,128)S(1)}, f32[256,128]{1,0:T(8,128)S(1)}, u32[]{:S(2)}, u32[]{:S(2)}) collective-permute-start(f32[256,128]{1,0:T(8,128)S(1)} %get-tuple-element.100), channel_id=1, source_target_pairs={{0,28},{4,24},{8,20},{12,16},{16,12},{20,8},{24,4},{28,0},{1,29},{... | collective-permute-start | bytes 393224 | tf_op jit(solution)/shard_map/ppermute | solution.py:474
  35.2 14.4 %collective-permute-start.7 = (f32[256,128]{1,0:T(8,128)S(1)}, f32[256,128]{1,0:T(8,128)S(1)}, u32[]{:S(2)}, u32[]{:S(2)}) collective-permute-start(f32[256,128]{1,0:T(8,128)S(1)} %get-tuple-element.106), channel_id=1, source_target_pairs={{0,4},{4,0},{8,12},{12,8},{16,20},{20,16},{24,28},{28,24},{1,5},{5... | collective-permute-start | bytes 393224 | tf_op jit(solution)/shard_map/ppermute | solution.py:474
  37.1 12.5 %collective-permute-start.8 = (f32[256,128]{1,0:T(8,128)S(1)}, f32[256,128]{1,0:T(8,128)S(1)}, u32[]{:S(2)}, u32[]{:S(2)}) collective-permute-start(f32[256,128]{1,0:T(8,128)S(1)} %get-tuple-element.105), channel_id=1, source_target_pairs={{0,8},{4,12},{8,0},{12,4},{16,24},{20,28},{24,16},{28,20},{1,9},{5... | collective-permute-start | bytes 393224 | tf_op jit(solution)/shard_map/ppermute | solution.py:474
  39.3 10.3 %collective-permute-start.9 = (f32[256,128]{1,0:T(8,128)S(1)}, f32[256,128]{1,0:T(8,128)S(1)}, u32[]{:S(2)}, u32[]{:S(2)}) collective-permute-start(f32[256,128]{1,0:T(8,128)S(1)} %get-tuple-element.104), channel_id=1, source_target_pairs={{0,12},{4,8},{8,4},{12,0},{16,28},{20,24},{24,20},{28,16},{1,13},{... | collective-permute-start | bytes 393224 | tf_op jit(solution)/shard_map/ppermute | solution.py:474
  45.1 13.3 %collective-permute-start.36 = (f32[16,8,128]{2,1,0:T(8,128)}, f32[16,8,128]{2,1,0:T(8,128)S(1)}, u32[]{:S(2)}, u32[]{:S(2)}) collective-permute-start(f32[16,8,128]{2,1,0:T(8,128)} %get-tuple-element.71), channel_id=1, source_target_pairs={{0,1},{1,0},{2,3},{3,2},{4,5},{5,4},{6,7},{7,6},{8,9},{9,8},{10,11... | collective-permute-start | bytes 196616 | tf_op jit(solution)/shard_map/ppermute | solution.py:565
  46.7 11.7 %collective-permute-start.37 = (f32[16,8,128]{2,1,0:T(8,128)}, f32[16,8,128]{2,1,0:T(8,128)S(1)}, u32[]{:S(2)}, u32[]{:S(2)}) collective-permute-start(f32[16,8,128]{2,1,0:T(8,128)} %get-tuple-element.72), channel_id=1, source_target_pairs={{0,3},{1,2},{2,1},{3,0},{4,7},{5,6},{6,5},{7,4},{8,11},{9,10},{10,... | collective-permute-start | bytes 196616 | tf_op jit(solution)/shard_map/ppermute | solution.py:566
  55.0 10.3 %collective-permute-start.14 = (f32[16,8,128]{2,1,0:T(8,128)}, f32[16,8,128]{2,1,0:T(8,128)S(1)}, u32[]{:S(2)}, u32[]{:S(2)}) collective-permute-start(f32[16,8,128]{2,1,0:T(8,128)} %get-tuple-element.51), channel_id=1, source_target_pairs={{0,1},{1,0},{2,3},{3,2},{4,5},{5,4},{6,7},{7,6},{8,9},{9,8},{10,11... | collective-permute-start | bytes 196616 | tf_op jit(solution)/shard_map/ppermute | solution.py:565
  63.5 10.1 %collective-permute-start.38 = (f32[16,8,128]{2,1,0:T(8,128)S(1)}, f32[16,8,128]{2,1,0:T(8,128)S(1)}, u32[]{:S(2)}, u32[]{:S(2)}) collective-permute-start(f32[16,8,128]{2,1,0:T(8,128)S(1)} %get-tuple-element.74), channel_id=1, source_target_pairs={{0,1},{1,0},{2,3},{3,2},{4,5},{5,4},{6,7},{7,6},{8,9},{9,8},{10,11... | collective-permute-start | bytes 196616 | tf_op jit(solution)/shard_map/ppermute | solution.py:565
  70.3 10.2 %collective-permute-start.16 = (f32[16,8,128]{2,1,0:T(8,128)S(1)}, f32[16,8,128]{2,1,0:T(8,128)S(1)}, u32[]{:S(2)}, u32[]{:S(2)}) collective-permute-start(f32[16,8,128]{2,1,0:T(8,128)S(1)} %get-tuple-element.54), channel_id=1, source_target_pairs={{0,1},{1,0},{2,3},{3,2},{4,5},{5,4},{6,7},{7,6},{8,9},{9,8},{10,11... | collective-permute-start | bytes 196616 | tf_op jit(solution)/shard_map/ppermute | solution.py:565
  78.8 10.2 %collective-permute-start.40 = (f32[16,8,128]{2,1,0:T(8,128)S(1)}, f32[16,8,128]{2,1,0:T(8,128)S(1)}, u32[]{:S(2)}, u32[]{:S(2)}) collective-permute-start(f32[16,8,128]{2,1,0:T(8,128)S(1)} %get-tuple-element.77), channel_id=1, source_target_pairs={{0,1},{1,0},{2,3},{3,2},{4,5},{5,4},{6,7},{7,6},{8,9},{9,8},{10,11... | collective-permute-start | bytes 196616 | tf_op jit(solution)/shard_map/ppermute | solution.py:565
  85.6 10.2 %collective-permute-start.18 = (f32[16,8,128]{2,1,0:T(8,128)S(1)}, f32[16,8,128]{2,1,0:T(8,128)S(1)}, u32[]{:S(2)}, u32[]{:S(2)}) collective-permute-start(f32[16,8,128]{2,1,0:T(8,128)S(1)} %get-tuple-element.57), channel_id=1, source_target_pairs={{0,1},{1,0},{2,3},{3,2},{4,5},{5,4},{6,7},{7,6},{8,9},{9,8},{10,11... | collective-permute-start | bytes 196616 | tf_op jit(solution)/shard_map/ppermute | solution.py:565
  94.1 10.2 %collective-permute-start.42 = (f32[16,8,128]{2,1,0:T(8,128)S(1)}, f32[16,8,128]{2,1,0:T(8,128)S(1)}, u32[]{:S(2)}, u32[]{:S(2)}) collective-permute-start(f32[16,8,128]{2,1,0:T(8,128)S(1)} %get-tuple-element.80), channel_id=1, source_target_pairs={{0,1},{1,0},{2,3},{3,2},{4,5},{5,4},{6,7},{7,6},{8,9},{9,8},{10,11... | collective-permute-start | bytes 196616 | tf_op jit(solution)/shard_map/ppermute | solution.py:565
  100.9 12.5 %collective-permute-start.20 = (f32[16,8,128]{2,1,0:T(8,128)S(1)}, f32[16,8,128]{2,1,0:T(8,128)S(1)}, u32[]{:S(2)}, u32[]{:S(2)}) collective-permute-start(f32[16,8,128]{2,1,0:T(8,128)S(1)} %get-tuple-element.60), channel_id=1, source_target_pairs={{0,1},{1,0},{2,3},{3,2},{4,5},{5,4},{6,7},{7,6},{8,9},{9,8},{10,11... | collective-permute-start | bytes 196616 | tf_op jit(solution)/shard_map/ppermute | solution.py:565
  101.8 12.5 %collective-permute-start.21 = (f32[16,8,128]{2,1,0:T(8,128)S(1)}, f32[16,8,128]{2,1,0:T(8,128)S(1)}, u32[]{:S(2)}, u32[]{:S(2)}) collective-permute-start(f32[16,8,128]{2,1,0:T(8,128)S(1)} %get-tuple-element.61), channel_id=1, source_target_pairs={{0,3},{1,2},{2,1},{3,0},{4,7},{5,6},{6,5},{7,4},{8,11},{9,10},{10,... | collective-permute-start | bytes 196616 | tf_op jit(solution)/shard_map/ppermute | solution.py:566
  111.3 11.2 %collective-permute-start.44 = (f32[256,128]{1,0:T(8,128)S(1)}, f32[256,128]{1,0:T(8,128)S(1)}, u32[]{:S(2)}, u32[]{:S(2)}) collective-permute-start(f32[256,128]{1,0:T(8,128)S(1)} %get-tuple-element.83), channel_id=1, source_target_pairs={{0,4},{4,0},{8,12},{12,8},{16,20},{20,16},{24,28},{28,24},{1,5},{5... | collective-permute-start | bytes 393224 | tf_op jit(solution)/shard_map/ppermute | solution.py:474
  111.4 13.0 %collective-permute-start.45 = (f32[256,128]{1,0:T(8,128)S(1)}, f32[256,128]{1,0:T(8,128)S(1)}, u32[]{:S(2)}, u32[]{:S(2)}) collective-permute-start(f32[256,128]{1,0:T(8,128)S(1)} %get-tuple-element.84), channel_id=1, source_target_pairs={{0,8},{4,12},{8,0},{12,4},{16,24},{20,28},{24,16},{28,20},{1,9},{5... | collective-permute-start | bytes 393224 | tf_op jit(solution)/shard_map/ppermute | solution.py:474
  113.3 12.0 %collective-permute-start.46 = (f32[256,128]{1,0:T(8,128)S(1)}, f32[256,128]{1,0:T(8,128)S(1)}, u32[]{:S(2)}, u32[]{:S(2)}) collective-permute-start(f32[256,128]{1,0:T(8,128)S(1)} %get-tuple-element.85), channel_id=1, source_target_pairs={{0,12},{4,8},{8,4},{12,0},{16,28},{20,24},{24,20},{28,16},{1,13},{... | collective-permute-start | bytes 393224 | tf_op jit(solution)/shard_map/ppermute | solution.py:474
  113.4 12.1 %collective-permute-start.47 = (f32[256,128]{1,0:T(8,128)S(1)}, f32[256,128]{1,0:T(8,128)S(1)}, u32[]{:S(2)}, u32[]{:S(2)}) collective-permute-start(f32[256,128]{1,0:T(8,128)S(1)} %get-tuple-element.86), channel_id=1, source_target_pairs={{0,16},{4,20},{8,24},{12,28},{16,0},{20,4},{24,8},{28,12},{1,17},{... | collective-permute-start | bytes 393224 | tf_op jit(solution)/shard_map/ppermute | solution.py:474
  114.3 13.2 %collective-permute-start.48 = (f32[256,128]{1,0:T(8,128)S(1)}, f32[256,128]{1,0:T(8,128)S(1)}, u32[]{:S(2)}, u32[]{:S(2)}) collective-permute-start(f32[256,128]{1,0:T(8,128)S(1)} %get-tuple-element.87), channel_id=1, source_target_pairs={{0,20},{4,16},{8,28},{12,24},{16,4},{20,0},{24,12},{28,8},{1,21},{... | collective-permute-start | bytes 393224 | tf_op jit(solution)/shard_map/ppermute | solution.py:474
  125.6 9.8 %collective-permute-start.23 = (f32[256,128]{1,0:T(8,128)S(1)}, f32[256,128]{1,0:T(8,128)S(1)}, u32[]{:S(2)}, u32[]{:S(2)}) collective-permute-start(f32[256,128]{1,0:T(8,128)S(1)} %get-tuple-element.64), channel_id=1, source_target_pairs={{0,8},{4,12},{8,0},{12,4},{16,24},{20,28},{24,16},{28,20},{1,9},{5... | collective-permute-start | bytes 393224 | tf_op jit(solution)/shard_map/ppermute | solution.py:474
  127.4 10.3 %collective-permute-start.24 = (f32[256,128]{1,0:T(8,128)S(1)}, f32[256,128]{1,0:T(8,128)S(1)}, u32[]{:S(2)}, u32[]{:S(2)}) collective-permute-start(f32[256,128]{1,0:T(8,128)S(1)} %get-tuple-element.65), channel_id=1, source_target_pairs={{0,12},{4,8},{8,4},{12,0},{16,28},{20,24},{24,20},{28,16},{1,13},{... | collective-permute-start | bytes 393224 | tf_op jit(solution)/shard_map/ppermute | solution.py:474
  132.6 9.9 %collective-permute-start.27 = (f32[256,128]{1,0:T(8,128)S(1)}, f32[256,128]{1,0:T(8,128)S(1)}, u32[]{:S(2)}, u32[]{:S(2)}) collective-permute-start(f32[256,128]{1,0:T(8,128)S(1)} %get-tuple-element.68), channel_id=1, source_target_pairs={{0,24},{4,28},{8,16},{12,20},{16,8},{20,12},{24,0},{28,4},{1,25},{... | collective-permute-start | bytes 393224 | tf_op jit(solution)/shard_map/ppermute | solution.py:474
  (67 other events, 493.0 us)

commit v3 on v2

v3 whole, which is shorter than its diff:
```python
import functools
import math

import jax
import jax.numpy as jnp
import ml_dtypes
import numpy as np
from jax import lax
from jax.experimental import pallas as pl
from jax.experimental.pallas import tpu as pltpu
from jax.sharding import PartitionSpec as P

DEGREE = 4
CHUNKS = 2

STENCIL = (
    -5369.0 / 1800.0,
    12.0 / 7.0,
    -15.0 / 56.0,
    10.0 / 189.0,
    -1.0 / 112.0,
    2.0 / 1925.0,
    -1.0 / 16632.0,
)
SPACING = 0.224
CENTER = 210.5
HALF = 209.5
REACH = 6
TILE = 64
LANES = 128
SUBS = 8
KINETIC = -0.5 / (SPACING * SPACING) / HALF
TAPS = tuple(KINETIC * c for c in STENCIL)
DIAGONAL = 3.0 * TAPS[0] - CENTER / HALF

F32 = jnp.float32
BF16 = jnp.bfloat16
VMEM = pl.BlockSpec(memory_space=pltpu.VMEM)
SMEM = pl.BlockSpec(memory_space=pltpu.SMEM)
ANY = pl.BlockSpec(memory_space=pl.ANY)
HBM = pl.BlockSpec(memory_space=pltpu.HBM)


PARAMS = pltpu.CompilerParams(vmem_limit_bytes=24 << 20)


def split_halves(matrix):
    high = matrix.astype(ml_dtypes.bfloat16)
    low = (matrix - high.astype(np.float64)).astype(ml_dtypes.bfloat16)
    wide = np.concatenate([high, low], axis=1)
    return np.concatenate([wide, wide], axis=0)


def line_weights():
    own = np.zeros((LANES, LANES))
    halo = np.zeros((8, LANES, LANES))
    for k in range(1, REACH + 1):
        for z in range(LANES):
            for cell in (z + k, z - k):
                if 0 <= cell < LANES:
                    own[cell, z] = TAPS[k]
                else:
                    lane = 8 + cell - LANES if cell >= LANES else 8 + cell
                    for slot in range(8):
                        halo[slot, 16 * slot + lane, z] = TAPS[k]
    return split_halves(own), np.stack([split_halves(slot) for slot in halo])


def halves(value):
    high = value.astype(BF16)
    low = (value - high.astype(F32)).astype(BF16)
    return high, low


def parts_kernel(count, fold, index_ref, proj_ref, root_ref, pot_ref, meta_ref, out_ref):
    out_ref[0:64, :] = pot_ref[...]
    point = lax.broadcasted_iota(jnp.int32, (TILE, TILE), 0)
    width = TILE // fold
    sorted_rows = []
    for atom in range(count):
        order = index_ref[atom : atom + 1, :]
        if fold == 2:
            order = ((order >> 4) & 1) * width + (order >> 5) * 16 + (order & 15)
        hot = (point == order).astype(F32)
        sorted_rows.append(
            lax.dot_general(
                proj_ref[atom],
                hot,
                (((1,), (1,)), ((), ())),
                precision=lax.Precision.HIGHEST,
                preferred_element_type=F32,
            )
            * root_ref[:, atom : atom + 1]
        )
    row = 64
    for first in range(0, count, 2 * fold):
        for f in range(fold):
            out_ref[row : row + 8, :] = jnp.concatenate(
                [sorted_rows[first + q][:, f * width : (f + 1) * width] for q in range(2 * fold)],
                axis=1,
            )
            row += 8
    out_ref[row : row + 8, :] = meta_ref[...]


def swapped(rows):
    if len(rows) == 1:
        return [rows[0][y : y + 1] for y in range(8)]
    return jnp.swapaxes(jnp.stack(rows, axis=0), 0, 1)


def column_sources(me, crossed, beside, size, core):
    pairs = []
    for n, block in enumerate(crossed):
        pairs.append((me ^ (2 * n), block.at[pl.ds(pl.multiple_of(core * size, 8), size)]))
        pairs.append((me ^ (2 * n) ^ 1, beside.at[pl.ds(n * size, size)]))
    return pairs


def setup_kernel(gx, gy, nb, count, fold, me_ref, after_ref, *refs):
    half = gx * gy // 2
    diag_ref, roots_ref, meta_ref, raw, sem = refs[half:]
    rows = 4 * count
    sources = []
    for n in range(half):
        for other in range(2):
            at = 2 * nb * 64 + other * (72 + rows)
            sources.append((me_ref[0] ^ (2 * n + other), refs[n].at[pl.ds(at, 72 + rows)]))
    copies = [
        pltpu.make_async_copy(
            source.at[pl.ds(64 + rows, 8)],
            raw.at[pl.ds(pl.multiple_of(slot * 8, 8), 8)],
            sem.at[0],
        )
        for slot, source in sources
    ]
    for copy in copies:
        copy.start()
    sub = lax.broadcasted_iota(jnp.int32, (SUBS, LANES), 0)
    per_slot = count // (2 * fold)
    for slot, source in sources:
        i, j = slot // gy, slot % gy
        for x in range(8):
            value = source[x * 8 : x * 8 + 8, :] * (1.0 / HALF) + DIAGONAL
            for y in range(8):
                at = ((j * 8 + y) * 8 + x) * SUBS + i * nb
                diag_ref[pl.ds(at, nb)] = jnp.broadcast_to(value[y : y + 1], (nb, LANES))
        for m in range(per_slot):
            for k in range(8):
                parts = []
                for f in range(fold):
                    at = 64 + (m * fold + f) * 8 + k
                    parts.append(jnp.broadcast_to(source[at : at + 1, :], (SUBS, LANES)))
                value = parts[0] if fold == 1 else jnp.where(sub < SUBS // 2, parts[0], parts[1])
                roots_ref[(slot * per_slot + m) * 8 + k] = value
    for copy in copies:
        copy.wait()

    def corners(slot, carry):
        for atom in range(count):
            n = slot * count + atom
            first = (raw[slot * 8, atom].astype(jnp.int32) + (slot % gy) * 64) * SUBS
            meta_ref[2 * n] = first + (slot // gy * nb if fold == 2 else 0)
            meta_ref[2 * n + 1] = raw[slot * 8, count + atom].astype(jnp.int32)
        return carry

    lax.fori_loop(0, gx * gy, corners, 0)


def pack_edges(values, lane):
    wide = []
    for first in (0, 8):
        tile = None
        for slot in range(8):
            moved = pltpu.roll(values[first + slot], (16 * slot + 2 + REACH) % LANES, 1)
            tile = moved if tile is None else jnp.where((lane >> 4) == slot, moved, tile)
        wide.append(tile)
    lower = (lane & 15) < 8
    low = jnp.where(lower, pltpu.roll(wide[0], LANES - 8, 1), wide[1])
    high = jnp.where(lower, wide[0], pltpu.roll(wide[1], 8, 1))
    return low, high


def send_edges(even, low, high):
    return jnp.where(even, high, low), jnp.where(even, low, high)


def pack_kernel(group, size, chunk, tables, me_ref, field, passed, *refs):
    blocks, sem = refs[2 if tables else 1 : -1], refs[-1]
    copies = []
    for n, block in enumerate(blocks):
        chip = me_ref[0] // 2 ^ n
        row = (chunk * group + chip * 2 + me_ref[0] % 2) * size
        copies.append(
            pltpu.make_async_copy(
                field.at[pl.ds(pl.multiple_of(row, 64), size)],
                block.at[pl.ds(0, size)],
                sem.at[0],
            )
        )
    for copy in copies:
        copy.start()
    for n, block in enumerate(blocks):
        chip = me_ref[0] // 2 ^ n
        block[pl.ds(size, size)] = passed[pl.ds(pl.multiple_of(chip * size, 64), size)]
        if tables:
            block[pl.ds(2 * size, tables)] = refs[0][...]
            block[pl.ds(2 * size + tables, tables)] = refs[1][...]
    for copy in copies:
        copy.wait()


def unpack_kernel(gx, gy, nb, me_ref, after_ref, *refs):
    half = gx * gy // 2
    z_ref, one_ref, two_ref = refs[half:]
    size = nb * 64
    for n in range(half):
        for other in range(2):
            slot = me_ref[0] ^ (2 * n + other)
            i, j = slot // gy, slot % gy
            for x in range(8):
                first = other * size + x * 8
                turned = swapped([refs[n][first + b * 64 : first + b * 64 + 8] for b in range(nb)])
                for y in range(8):
                    z_ref[pl.ds(((j * 8 + y) * 8 + x) * SUBS + i * nb, nb)] = turned[y]
    lane = lax.broadcasted_iota(jnp.int32, (SUBS, LANES), 1)
    even = me_ref[1] == 0

    def lines(pair, carry):
        tiles = z_ref[pl.ds(pl.multiple_of(pair * LANES, LANES), LANES)]
        values = [tiles[SUBS * q : SUBS * (q + 1)] for q in range(16)]
        low, high = pack_edges(values, lane)
        one_ref[pair], two_ref[pair] = send_edges(even, low, high)
        return carry

    lax.fori_loop(0, gy * 4, lines, 0, unroll=4)


def tile_rows(row):
    return pl.ds(pl.multiple_of(row * SUBS, SUBS), SUBS)


def inner_kernel(gx, gy, nb, count, fold, first, after_ref, meta_ref, *refs):
    if first:
        z_ref, diag_ref, roots_ref, w_ref, sum_ref = refs[:5]
    else:
        z_ref, prev_ref, diag_ref, roots_ref, w_ref, sum_ref = refs[:6]
    out_ref, atoms_ref, acc, tile_ref, spread_ref = refs[-5:]
    group = gx * gy
    ny = gy * 8
    width = TILE // fold
    per_tile = 2 * fold
    per_slot = count // per_tile
    lane = lax.broadcasted_iota(jnp.int32, (SUBS, LANES), 1)
    sub = lax.broadcasted_iota(jnp.int32, (SUBS, LANES), 0)

    def tile_row(t):
        return ((t % 4) * 8 + (t // 4) * fold) * SUBS

    def gather(slot):
        for m in range(per_slot):
            tile = jnp.zeros((SUBS, LANES), F32)
            for q in range(per_tile):
                n = slot * count + per_tile * m + q
                start = meta_ref[2 * n]
                back = LANES - meta_ref[2 * n + 1]
                for t in range(16 // fold):
                    value = z_ref[pl.ds(start + tile_row(t), SUBS)]
                    if fold == 2:
                        beyond = z_ref[pl.ds(start + (tile_row(t) + nb), SUBS)]
                        value = jnp.where(sub < nb, value, beyond)
                    value = pltpu.roll(value, back + (4 * t + width * q), 1)
                    tile = jnp.where((lane >> 2) == t + q * (width // 4), value, tile)
            tile_ref[slot * per_slot + m] = tile

    def scatter(slot, i):
        for m in range(per_slot):
            spread = spread_ref[slot * per_slot + m]
            for q in range(per_tile):
                n = slot * count + per_tile * m + q
                start = meta_ref[2 * n]
                z0 = meta_ref[2 * n + 1]
                inside = (lane >= z0) & (lane < z0 + 4)
                if fold == 1:
                    masks = [inside & (sub // nb == i)]
                else:
                    masks = [inside & (sub < nb), inside & (sub >= nb)]
                sums = []
                for t in range(16 // fold):
                    value = pltpu.roll(spread, z0 + (LANES - 4 * t - width * q), 1)
                    for f, mask in enumerate(masks):
                        here = pl.ds(start + (tile_row(t) + f * nb), SUBS)
                        sums.append((here, atoms_ref[here] + jnp.where(mask, value, 0.0)))
                for here, value in sums:
                    atoms_ref[here] = value

    def second_dim(x, carry):
        for c in range(group // 8):
            gather(x * (group // 8) + c)
        block = pl.ds(pl.multiple_of(x * 32 * SUBS, 32 * SUBS), 32 * SUBS)
        operand = jnp.concatenate(halves(z_ref[block]), axis=1)
        product = jnp.dot(operand, w_ref[...], preferred_element_type=F32)
        out_ref[block] = product[:, :LANES] + product[:, LANES:]
        values = [z_ref[tile_rows(y * 8 + x)] for y in range(ny)]
        for y in range(ny):
            total = None
            for k in range(1, REACH + 1):
                term = TAPS[k] * (values[(y + k) % ny] + values[(y - k) % ny])
                total = term if total is None else total + term
            acc[tile_rows(y * 8 + x)] = total
            atoms_ref[tile_rows(y * 8 + x)] = jnp.zeros((SUBS, LANES), F32)
        return carry

    lax.fori_loop(0, 8, second_dim, 0, unroll=2)

    def contract(eight, carry):
        products = []
        for m in range(8):
            tile = tile_ref[eight * 8 + m]
            for k in range(8):
                products.append(tile * roots_ref[(eight * 8 + m) * 8 + k])
        sums = jnp.dot(
            jnp.concatenate(halves(jnp.concatenate(products, axis=0)), axis=1),
            sum_ref[...],
            preferred_element_type=F32,
        )
        for m in range(8):
            spread = None
            for k in range(8):
                at = (m * 8 + k) * SUBS
                coeff = sums[at : at + SUBS]
                if fold == 2:
                    coeff = coeff + pltpu.roll(coeff, nb, 0)
                term = coeff * roots_ref[(eight * 8 + m) * 8 + k]
                spread = term if spread is None else spread + term
            spread_ref[eight * 8 + m] = spread if first else 2.0 * spread
        return carry

    lax.fori_loop(0, group * per_slot // 8, contract, 0, unroll=2)

    def rest(four):
        for q in range(4):
            values = [z_ref[tile_rows(four * 32 + 8 * q + x)] for x in range(8)]
            after = [pltpu.roll(value, SUBS - nb, 0) for value in values]
            before = after if gx == 2 else [pltpu.roll(value, nb, 0) for value in values]
            wide = before + values + after
            for x in range(8):
                here = tile_rows(four * 32 + 8 * q + x)
                total = acc[here] + out_ref[here]
                total = total + diag_ref[here] * values[x]
                for k in range(1, REACH + 1):
                    total = total + TAPS[k] * (wide[8 + x + k] + wide[8 + x - k])
                if not first:
                    total = 2.0 * total - prev_ref[here]
                out_ref[here] = total

    def block(j, carry):
        for half in range(2):
            for i in range(half * gx // 2, (half + 1) * gx // 2):
                scatter(i * gy + j, i)
            rest(2 * j + half)
        return carry

    lax.fori_loop(0, gy, block, 0)


def outer_kernel(gx, gy, nb, first, last, edge, me_ref, part_ref, atoms_ref, one_in, two_in, *refs):
    group = gx * gy
    w_ref, refs = refs[0], refs[1:]
    if last:
        blocks, acc = refs[: group // 2], refs[group // 2]
    else:
        acc, one_ref, two_ref = refs
    lane = lax.broadcasted_iota(jnp.int32, (SUBS, LANES), 1)
    even = me_ref[1] == 0
    lower = (lane & 15) < 8
    ny = gy * 8
    tiles = []
    for pair in range(ny // 2):
        one = one_in[edge + pair]
        two = two_in[edge + pair]
        below = jnp.where(even, two, one)
        above = jnp.where(even, one, two)
        tiles.append(jnp.where(lower, below, pltpu.roll(above, 8, 1)))
        tiles.append(jnp.where(lower, pltpu.roll(below, LANES - 8, 1), above))
    halo = jnp.concatenate(tiles, axis=0)
    operand = jnp.concatenate(halves(halo if first else 2.0 * halo), axis=1)
    for x in range(8):
        product = jnp.dot(operand, w_ref[x], preferred_element_type=F32)
        third = product[:, :LANES] + product[:, LANES:]
        for y in range(ny):
            here = pl.ds((y * 8 + x) * SUBS, SUBS)
            acc[here] = part_ref[here] + atoms_ref[here] + third[y * SUBS : (y + 1) * SUBS]
    if not last:

        def edges(pair, carry):
            rows = acc[pl.ds(pl.multiple_of(pair * LANES, LANES), LANES)]
            low, high = pack_edges([rows[SUBS * m : SUBS * (m + 1)] for m in range(16)], lane)
            one_ref[pair], two_ref[pair] = send_edges(even, low, high)
            return carry

        lax.fori_loop(0, ny // 2, edges, 0, unroll=4)
    if last:
        size = nb * 64
        for n in range(group // 2):
            for core in range(2):
                slot = (me_ref[0] // 2 ^ n) * 2 + core
                i, j = slot // gy, slot % gy
                for x in range(8):
                    rows = [
                        acc[pl.ds(((j * 8 + y) * 8 + x) * SUBS + i * nb, nb)] for y in range(8)
                    ]
                    if nb == 1:
                        turned = [jnp.concatenate(rows, axis=0)]
                    else:
                        turned = jnp.swapaxes(jnp.stack(rows, axis=0), 0, 1)
                    for b in range(nb):
                        at = core * size + b * 64 + x * 8
                        blocks[n][at : at + 8] = turned[b]


def turn(ref, first):
    return swapped(
        [ref[pl.ds(pl.multiple_of(first + 64 * s, SUBS), SUBS)] for s in range(SUBS)]
    )


def gather_kernel(group, nb, bands, scale, me_ref, *refs):
    half = group // 2
    out_ref, gram_ref, field, sem = refs[CHUNKS * (half + 1) :]
    size = nb * 64
    for chunk in range(CHUNKS):
        blocks = refs[chunk * (half + 1) : (chunk + 1) * (half + 1)]
        for slot, source in column_sources(
            me_ref[0], blocks[:half], blocks[half], size, me_ref[0] % 2
        ):
            row = (chunk * group + slot) * size
            field[pl.ds(pl.multiple_of(row, 64), size)] = source[...]
    store = pltpu.make_async_copy(field, out_ref, sem.at[0])
    store.start()
    gram_ref[...] = jnp.zeros_like(gram_ref)

    def cells(n, carry):
        total = None
        turned = [turn(field, g * SUBS * 64 + n * 8) for g in range(bands // SUBS)]
        for m in range(4):
            pieces = []
            for c in range(2):
                cell = m * 2 + c
                pieces.append(jnp.concatenate([group_[cell] for group_ in turned], axis=0))
            value = jnp.concatenate(pieces, axis=1)
            high, low = halves(value)
            both = jnp.concatenate([high, low], axis=0)
            product = lax.dot_general(
                both, both, (((1,), (1,)), ((), ())), preferred_element_type=F32
            )
            total = product if total is None else total + product
        gram_ref[...] += (
            total[:bands, :bands]
            + total[bands:, :bands]
            + total[:bands, bands:]
            + total[bands:, bands:]
        )
        return carry

    lax.fori_loop(0, 8, cells, 0)
    gram_ref[...] *= scale
    store.wait()


def shape(*dims, dtype=F32):
    return jax.ShapeDtypeStruct(dims, dtype)


def cost(microseconds):
    return pl.CostEstimate(
        flops=int(microseconds * 1e9), bytes_accessed=int(microseconds * 3e6), transcendentals=0
    )


def shards(panel, potential, atom_corner, proj_index, projectors, couplings):
    bands, size_x, size_y, size_z = panel.shape
    count, nproj = couplings.shape
    gx, gy, gz = lax.axis_size("gx"), lax.axis_size("gy"), lax.axis_size("gz")
    group = gx * gy
    nb = bands // (CHUNKS * group)
    fold = 2 if gx == 2 else 1
    column = ("gx", "gy")
    me = lax.axis_index("gx") * gy + lax.axis_index("gy")
    me_z = lax.axis_index("gz")
    me_arr = jnp.stack([me, me_z % 2])
    rows = gy * 64
    pairs = gy * 4

    def swap(block, d):
        return lax.ppermute(block, column, [(s, s ^ d) for s in range(group)])

    def swap_z(block, d):
        return lax.ppermute(block, "gz", [(s, s ^ d) for s in range(gz)])

    anchor = jnp.stack(
        [
            lax.axis_index("gx") * size_x,
            lax.axis_index("gy") * size_y,
            me_z * size_z,
        ]
    )
    local = atom_corner - anchor[None, :]
    meta = jnp.concatenate([local[:, 1] * 8 + local[:, 0], local[:, 2]]).astype(F32)
    meta = jnp.broadcast_to(jnp.pad(meta, (0, LANES - 2 * count))[None], (8, LANES))
    part_rows = 64 + 4 * count + 8
    size = nb * 64
    core = me % 2

    def cross(blocks):
        return [blocks[0]] + [swap(blocks[n], 2 * n) for n in range(1, group // 2)]

    def beside(crossed):
        halves_of = [lax.dynamic_slice_in_dim(b, (1 - core) * size, size, 0) for b in crossed]
        return swap(jnp.concatenate(halves_of, axis=0), 1)

    field = panel.reshape(bands * 64, LANES)
    parts = pl.pallas_call(
        functools.partial(parts_kernel, count, fold),
        out_shape=shape(part_rows, LANES),
        in_specs=[VMEM] * 5,
        out_specs=VMEM,
        compiler_params=PARAMS,
        cost_estimate=cost(1),
        name="parts",
    )(
        proj_index,
        projectors,
        jnp.sqrt(couplings * (1.0 / HALF)).T,
        potential.reshape(64, LANES),
        meta,
    )
    packed = []
    forward = []
    for chunk in range(CHUNKS):
        tables = part_rows if chunk == 0 else 0
        mine = lax.dynamic_slice_in_dim(field, chunk * group * size, group * size, 0)
        mine = mine.reshape(group // 2, 2, size, LANES)
        passed = lax.dynamic_slice_in_dim(mine, 1 - core, 1, 1).reshape(group // 2 * size, LANES)
        passed = swap(passed, 1)
        if chunk == 0:
            extra = [parts, swap(parts, 1)]
            field, passed = lax.optimization_barrier((field, passed))
        else:
            extra = packed[0][:1]
        packed.append(
            pl.pallas_call(
                functools.partial(pack_kernel, group, size, chunk, tables),
                out_shape=[shape(2 * (size + tables), LANES)] * (group // 2),
                in_specs=[SMEM, HBM, VMEM] + ([ANY] if chunk else [VMEM] * 2),
                out_specs=[VMEM] * (group // 2),
                scratch_shapes=[pltpu.SemaphoreType.DMA((1,))],
                compiler_params=PARAMS,
                cost_estimate=cost(1),
                name="pack",
            )(me_arr, field, passed, *extra)
        )
        forward.append(cross(packed[chunk]))

    tile_shape = shape(rows * SUBS, LANES)
    edge_shape = shape(pairs, SUBS, LANES)
    def unpack(chunk, after):
        tiles, one, two = pl.pallas_call(
            functools.partial(unpack_kernel, gx, gy, nb),
            out_shape=[tile_shape, edge_shape, edge_shape],
            in_specs=[SMEM, ANY] + [VMEM] * (group // 2),
            out_specs=[VMEM] * 3,
            compiler_params=PARAMS,
            cost_estimate=cost(2),
            name="unpack",
        )(me_arr, after, *forward[chunk])
        return None, tiles, one, two

    states = [unpack(0, packed[-1][0])]
    root_tiles = group * count * 8 // (2 * fold)
    diag, roots, places = pl.pallas_call(
        functools.partial(setup_kernel, gx, gy, nb, count, fold),
        out_shape=[
            shape(rows * SUBS, LANES),
            shape(root_tiles, SUBS, LANES),
            shape(2 * group * count, dtype=jnp.int32),
        ],
        in_specs=[SMEM, ANY] + [VMEM] * (group // 2),
        out_specs=[VMEM, VMEM, SMEM],
        scratch_shapes=[
            pltpu.SMEM((group * 8, LANES), F32),
            pltpu.SemaphoreType.DMA((1,)),
        ],
        compiler_params=PARAMS,
        cost_estimate=cost(2),
        name="setup",
    )(me_arr, states[0][2], *forward[0])
    for chunk in range(1, CHUNKS):
        states.append(unpack(chunk, roots))

    own_weights, halo_weights = (jnp.asarray(w) for w in line_weights())
    summing = np.kron(np.eye(2 * fold), np.ones((TILE // fold, TILE // fold)))
    summing = jnp.asarray(np.concatenate([summing, summing], axis=0).astype(ml_dtypes.bfloat16))
    pair_one = [(s, s ^ 1) for s in range(gz)]
    pair_two = [(s, (s + (1 if s % 2 else -1)) % gz) for s in range(gz)]

    results = [None] * CHUNKS
    for degree_step in range(DEGREE):
        first, last = degree_step == 0, degree_step == DEGREE - 1
        outs = None
        if not first:
            joint_one = jnp.concatenate([state[2] for state in states], axis=0)
            joint_two = jnp.concatenate([state[3] for state in states], axis=0)
            joint_one = lax.ppermute(joint_one, "gz", pair_one)
            joint_two = lax.ppermute(joint_two, "gz", pair_two)
        for chunk in range(CHUNKS):
            prev, tiles, one, two = states[chunk]
            edge = 0 if first else chunk * pairs
            if first:
                one = lax.ppermute(one, "gz", pair_one)
                two = lax.ppermute(two, "gz", pair_two)
            else:
                one, two = joint_one, joint_two
            after = roots if outs is None or not last else outs[0]
            operands = [after, places, tiles]
            if not first:
                operands.append(prev)
            operands += [diag, roots, own_weights, summing]
            part, atoms = pl.pallas_call(
                functools.partial(inner_kernel, gx, gy, nb, count, fold, first),
                out_shape=[tile_shape, tile_shape],
                in_specs=[ANY, SMEM] + [VMEM] * (len(operands) - 2),
                out_specs=[VMEM] * 2,
                scratch_shapes=[pltpu.VMEM((rows * SUBS, LANES), F32)]
                + [pltpu.VMEM((root_tiles // 8, SUBS, LANES), F32)] * 2,
                compiler_params=PARAMS,
                cost_estimate=cost(4),
                name="inner",
            )(*operands)
            outs = pl.pallas_call(
                functools.partial(outer_kernel, gx, gy, nb, first, last, edge),
                out_shape=[shape(2 * size, LANES)] * (group // 2)
                if last
                else [tile_shape, edge_shape, edge_shape],
                in_specs=[SMEM] + [VMEM] * 5,
                out_specs=[VMEM] * (group // 2 if last else 3),
                scratch_shapes=[pltpu.VMEM((rows * SUBS, LANES), F32)] * last,
                compiler_params=PARAMS,
                cost_estimate=cost(1),
                name="outer",
            )(me_arr, part, atoms, one, two, halo_weights)
            if last:
                crossed = cross(outs)
                results[chunk] = crossed + [beside(crossed)]
            else:
                states[chunk] = (tiles, *outs)

    total_cells = size_x * size_y * size_z * group * gz
    filtered, gram = pl.pallas_call(
        functools.partial(gather_kernel, group, nb, bands, 1.0 / total_cells),
        out_shape=[shape(bands * 64, LANES), shape(bands, bands)],
        in_specs=[SMEM] + [VMEM] * (CHUNKS * (group // 2 + 1)),
        out_specs=[ANY, VMEM],
        scratch_shapes=[
            pltpu.VMEM((bands * 64, LANES), F32),
            pltpu.SemaphoreType.DMA((1,)),
        ],
        compiler_params=PARAMS,
        cost_estimate=cost(5),
        name="gather",
    )(me_arr, *[block for chunk in results for block in chunk])

    gram = gram + swap(gram, 1)
    d = 2
    while d < group:
        if 2 * d < group:
            gram = gram + (swap(gram, d) + swap(gram, 2 * d) + swap(gram, 3 * d))
        else:
            gram = gram + swap(gram, d)
        d *= 4
    share = bands // gz
    terms = []
    for d in range(gz):
        term = lax.dynamic_slice_in_dim(gram, (me_z ^ d) * share, share, 0)
        terms.append(swap_z(term, d) if d else term)
    return filtered.reshape(panel.shape), sum(terms[1:], terms[0])


def solution(mesh):
    placed = (
        P(None, "gx", "gy", "gz"),
        P("gx", "gy", "gz"),
        P(("gx", "gy", "gz"), None),
        P(("gx", "gy", "gz"), None),
        P(("gx", "gy", "gz"), None, None),
        P(("gx", "gy", "gz"), None),
    )
    return jax.shard_map(
        shards,
        mesh=mesh,
        in_specs=placed,
        out_specs=(P(None, "gx", "gy", "gz"), P("gz", None)),
        check_vma=False,
    )
```

time: 168 us -> 144 us (0.86)
  starting transfers between devices: 68 us -> 39 us
  waiting for transfers between devices: 24.5 us -> 42.7 us
  Pallas kernels: 65 us -> 57.1 us
  other arithmetic: 4.3 us -> 1.08 us
  local copies, waits for them, and re-layouts: 4.94 us -> 3.16 us
    ppermute x39 -> x21, starting transfers between devices: 40.3 us -> 22.9 us  [swap(): return lax.ppermute(block, column, [(s, s ^ d) for s in range(group)])]
    ppermute x8 -> x2, starting transfers between devices: 15.5 us -> 3.36 us  [shards(): two = lax.ppermute(two, 'gz', pair_two)]
    ppermute x39 -> x21, waiting for transfers between devices: 21.5 us -> 30.9 us  [swap(): return lax.ppermute(block, column, [(s, s ^ d) for s in range(group)])]
    ppermute x0 -> x6, waiting for transfers between devices: none -> 7.09 us  [the longest x3 3.81 us: shards(): joint_one = lax.ppermute(joint_one, 'gz', pair_one)]
    ppermute x0 -> x6, starting transfers between devices: none -> 5.49 us  [the longest x3 5.28 us: shards(): joint_two = lax.ppermute(joint_two, 'gz', pair_two)]
    ppermute x8 -> x2, starting transfers between devices: 7.73 us -> 2.87 us  [shards(): one = lax.ppermute(one, 'gz', pair_one)]
    pallas_call x11 -> x21, Pallas kernels: 58.3 us -> 53.9 us  [the longest x8 31.3 us: shards(): pl.pallas_call(functools.partial(inner_kernel, gx, gy, nb, count, fold, f...]
    unnamed x83 -> x19, local copies, waits for them, and re-layouts: 3.4 us -> 0.11 us
  transfers between devices with their start and end apart: 58 -> 34, of which waited for: 16 -> 22; matrix products, arithmetic and copies ran while one was open for 1% -> 0% of each run, Pallas kernels for 34% -> 23%
where the time goes in v3:
time: 144 us
  Pallas kernels  57.1 us (40%)
  waiting for transfers between devices  42.7 us (30%)
  starting transfers between devices  39 us (27%)
  local copies, waits for them, and re-layouts  3.16 us (2%)
    pallas_call x8, Pallas kernels, shards(): pl.pallas_call(functools.partial(inner_kernel, gx, gy, nb, count, fold, f...  31.3 us
    ppermute x21, waiting for transfers between devices, swap(): return lax.ppermute(block, column, [(s, s ^ d) for s in range(group)])  30.9 us
    ppermute x21, starting transfers between devices, swap(): return lax.ppermute(block, column, [(s, s ^ d) for s in range(group)])  22.9 us
    pallas_call x8, Pallas kernels, shards(): pl.pallas_call(functools.partial(outer_kernel, gx, gy, nb, first, last, e...  13.5 us
    ppermute x3, starting transfers between devices, shards(): joint_two = lax.ppermute(joint_two, 'gz', pair_two)  5.28 us
    ppermute x3, starting transfers between devices, swap_z(): return lax.ppermute(block, 'gz', [(s, s ^ d) for s in range(gz)])  4.45 us
    ppermute x3, waiting for transfers between devices, shards(): joint_one = lax.ppermute(joint_one, 'gz', pair_one)  3.81 us
    ppermute x3, waiting for transfers between devices, swap_z(): return lax.ppermute(block, 'gz', [(s, s ^ d) for s in range(gz)])  3.45 us
  transfers between devices with their start and end apart: 34, of which 22 were waited for; matrix products, arithmetic and copies ran while one was open for 0% of the time, Pallas kernels for 23%

profile of v3, /device:TPU:0, one launch (start us, length us, event | category | flops | bytes accessed | tf_op | source)
XLA Modules:
  0.0 144.2 jit_solution(5140976313892183100)
XLA Ops:
  9.4 2.7 %collective-permute-start.3 = (f32[720,128]{1,0:T(8,128)S(1)}, f32[720,128]{1,0:T(8,128)S(1)}, u32[]{:S(2)}, u32[]{:S(2)}) collective-permute-start(f32[720,128]{1,0:T(8,128)S(1)} %get-tuple-element.69), channel_id=1, source_target_pairs={{0,8},{4,12},{8,0},{12,4},{16,24},{20,28},{24,16},{28,20},{1,9},{5... | collective-permute-start | bytes 1105928 | tf_op jit(solution)/shard_map/ppermute | solution.py:496
  14.9 2.9 %collective-permute-start.10 = (f32[512,128]{1,0:T(8,128)S(1)}, f32[512,128]{1,0:T(8,128)S(1)}, u32[]{:S(2)}, u32[]{:S(2)}) collective-permute-start(f32[512,128]{1,0:T(8,128)S(1)} %get-tuple-element.86), channel_id=1, source_target_pairs={{0,24},{4,28},{8,16},{12,20},{16,8},{20,12},{24,0},{28,4},{1,25},{... | collective-permute-start | bytes 786440 | tf_op jit(solution)/shard_map/ppermute | solution.py:496
  18.4 3.1 %collective-permute-done.3.refs_1_ = f32[720,128]{1,0:T(8,128)S(1)} collective-permute-done((f32[720,128]{1,0:T(8,128)S(1)}, f32[720,128]{1,0:T(8,128)S(1)}, u32[]{:S(2)}, u32[]{:S(2)}) %collective-permute-start.3) | collective-permute-done | bytes 368672 | tf_op jit(solution)/shard_map/ppermute | solution.py:496
  21.5 2.2 %collective-permute-start.9 = (f32[512,128]{1,0:T(8,128)S(1)}, f32[512,128]{1,0:T(8,128)S(1)}, u32[]{:S(2)}, u32[]{:S(2)}) collective-permute-start(f32[512,128]{1,0:T(8,128)S(1)} %get-tuple-element.85), channel_id=1, source_target_pairs={{0,16},{4,20},{8,24},{12,28},{16,0},{20,4},{24,8},{28,12},{1,17},{... | collective-permute-start | bytes 786440 | tf_op jit(solution)/shard_map/ppermute | solution.py:496
  23.7 7.3 %collective-permute-done.5.refs_3_ = f32[720,128]{1,0:T(8,128)S(1)} collective-permute-done((f32[720,128]{1,0:T(8,128)S(1)}, f32[720,128]{1,0:T(8,128)S(1)}, u32[]{:S(2)}, u32[]{:S(2)}) %collective-permute-start.5) | collective-permute-done | bytes 368672 | tf_op jit(solution)/shard_map/ppermute | solution.py:496
  32.6 2.1 %collective-permute-start.6 = (f32[16,8,128]{2,1,0:T(8,128)S(1)}, f32[16,8,128]{2,1,0:T(8,128)S(1)}, u32[]{:S(2)}, u32[]{:S(2)}) collective-permute-start(f32[16,8,128]{2,1,0:T(8,128)S(1)} %get-tuple-element.72.after_ref), channel_id=1, source_target_pairs={{0,1},{1,0},{2,3},{3,2},{4,5},{5,4},{6,7},{7,6},{8,9},{9,8},{10,11... | collective-permute-start | bytes 196616 | tf_op jit(solution)/shard_map/ppermute | solution.py:620
  34.7 2.5 %collective-permute-start.7 = (f32[16,8,128]{2,1,0:T(8,128)S(1)}, f32[16,8,128]{2,1,0:T(8,128)S(1)}, u32[]{:S(2)}, u32[]{:S(2)}) collective-permute-start(f32[16,8,128]{2,1,0:T(8,128)S(1)} %get-tuple-element.79), channel_id=1, source_target_pairs={{0,3},{1,2},{2,1},{3,0},{4,7},{5,6},{6,5},{7,4},{8,11},{9,10},{10,... | collective-permute-start | bytes 196616 | tf_op jit(solution)/shard_map/ppermute | solution.py:621
  37.1 2.6 %setup.1 = (f32[2048,128]{1,0:T(8,128)S(1)}, f32[128,8,128]{2,1,0:T(8,128)S(1)}, s32[128]{0:T(128)S(1)}) custom-call(s32[2]{0:T(128)S(1)} %pad_add_fusion.me_ref, f32[16,8,128]{2,1,0:T(8,128)S(1)} %get-tuple-element.72.after_ref, f32[720,128]{1,0:T(8,128)S(1)} %get-tuple-element.67.refs_0_, f32[720,128]{1,0:T(8,128)S(1)} %collective-permute-done.3.refs_1_, ...), custom_call_target="tpu_custom_call" | custom-call | flops 2000000000 | bytes 6000000 | tf_op jit(solution)/shard_map/setup/pallas_call | solution.py:581
  39.8 3.8 %inner.8 = (f32[2048,128]{1,0:T(8,128)S(1)}, f32[2048,128]{1,0:T(8,128)S(1)}) custom-call(f32[128,8,128]{2,1,0:T(8,128)S(1)} %get-tuple-element.73.after_ref.refs_2_.refs_3_, s32[128]{0:T(128)S(1)} %get-tuple-element.74.meta_ref, f32[2048,128]{1,0:T(8,128)S(1)} %get-tuple-element.75.refs_0_.refs_1_, f32[2048,128]{1,0:T(8,128)S(1)} %get-tuple-element.76.refs_1_.refs_2_, ...), custom_call_target="tpu_custom_call" | custom-call | flops 4000000000 | bytes 12000000 | tf_op jit(solution)/shard_map/inner/pallas_call | solution.py:629
  43.7 1.8 %outer.8 = (f32[2048,128]{1,0:T(8,128)S(1)}, f32[16,8,128]{2,1,0:T(8,128)S(1)}, f32[16,8,128]{2,1,0:T(8,128)S(1)}) custom-call(s32[2]{0:T(128)S(1)} %pad_add_fusion.me_ref, f32[2048,128]{1,0:T(8,128)S(1)} %get-tuple-element.77.part_ref, f32[2048,128]{1,0:T(8,128)S(1)} %get-tuple-element.78.atoms_ref, f32[16,8,128]{2,1,0:T(8,128)S(1)} %collective-permute-done.6.one_in, ...), custom_call_target="tpu_custom_call" | custom-call | flops 1000000000 | bytes 3000000 | tf_op jit(solution)/shard_map/outer/pallas_call | solution.py:640
  45.5 3.9 %inner.9 = (f32[2048,128]{1,0:T(8,128)S(1)}, f32[2048,128]{1,0:T(8,128)S(1)}) custom-call(f32[128,8,128]{2,1,0:T(8,128)S(1)} %get-tuple-element.73.after_ref.refs_2_.refs_3_, s32[128]{0:T(128)S(1)} %get-tuple-element.74.meta_ref, f32[2048,128]{1,0:T(8,128)S(1)} %get-tuple-element.80.refs_0_.refs_1_, f32[2048,128]{1,0:T(8,128)S(1)} %get-tuple-element.75.refs_0_.refs_1_, ...), custom_call_target="tpu_custom_call" | custom-call | flops 4000000000 | bytes 12000000 | tf_op jit(solution)/shard_map/inner/pallas_call | solution.py:629
  52.7 3.8 %inner.10 = (f32[2048,128]{1,0:T(8,128)S(1)}, f32[2048,128]{1,0:T(8,128)S(1)}) custom-call(f32[128,8,128]{2,1,0:T(8,128)S(1)} %get-tuple-element.73.after_ref.refs_2_.refs_3_, s32[128]{0:T(128)S(1)} %get-tuple-element.74.meta_ref, f32[2048,128]{1,0:T(8,128)S(1)} %get-tuple-element.87.refs_0_.refs_1_, f32[2048,128]{1,0:T(8,128)S(1)} %get-tuple-element.76.refs_1_.refs_2_, ...), custom_call_target="tpu_custom_call" | custom-call | flops 4000000000 | bytes 12000000 | tf_op jit(solution)/shard_map/inner/pallas_call | solution.py:629
  57.9 1.8 %outer.9 = (f32[2048,128]{1,0:T(8,128)S(1)}, f32[16,8,128]{2,1,0:T(8,128)S(1)}, f32[16,8,128]{2,1,0:T(8,128)S(1)}) custom-call(s32[2]{0:T(128)S(1)} %pad_add_fusion.me_ref, f32[2048,128]{1,0:T(8,128)S(1)} %get-tuple-element.88.part_ref, f32[2048,128]{1,0:T(8,128)S(1)} %get-tuple-element.89.atoms_ref, f32[16,8,128]{2,1,0:T(8,128)S(1)} %collective-permute-done.11.one_in, ...), custom_call_target="tpu_custom_call" | custom-call | flops 1000000000 | bytes 3000000 | tf_op jit(solution)/shard_map/outer/pallas_call | solution.py:640
  61.5 3.9 %inner.12 = (f32[2048,128]{1,0:T(8,128)S(1)}, f32[2048,128]{1,0:T(8,128)S(1)}) custom-call(f32[128,8,128]{2,1,0:T(8,128)S(1)} %get-tuple-element.73.after_ref.refs_2_.refs_3_, s32[128]{0:T(128)S(1)} %get-tuple-element.74.meta_ref, f32[2048,128]{1,0:T(8,128)S(1)} %get-tuple-element.99.refs_0_.refs_1_, f32[2048,128]{1,0:T(8,128)S(1)} %get-tuple-element.87.refs_0_.refs_1_, ...), custom_call_target="tpu_custom_call" | custom-call | flops 4000000000 | bytes 12000000 | tf_op jit(solution)/shard_map/inner/pallas_call | solution.py:629
  67.9 1.8 %outer.11 = (f32[2048,128]{1,0:T(8,128)S(1)}, f32[16,8,128]{2,1,0:T(8,128)S(1)}, f32[16,8,128]{2,1,0:T(8,128)S(1)}) custom-call(s32[2]{0:T(128)S(1)} %pad_add_fusion.me_ref, f32[2048,128]{1,0:T(8,128)S(1)} %get-tuple-element.100.part_ref, f32[2048,128]{1,0:T(8,128)S(1)} %get-tuple-element.101.atoms_ref, f32[32,8,128]{2,1,0:T(8,128)S(1)} %collective-permute-done.13.one_in, ...), custom_call_target="tpu_custom_call" | custom-call | flops 1000000000 | bytes 3000000 | tf_op jit(solution)/shard_map/outer/pallas_call | solution.py:640
  69.7 3.9 %inner.14 = (f32[2048,128]{1,0:T(8,128)S(1)}, f32[2048,128]{1,0:T(8,128)S(1)}) custom-call(f32[128,8,128]{2,1,0:T(8,128)S(1)} %get-tuple-element.73.after_ref.refs_2_.refs_3_, s32[128]{0:T(128)S(1)} %get-tuple-element.74.meta_ref, f32[2048,128]{1,0:T(8,128)S(1)} %get-tuple-element.109.refs_0_.refs_1_, f32[2048,128]{1,0:T(8,128)S(1)} %get-tuple-element.99.refs_0_.refs_1_, ...), custom_call_target="tpu_custom_call" | custom-call | flops 4000000000 | bytes 12000000 | tf_op jit(solution)/shard_map/inner/pallas_call | solution.py:629
  73.6 1.8 %outer.10 = (f32[2048,128]{1,0:T(8,128)S(1)}, f32[16,8,128]{2,1,0:T(8,128)S(1)}, f32[16,8,128]{2,1,0:T(8,128)S(1)}) custom-call(s32[2]{0:T(128)S(1)} %pad_add_fusion.me_ref, f32[2048,128]{1,0:T(8,128)S(1)} %get-tuple-element.81.part_ref, f32[2048,128]{1,0:T(8,128)S(1)} %get-tuple-element.82.atoms_ref, f32[32,8,128]{2,1,0:T(8,128)S(1)} %collective-permute-done.13.one_in, ...), custom_call_target="tpu_custom_call" | custom-call | flops 1000000000 | bytes 3000000 | tf_op jit(solution)/shard_map/outer/pallas_call | solution.py:640
  77.4 3.9 %inner.11 = (f32[2048,128]{1,0:T(8,128)S(1)}, f32[2048,128]{1,0:T(8,128)S(1)}) custom-call(f32[128,8,128]{2,1,0:T(8,128)S(1)} %get-tuple-element.73.after_ref.refs_2_.refs_3_, s32[128]{0:T(128)S(1)} %get-tuple-element.74.meta_ref, f32[2048,128]{1,0:T(8,128)S(1)} %get-tuple-element.95.refs_0_.refs_1_, f32[2048,128]{1,0:T(8,128)S(1)} %get-tuple-element.80.refs_0_.refs_1_, ...), custom_call_target="tpu_custom_call" | custom-call | flops 4000000000 | bytes 12000000 | tf_op jit(solution)/shard_map/inner/pallas_call | solution.py:629
  83.7 1.8 %outer.13 = (f32[2048,128]{1,0:T(8,128)S(1)}, f32[16,8,128]{2,1,0:T(8,128)S(1)}, f32[16,8,128]{2,1,0:T(8,128)S(1)}) custom-call(s32[2]{0:T(128)S(1)} %pad_add_fusion.me_ref, f32[2048,128]{1,0:T(8,128)S(1)} %get-tuple-element.110.part_ref, f32[2048,128]{1,0:T(8,128)S(1)} %get-tuple-element.111.atoms_ref, f32[32,8,128]{2,1,0:T(8,128)S(1)} %collective-permute-done.15.one_in, ...), custom_call_target="tpu_custom_call" | custom-call | flops 1000000000 | bytes 3000000 | tf_op jit(solution)/shard_map/outer/pallas_call | solution.py:640
  85.5 1.9 %outer.12 = (f32[2048,128]{1,0:T(8,128)S(1)}, f32[16,8,128]{2,1,0:T(8,128)S(1)}, f32[16,8,128]{2,1,0:T(8,128)S(1)}) custom-call(s32[2]{0:T(128)S(1)} %pad_add_fusion.me_ref, f32[2048,128]{1,0:T(8,128)S(1)} %get-tuple-element.96.part_ref, f32[2048,128]{1,0:T(8,128)S(1)} %get-tuple-element.97.atoms_ref, f32[32,8,128]{2,1,0:T(8,128)S(1)} %collective-permute-done.15.one_in, ...), custom_call_target="tpu_custom_call" | custom-call | flops 1000000000 | bytes 3000000 | tf_op jit(solution)/shard_map/outer/pallas_call | solution.py:640
  89.3 4.1 %inner.13 = (f32[2048,128]{1,0:T(8,128)S(1)}, f32[2048,128]{1,0:T(8,128)S(1)}) custom-call(f32[128,8,128]{2,1,0:T(8,128)S(1)} %get-tuple-element.73.after_ref.refs_2_.refs_3_, s32[128]{0:T(128)S(1)} %get-tuple-element.74.meta_ref, f32[2048,128]{1,0:T(8,128)S(1)} %get-tuple-element.105.refs_0_, f32[2048,128]{1,0:T(8,128)S(1)} %get-tuple-element.95.refs_0_.refs_1_, ...), custom_call_target="tpu_custom_call" | custom-call | flops 4000000000 | bytes 12000000 | tf_op jit(solution)/shard_map/inner/pallas_call | solution.py:629
  96.9 3.9 %inner.15 = (f32[2048,128]{1,0:T(8,128)S(1)}, f32[2048,128]{1,0:T(8,128)S(1)}) custom-call(f32[512,128]{1,0:T(8,128)S(1)} %get-tuple-element.115.after_ref.refs_0_, s32[128]{0:T(128)S(1)} %get-tuple-element.74.meta_ref, f32[2048,128]{1,0:T(8,128)S(1)} %get-tuple-element.119.refs_0_, f32[2048,128]{1,0:T(8,128)S(1)} %get-tuple-element.109.refs_0_.refs_1_, ...), custom_call_target="tpu_custom_call" | custom-call | flops 4000000000 | bytes 12000000 | tf_op jit(solution)/shard_map/inner/pallas_call | solution.py:629
  102.1 2.5 %collective-permute-start.25 = (f32[512,128]{1,0:T(8,128)S(1)}, f32[512,128]{1,0:T(8,128)S(1)}, u32[]{:S(2)}, u32[]{:S(2)}) collective-permute-start(f32[512,128]{1,0:T(8,128)S(1)} %get-tuple-element.125), channel_id=1, source_target_pairs={{0,24},{4,28},{8,16},{12,20},{16,8},{20,12},{24,0},{28,4},{1,25},{... | collective-permute-start | bytes 786440 | tf_op jit(solution)/shard_map/ppermute | solution.py:496
  105.6 2.5 %collective-permute-start.21 = (f32[512,128]{1,0:T(8,128)S(1)}, f32[512,128]{1,0:T(8,128)S(1)}, u32[]{:S(2)}, u32[]{:S(2)}) collective-permute-start(f32[512,128]{1,0:T(8,128)S(1)} %get-tuple-element.118), channel_id=1, source_target_pairs={{0,24},{4,28},{8,16},{12,20},{16,8},{20,12},{24,0},{28,4},{1,25},{... | collective-permute-start | bytes 786440 | tf_op jit(solution)/shard_map/ppermute | solution.py:496
  108.7 3.6 %collective-permute-done.25.refs_8_ = f32[512,128]{1,0:T(8,128)S(1)} collective-permute-done((f32[512,128]{1,0:T(8,128)S(1)}, f32[512,128]{1,0:T(8,128)S(1)}, u32[]{:S(2)}, u32[]{:S(2)}) %collective-permute-start.25) | collective-permute-done | bytes 262176 | tf_op jit(solution)/shard_map/ppermute | solution.py:496
  115.8 2.6 %collective-permute-done.21.refs_3_ = f32[512,128]{1,0:T(8,128)S(1)} collective-permute-done((f32[512,128]{1,0:T(8,128)S(1)}, f32[512,128]{1,0:T(8,128)S(1)}, u32[]{:S(2)}, u32[]{:S(2)}) %collective-permute-start.21) | collective-permute-done | bytes 262176 | tf_op jit(solution)/shard_map/ppermute | solution.py:496
  118.4 2.8 %collective-permute-done.20.refs_2_ = f32[512,128]{1,0:T(8,128)S(1)} collective-permute-done((f32[512,128]{1,0:T(8,128)S(1)}, f32[512,128]{1,0:T(8,128)S(1)}, u32[]{:S(2)}, u32[]{:S(2)}) %collective-permute-start.20) | collective-permute-done | bytes 262176 | tf_op jit(solution)/shard_map/ppermute | solution.py:496
  121.4 1.9 %collective-permute-done.22.refs_4_ = f32[1024,128]{1,0:T(8,128)S(1)} collective-permute-done((f32[1024,128]{1,0:T(8,128)S(1)}, f32[1024,128]{1,0:T(8,128)S(1)}, u32[]{:S(2)}, u32[]{:S(2)}) %collective-permute-start.22) | collective-permute-done | bytes 524320 | tf_op jit(solution)/shard_map/ppermute | solution.py:496
  123.3 3.4 %gather.1 = (f32[4096,128]{1,0:T(8,128)}, f32[64,64]{1,0:T(8,128)S(1)}) custom-call(s32[2]{0:T(128)S(1)} %pad_add_fusion.me_ref, f32[512,128]{1,0:T(8,128)S(1)} %get-tuple-element.115.after_ref.refs_0_, f32[512,128]{1,0:T(8,128)S(1)} %collective-permute-done.19.refs_1_, f32[512,128]{1,0:T(8,128)S(1)} %collective-permute-done.20.refs_2_, ...), custom_call_target="tpu_custom_call" | custom-call | flops 5000000000 | bytes 15000000 | tf_op jit(solution)/shard_map/gather/pallas_call | solution.py:659
  133.4 2.3 %collective-permute-done.30 = f32[64,64]{1,0:T(8,128)S(1)} collective-permute-done((f32[64,64]{1,0:T(8,128)S(1)}, f32[64,64]{1,0:T(8,128)S(1)}, u32[]{:S(2)}, u32[]{:S(2)}) %collective-permute-start.30) | collective-permute-done | bytes 16416 | tf_op jit(solution)/shard_map/ppermute | solution.py:496
  138.2 2.0 %collective-permute-start.33 = (f32[16,64]{1,0:T(8,128)S(1)}, f32[16,64]{1,0:T(8,128)S(1)}, u32[]{:S(2)}, u32[]{:S(2)}) collective-permute-start(f32[16,64]{1,0:T(8,128)S(1)} %get-tuple-element.129), channel_id=1, source_target_pairs={{0,3},{1,2},{2,1},{3,0},{4,7},{5,6},{6,5},{7,4},{8,11},{9,10},{10,... | collective-permute-start | bytes 12296 | tf_op jit(solution)/shard_map/ppermute | solution.py:499
  140.9 2.7 %collective-permute-done.33 = f32[16,64]{1,0:T(8,128)S(1)} collective-permute-done((f32[16,64]{1,0:T(8,128)S(1)}, f32[16,64]{1,0:T(8,128)S(1)}, u32[]{:S(2)}, u32[]{:S(2)}) %collective-permute-start.33) | collective-permute-done | bytes 4128 | tf_op jit(solution)/shard_map/ppermute | solution.py:499
  (111 shorter events, 48.9 us)
Async XLA Ops:
  2.7 2.2 %collective-permute-start = (f32[1024,128]{1,0:T(8,128)}, f32[1024,128]{1,0:T(8,128)S(1)}, u32[]{:S(2)}, u32[]{:S(2)}) collective-permute-start(f32[1024,128]{1,0:T(8,128)} %bitcast.4), channel_id=1, source_target_pairs={{0,4},{4,0},{8,12},{12,8},{16,20},{20,16},{24,28},{28,24},{1,5},{5... | collective-permute-start | bytes 1572872 | tf_op jit(solution)/shard_map/ppermute | solution.py:496
  5.8 7.8 %collective-permute-start.1 = (f32[1024,128]{1,0:T(8,128)}, f32[1024,128]{1,0:T(8,128)S(1)}, u32[]{:S(2)}, u32[]{:S(2)}) collective-permute-start(f32[1024,128]{1,0:T(8,128)} %bitcast.6), channel_id=1, source_target_pairs={{0,4},{4,0},{8,12},{12,8},{16,20},{20,16},{24,28},{28,24},{1,5},{5... | collective-permute-start | bytes 1572872 | tf_op jit(solution)/shard_map/ppermute | solution.py:496
  9.4 12.2 %collective-permute-start.3 = (f32[720,128]{1,0:T(8,128)S(1)}, f32[720,128]{1,0:T(8,128)S(1)}, u32[]{:S(2)}, u32[]{:S(2)}) collective-permute-start(f32[720,128]{1,0:T(8,128)S(1)} %get-tuple-element.69), channel_id=1, source_target_pairs={{0,8},{4,12},{8,0},{12,4},{16,24},{20,28},{24,16},{28,20},{1,9},{5... | collective-permute-start | bytes 1105928 | tf_op jit(solution)/shard_map/ppermute | solution.py:496
  12.1 11.6 %collective-permute-start.4 = (f32[720,128]{1,0:T(8,128)S(1)}, f32[720,128]{1,0:T(8,128)S(1)}, u32[]{:S(2)}, u32[]{:S(2)}) collective-permute-start(f32[720,128]{1,0:T(8,128)S(1)} %get-tuple-element.70), channel_id=1, source_target_pairs={{0,16},{4,20},{8,24},{12,28},{16,0},{20,4},{24,8},{28,12},{1,17},{... | collective-permute-start | bytes 1105928 | tf_op jit(solution)/shard_map/ppermute | solution.py:496
  13.6 17.4 %collective-permute-start.5 = (f32[720,128]{1,0:T(8,128)S(1)}, f32[720,128]{1,0:T(8,128)S(1)}, u32[]{:S(2)}, u32[]{:S(2)}) collective-permute-start(f32[720,128]{1,0:T(8,128)S(1)} %get-tuple-element.71), channel_id=1, source_target_pairs={{0,24},{4,28},{8,16},{12,20},{16,8},{20,12},{24,0},{28,4},{1,25},{... | collective-permute-start | bytes 1105928 | tf_op jit(solution)/shard_map/ppermute | solution.py:496
  14.9 34.5 %collective-permute-start.10 = (f32[512,128]{1,0:T(8,128)S(1)}, f32[512,128]{1,0:T(8,128)S(1)}, u32[]{:S(2)}, u32[]{:S(2)}) collective-permute-start(f32[512,128]{1,0:T(8,128)S(1)} %get-tuple-element.86), channel_id=1, source_target_pairs={{0,24},{4,28},{8,16},{12,20},{16,8},{20,12},{24,0},{28,4},{1,25},{... | collective-permute-start | bytes 786440 | tf_op jit(solution)/shard_map/ppermute | solution.py:496
  17.9 31.6 %collective-permute-start.8 = (f32[512,128]{1,0:T(8,128)S(1)}, f32[512,128]{1,0:T(8,128)S(1)}, u32[]{:S(2)}, u32[]{:S(2)}) collective-permute-start(f32[512,128]{1,0:T(8,128)S(1)} %get-tuple-element.84), channel_id=1, source_target_pairs={{0,8},{4,12},{8,0},{12,4},{16,24},{20,28},{24,16},{28,20},{1,9},{5... | collective-permute-start | bytes 786440 | tf_op jit(solution)/shard_map/ppermute | solution.py:496
  21.5 27.9 %collective-permute-start.9 = (f32[512,128]{1,0:T(8,128)S(1)}, f32[512,128]{1,0:T(8,128)S(1)}, u32[]{:S(2)}, u32[]{:S(2)}) collective-permute-start(f32[512,128]{1,0:T(8,128)S(1)} %get-tuple-element.85), channel_id=1, source_target_pairs={{0,16},{4,20},{8,24},{12,28},{16,0},{20,4},{24,8},{28,12},{1,17},{... | collective-permute-start | bytes 786440 | tf_op jit(solution)/shard_map/ppermute | solution.py:496
  32.6 11.1 %collective-permute-start.6 = (f32[16,8,128]{2,1,0:T(8,128)S(1)}, f32[16,8,128]{2,1,0:T(8,128)S(1)}, u32[]{:S(2)}, u32[]{:S(2)}) collective-permute-start(f32[16,8,128]{2,1,0:T(8,128)S(1)} %get-tuple-element.72.after_ref), channel_id=1, source_target_pairs={{0,1},{1,0},{2,3},{3,2},{4,5},{5,4},{6,7},{7,6},{8,9},{9,8},{10,11... | collective-permute-start | bytes 196616 | tf_op jit(solution)/shard_map/ppermute | solution.py:620
  34.7 9.0 %collective-permute-start.7 = (f32[16,8,128]{2,1,0:T(8,128)S(1)}, f32[16,8,128]{2,1,0:T(8,128)S(1)}, u32[]{:S(2)}, u32[]{:S(2)}) collective-permute-start(f32[16,8,128]{2,1,0:T(8,128)S(1)} %get-tuple-element.79), channel_id=1, source_target_pairs={{0,3},{1,2},{2,1},{3,0},{4,7},{5,6},{6,5},{7,4},{8,11},{9,10},{10,... | collective-permute-start | bytes 196616 | tf_op jit(solution)/shard_map/ppermute | solution.py:621
  51.0 5.5 %collective-permute-start.11 = (f32[16,8,128]{2,1,0:T(8,128)S(1)}, f32[16,8,128]{2,1,0:T(8,128)S(1)}, u32[]{:S(2)}, u32[]{:S(2)}) collective-permute-start(f32[16,8,128]{2,1,0:T(8,128)S(1)} %get-tuple-element.90), channel_id=1, source_target_pairs={{0,1},{1,0},{2,3},{3,2},{4,5},{5,4},{6,7},{7,6},{8,9},{9,8},{10,11... | collective-permute-start | bytes 196616 | tf_op jit(solution)/shard_map/ppermute | solution.py:620
  51.8 6.1 %collective-permute-start.12 = (f32[16,8,128]{2,1,0:T(8,128)S(1)}, f32[16,8,128]{2,1,0:T(8,128)S(1)}, u32[]{:S(2)}, u32[]{:S(2)}) collective-permute-start(f32[16,8,128]{2,1,0:T(8,128)S(1)} %get-tuple-element.91), channel_id=1, source_target_pairs={{0,3},{1,2},{2,1},{3,0},{4,7},{5,6},{6,5},{7,4},{8,11},{9,10},{10,... | collective-permute-start | bytes 196616 | tf_op jit(solution)/shard_map/ppermute | solution.py:621
  59.7 6.9 %collective-permute-start.14 = (f32[32,8,128]{2,1,0:T(8,128)S(1)}, f32[32,8,128]{2,1,0:T(8,128)S(1)}, u32[]{:S(2)}, u32[]{:S(2)}) collective-permute-start(f32[32,8,128]{2,1,0:T(8,128)S(1)} %pad_maximum_fusion.3), channel_id=1, source_target_pairs={{0,3},{1,2},{2,1},{3,0},{4,7},{5,6},{6,5},{7,4},{8,11},{9,10},{10,... | collective-permute-start | bytes 393224 | tf_op jit(solution)/shard_map/ppermute | solution.py:615
  61.4 6.4 %collective-permute-start.13 = (f32[32,8,128]{2,1,0:T(8,128)S(1)}, f32[32,8,128]{2,1,0:T(8,128)S(1)}, u32[]{:S(2)}, u32[]{:S(2)}) collective-permute-start(f32[32,8,128]{2,1,0:T(8,128)S(1)} %pad_maximum_fusion.2), channel_id=1, source_target_pairs={{0,1},{1,0},{2,3},{3,2},{4,5},{5,4},{6,7},{7,6},{8,9},{9,8},{10,11... | collective-permute-start | bytes 393224 | tf_op jit(solution)/shard_map/ppermute | solution.py:614
  75.5 6.9 %collective-permute-start.16 = (f32[32,8,128]{2,1,0:T(8,128)S(1)}, f32[32,8,128]{2,1,0:T(8,128)S(1)}, u32[]{:S(2)}, u32[]{:S(2)}) collective-permute-start(f32[32,8,128]{2,1,0:T(8,128)S(1)} %pad_maximum_fusion.5), channel_id=1, source_target_pairs={{0,3},{1,2},{2,1},{3,0},{4,7},{5,6},{6,5},{7,4},{8,11},{9,10},{10,... | collective-permute-start | bytes 393224 | tf_op jit(solution)/shard_map/ppermute | solution.py:615
  77.3 6.4 %collective-permute-start.15 = (f32[32,8,128]{2,1,0:T(8,128)S(1)}, f32[32,8,128]{2,1,0:T(8,128)S(1)}, u32[]{:S(2)}, u32[]{:S(2)}) collective-permute-start(f32[32,8,128]{2,1,0:T(8,128)S(1)} %pad_maximum_fusion.4), channel_id=1, source_target_pairs={{0,1},{1,0},{2,3},{3,2},{4,5},{5,4},{6,7},{7,6},{8,9},{9,8},{10,11... | collective-permute-start | bytes 393224 | tf_op jit(solution)/shard_map/ppermute | solution.py:614
  87.4 6.9 %collective-permute-start.18 = (f32[32,8,128]{2,1,0:T(8,128)S(1)}, f32[32,8,128]{2,1,0:T(8,128)S(1)}, u32[]{:S(2)}, u32[]{:S(2)}) collective-permute-start(f32[32,8,128]{2,1,0:T(8,128)S(1)} %pad_maximum_fusion.7), channel_id=1, source_target_pairs={{0,3},{1,2},{2,1},{3,0},{4,7},{5,6},{6,5},{7,4},{8,11},{9,10},{10,... | collective-permute-start | bytes 393224 | tf_op jit(solution)/shard_map/ppermute | solution.py:615
  89.3 6.4 %collective-permute-start.17 = (f32[32,8,128]{2,1,0:T(8,128)S(1)}, f32[32,8,128]{2,1,0:T(8,128)S(1)}, u32[]{:S(2)}, u32[]{:S(2)}) collective-permute-start(f32[32,8,128]{2,1,0:T(8,128)S(1)} %pad_maximum_fusion.6), channel_id=1, source_target_pairs={{0,1},{1,0},{2,3},{3,2},{4,5},{5,4},{6,7},{7,6},{8,9},{9,8},{10,11... | collective-permute-start | bytes 393224 | tf_op jit(solution)/shard_map/ppermute | solution.py:614
  102.1 10.2 %collective-permute-start.25 = (f32[512,128]{1,0:T(8,128)S(1)}, f32[512,128]{1,0:T(8,128)S(1)}, u32[]{:S(2)}, u32[]{:S(2)}) collective-permute-start(f32[512,128]{1,0:T(8,128)S(1)} %get-tuple-element.125), channel_id=1, source_target_pairs={{0,24},{4,28},{8,16},{12,20},{16,8},{20,12},{24,0},{28,4},{1,25},{... | collective-permute-start | bytes 786440 | tf_op jit(solution)/shard_map/ppermute | solution.py:496
  104.6 11.0 %collective-permute-start.24 = (f32[512,128]{1,0:T(8,128)S(1)}, f32[512,128]{1,0:T(8,128)S(1)}, u32[]{:S(2)}, u32[]{:S(2)}) collective-permute-start(f32[512,128]{1,0:T(8,128)S(1)} %get-tuple-element.124), channel_id=1, source_target_pairs={{0,16},{4,20},{8,24},{12,28},{16,0},{20,4},{24,8},{28,12},{1,17},{... | collective-permute-start | bytes 786440 | tf_op jit(solution)/shard_map/ppermute | solution.py:496
  105.1 10.5 %collective-permute-start.23 = (f32[512,128]{1,0:T(8,128)S(1)}, f32[512,128]{1,0:T(8,128)S(1)}, u32[]{:S(2)}, u32[]{:S(2)}) collective-permute-start(f32[512,128]{1,0:T(8,128)S(1)} %get-tuple-element.123), channel_id=1, source_target_pairs={{0,8},{4,12},{8,0},{12,4},{16,24},{20,28},{24,16},{28,20},{1,9},{5... | collective-permute-start | bytes 786440 | tf_op jit(solution)/shard_map/ppermute | solution.py:496
  105.6 12.7 %collective-permute-start.21 = (f32[512,128]{1,0:T(8,128)S(1)}, f32[512,128]{1,0:T(8,128)S(1)}, u32[]{:S(2)}, u32[]{:S(2)}) collective-permute-start(f32[512,128]{1,0:T(8,128)S(1)} %get-tuple-element.118), channel_id=1, source_target_pairs={{0,24},{4,28},{8,16},{12,20},{16,8},{20,12},{24,0},{28,4},{1,25},{... | collective-permute-start | bytes 786440 | tf_op jit(solution)/shard_map/ppermute | solution.py:496
  108.2 13.1 %collective-permute-start.20 = (f32[512,128]{1,0:T(8,128)S(1)}, f32[512,128]{1,0:T(8,128)S(1)}, u32[]{:S(2)}, u32[]{:S(2)}) collective-permute-start(f32[512,128]{1,0:T(8,128)S(1)} %get-tuple-element.117), channel_id=1, source_target_pairs={{0,16},{4,20},{8,24},{12,28},{16,0},{20,4},{24,8},{28,12},{1,17},{... | collective-permute-start | bytes 786440 | tf_op jit(solution)/shard_map/ppermute | solution.py:496
  112.3 9.0 %collective-permute-start.19 = (f32[512,128]{1,0:T(8,128)S(1)}, f32[512,128]{1,0:T(8,128)S(1)}, u32[]{:S(2)}, u32[]{:S(2)}) collective-permute-start(f32[512,128]{1,0:T(8,128)S(1)} %get-tuple-element.116), channel_id=1, source_target_pairs={{0,8},{4,12},{8,0},{12,4},{16,24},{20,28},{24,16},{28,20},{1,9},{5... | collective-permute-start | bytes 786440 | tf_op jit(solution)/shard_map/ppermute | solution.py:496
  115.7 5.7 %collective-permute-start.26 = (f32[1024,128]{1,0:T(8,128)S(1)}, f32[1024,128]{1,0:T(8,128)S(1)}, u32[]{:S(2)}, u32[]{:S(2)}) collective-permute-start(f32[1024,128]{1,0:T(8,128)S(1)} %pad_maximum_fusion.1), channel_id=1, source_target_pairs={{0,4},{4,0},{8,12},{12,8},{16,20},{20,16},{24,28},{28,24},{1,5},{5... | collective-permute-start | bytes 1572872 | tf_op jit(solution)/shard_map/ppermute | solution.py:496
  121.3 2.0 %collective-permute-start.22 = (f32[1024,128]{1,0:T(8,128)S(1)}, f32[1024,128]{1,0:T(8,128)S(1)}, u32[]{:S(2)}, u32[]{:S(2)}) collective-permute-start(f32[1024,128]{1,0:T(8,128)S(1)} %pad_maximum_fusion), channel_id=1, source_target_pairs={{0,4},{4,0},{8,12},{12,8},{16,20},{20,16},{24,28},{28,24},{1,5},{5... | collective-permute-start | bytes 1572872 | tf_op jit(solution)/shard_map/ppermute | solution.py:496
  128.0 3.9 %collective-permute-start.28 = (f32[64,64]{1,0:T(8,128)S(1)}, f32[64,64]{1,0:T(8,128)S(1)}, u32[]{:S(2)}, u32[]{:S(2)}) collective-permute-start(f32[64,64]{1,0:T(8,128)S(1)} %add.73), channel_id=1, source_target_pairs={{0,8},{4,12},{8,0},{12,4},{16,24},{20,28},{24,16},{28,20},{1,9},{5... | collective-permute-start | bytes 49160 | tf_op jit(solution)/shard_map/ppermute | solution.py:496
  129.4 4.0 %collective-permute-start.29 = (f32[64,64]{1,0:T(8,128)S(1)}, f32[64,64]{1,0:T(8,128)S(1)}, u32[]{:S(2)}, u32[]{:S(2)}) collective-permute-start(f32[64,64]{1,0:T(8,128)S(1)} %add.73), channel_id=1, source_target_pairs={{0,16},{4,20},{8,24},{12,28},{16,0},{20,4},{24,8},{28,12},{1,17},{... | collective-permute-start | bytes 49160 | tf_op jit(solution)/shard_map/ppermute | solution.py:496
  130.9 4.8 %collective-permute-start.30 = (f32[64,64]{1,0:T(8,128)S(1)}, f32[64,64]{1,0:T(8,128)S(1)}, u32[]{:S(2)}, u32[]{:S(2)}) collective-permute-start(f32[64,64]{1,0:T(8,128)S(1)} %add.73), channel_id=1, source_target_pairs={{0,24},{4,28},{8,16},{12,20},{16,8},{20,12},{24,0},{28,4},{1,25},{... | collective-permute-start | bytes 49160 | tf_op jit(solution)/shard_map/ppermute | solution.py:496
  135.7 4.5 %collective-permute-start.31 = (f32[16,64]{1,0:T(8,128)S(1)}, f32[16,64]{1,0:T(8,128)S(1)}, u32[]{:S(2)}, u32[]{:S(2)}) collective-permute-start(f32[16,64]{1,0:T(8,128)S(1)} %get-tuple-element.128), channel_id=1, source_target_pairs={{0,1},{1,0},{2,3},{3,2},{4,5},{5,4},{6,7},{7,6},{8,9},{9,8},{10,11... | collective-permute-start | bytes 12296 | tf_op jit(solution)/shard_map/ppermute | solution.py:499
  136.4 4.5 %collective-permute-start.32 = (f32[16,64]{1,0:T(8,128)S(1)}, f32[16,64]{1,0:T(8,128)S(1)}, u32[]{:S(2)}, u32[]{:S(2)}) collective-permute-start(f32[16,64]{1,0:T(8,128)S(1)} %get-tuple-element.130), channel_id=1, source_target_pairs={{0,2},{1,3},{2,0},{3,1},{4,6},{5,7},{6,4},{7,5},{8,10},{9,11},{10,... | collective-permute-start | bytes 12296 | tf_op jit(solution)/shard_map/ppermute | solution.py:499
  138.2 5.4 %collective-permute-start.33 = (f32[16,64]{1,0:T(8,128)S(1)}, f32[16,64]{1,0:T(8,128)S(1)}, u32[]{:S(2)}, u32[]{:S(2)}) collective-permute-start(f32[16,64]{1,0:T(8,128)S(1)} %get-tuple-element.129), channel_id=1, source_target_pairs={{0,3},{1,2},{2,1},{3,0},{4,7},{5,6},{6,5},{7,4},{8,11},{9,10},{10,... | collective-permute-start | bytes 12296 | tf_op jit(solution)/shard_map/ppermute | solution.py:499
  (12 other events, 40.4 us)

commit v4 on v3

--- a/solution.py
+++ b/solution.py
@@ -117,18 +117,18 @@
     return pairs
 
 
-def setup_kernel(gx, gy, nb, count, fold, me_ref, after_ref, *refs):
+def atoms_kernel(gx, gy, nb, count, fold, me_ref, after_ref, *refs):
     half = gx * gy // 2
-    diag_ref, roots_ref, meta_ref, raw, sem = refs[half:]
-    rows = 4 * count
+    roots_ref, meta_ref, raw, sem = refs[half:]
+    rows = 4 * count + 8
     sources = []
     for n in range(half):
         for other in range(2):
-            at = 2 * nb * 64 + other * (72 + rows)
-            sources.append((me_ref[0] ^ (2 * n + other), refs[n].at[pl.ds(at, 72 + rows)]))
+            at = 2 * nb * 64 + other * rows
+            sources.append((me_ref[0] ^ (2 * n + other), refs[n].at[pl.ds(at, rows)]))
     copies = [
         pltpu.make_async_copy(
-            source.at[pl.ds(64 + rows, 8)],
+            source.at[pl.ds(rows - 8, 8)],
             raw.at[pl.ds(pl.multiple_of(slot * 8, 8), 8)],
             sem.at[0],
         )
@@ -139,17 +139,11 @@
     sub = lax.broadcasted_iota(jnp.int32, (SUBS, LANES), 0)
     per_slot = count // (2 * fold)
     for slot, source in sources:
-        i, j = slot // gy, slot % gy
-        for x in range(8):
-            value = source[x * 8 : x * 8 + 8, :] * (1.0 / HALF) + DIAGONAL
-            for y in range(8):
-                at = ((j * 8 + y) * 8 + x) * SUBS + i * nb
-                diag_ref[pl.ds(at, nb)] = jnp.broadcast_to(value[y : y + 1], (nb, LANES))
         for m in range(per_slot):
             for k in range(8):
                 parts = []
                 for f in range(fold):
-                    at = 64 + (m * fold + f) * 8 + k
+                    at = (m * fold + f) * 8 + k
                     parts.append(jnp.broadcast_to(source[at : at + 1, :], (SUBS, LANES)))
                 value = parts[0] if fold == 1 else jnp.where(sub < SUBS // 2, parts[0], parts[1])
                 roots_ref[(slot * per_slot + m) * 8 + k] = value
@@ -165,6 +159,21 @@
         return carry
 
     lax.fori_loop(0, gx * gy, corners, 0)
+
+
+def diagonal_kernel(gx, gy, nb, me_ref, after_ref, *refs):
+    half = gx * gy // 2
+    diag_ref = refs[half]
+    for n in range(half):
+        for other in range(2):
+            slot = me_ref[0] ^ (2 * n + other)
+            i, j = slot // gy, slot % gy
+            for x in range(8):
+                first = 2 * nb * 64 + other * 64 + x * 8
+                value = refs[n][first : first + 8, :] * (1.0 / HALF) + DIAGONAL
+                for y in range(8):
+                    at = ((j * 8 + y) * 8 + x) * SUBS + i * nb
+                    diag_ref[pl.ds(at, nb)] = jnp.broadcast_to(value[y : y + 1], (nb, LANES))
 
 
 def pack_edges(values, lane):
@@ -185,8 +194,10 @@
     return jnp.where(even, high, low), jnp.where(even, low, high)
 
 
-def pack_kernel(group, size, chunk, tables, me_ref, field, passed, *refs):
-    blocks, sem = refs[2 if tables else 1 : -1], refs[-1]
+def join_kernel(
+    group, size, chunk, extra, me_ref, field, after_ref, passed, own_ref, other_ref, *refs
+):
+    blocks, sem = refs[:-1], refs[-1]
     copies = []
     for n, block in enumerate(blocks):
         chip = me_ref[0] // 2 ^ n
@@ -200,26 +211,28 @@
         )
     for copy in copies:
         copy.start()
+    first, rows = extra
     for n, block in enumerate(blocks):
         chip = me_ref[0] // 2 ^ n
-        block[pl.ds(size, size)] = passed[pl.ds(pl.multiple_of(chip * size, 64), size)]
-        if tables:
-            block[pl.ds(2 * size, tables)] = refs[0][...]
-            block[pl.ds(2 * size + tables, tables)] = refs[1][...]
+        row = (chunk * group // 2 + chip) * size
+        block[pl.ds(size, size)] = passed[pl.ds(pl.multiple_of(row, 64), size)]
+        if rows:
+            block[pl.ds(2 * size, rows)] = own_ref[pl.ds(first, rows)]
+            block[pl.ds(2 * size + rows, rows)] = other_ref[pl.ds(first, rows)]
     for copy in copies:
         copy.wait()
 
 
 def unpack_kernel(gx, gy, nb, me_ref, after_ref, *refs):
     half = gx * gy // 2
-    z_ref, one_ref, two_ref = refs[half:]
     size = nb * 64
+    z_ref, one_ref, two_ref = refs[-3:]
     for n in range(half):
         for other in range(2):
             slot = me_ref[0] ^ (2 * n + other)
             i, j = slot // gy, slot % gy
             for x in range(8):
-                first = other * size + x * 8
+                first = x * 8 + other * size
                 turned = swapped([refs[n][first + b * 64 : first + b * 64 + 8] for b in range(nb)])
                 for y in range(8):
                     z_ref[pl.ds(((j * 8 + y) * 8 + x) * SUBS + i * nb, nb)] = turned[y]
@@ -242,7 +255,7 @@
 
 def inner_kernel(gx, gy, nb, count, fold, first, after_ref, meta_ref, *refs):
     if first:
-        z_ref, diag_ref, roots_ref, w_ref, sum_ref = refs[:5]
+        z_ref, roots_ref, w_ref, sum_ref = refs[:4]
     else:
         z_ref, prev_ref, diag_ref, roots_ref, w_ref, sum_ref = refs[:6]
     out_ref, atoms_ref, acc, tile_ref, spread_ref = refs[-5:]
@@ -347,7 +360,8 @@
             for x in range(8):
                 here = tile_rows(four * 32 + 8 * q + x)
                 total = acc[here] + out_ref[here]
-                total = total + diag_ref[here] * values[x]
+                if not first:
+                    total = total + diag_ref[here] * values[x]
                 for k in range(1, REACH + 1):
                     total = total + TAPS[k] * (wide[8 + x + k] + wide[8 + x - k])
                 if not first:
@@ -364,9 +378,12 @@
     lax.fori_loop(0, gy, block, 0)
 
 
-def outer_kernel(gx, gy, nb, first, last, edge, me_ref, part_ref, atoms_ref, one_in, two_in, *refs):
+def outer_kernel(
+    gx, gy, nb, first, last, edge, me_ref, after_ref, part_ref, atoms_ref, one_in, two_in, w_ref, *refs
+):
     group = gx * gy
-    w_ref, refs = refs[0], refs[1:]
+    if first:
+        z_ref, diag_ref, refs = refs[0], refs[1], refs[2:]
     if last:
         blocks, acc = refs[: group // 2], refs[group // 2]
     else:
@@ -390,7 +407,10 @@
         third = product[:, :LANES] + product[:, LANES:]
         for y in range(ny):
             here = pl.ds((y * 8 + x) * SUBS, SUBS)
-            acc[here] = part_ref[here] + atoms_ref[here] + third[y * SUBS : (y + 1) * SUBS]
+            total = part_ref[here] + atoms_ref[here] + third[y * SUBS : (y + 1) * SUBS]
+            if first:
+                total = total + diag_ref[here] * z_ref[here]
+            acc[here] = total
     if not last:
 
         def edges(pair, carry):
@@ -425,45 +445,51 @@
     )
 
 
-def gather_kernel(group, nb, bands, scale, me_ref, *refs):
+def gather_kernel(group, nb, per_chunk, chunk, scale, me_ref, *refs):
     half = group // 2
-    out_ref, gram_ref, field, sem = refs[CHUNKS * (half + 1) :]
+    blocks, refs = refs[: half + 1], refs[half + 1 :]
+    if chunk:
+        earlier, refs = refs[:chunk], refs[chunk + 1 :]
+    out_ref, gram_ref, field, sem = refs[0], refs[1], refs[-2], refs[-1]
     size = nb * 64
-    for chunk in range(CHUNKS):
-        blocks = refs[chunk * (half + 1) : (chunk + 1) * (half + 1)]
-        for slot, source in column_sources(
-            me_ref[0], blocks[:half], blocks[half], size, me_ref[0] % 2
-        ):
-            row = (chunk * group + slot) * size
-            field[pl.ds(pl.multiple_of(row, 64), size)] = source[...]
-    store = pltpu.make_async_copy(field, out_ref, sem.at[0])
+    rows = per_chunk * 64
+    for slot, source in column_sources(
+        me_ref[0], blocks[:half], blocks[half], size, me_ref[0] % 2
+    ):
+        field[pl.ds(pl.multiple_of(slot * size, 64), size)] = source[...]
+    store = pltpu.make_async_copy(field, out_ref.at[pl.ds(chunk * rows, rows)], sem.at[0])
     store.start()
     gram_ref[...] = jnp.zeros_like(gram_ref)
 
     def cells(n, carry):
         total = None
-        turned = [turn(field, g * SUBS * 64 + n * 8) for g in range(bands // SUBS)]
+        turned = [turn(field, g * SUBS * 64 + n * 8) for g in range(per_chunk // SUBS)]
         for m in range(4):
             pieces = []
             for c in range(2):
                 cell = m * 2 + c
                 pieces.append(jnp.concatenate([group_[cell] for group_ in turned], axis=0))
-            value = jnp.concatenate(pieces, axis=1)
-            high, low = halves(value)
-            both = jnp.concatenate([high, low], axis=0)
+            both = jnp.concatenate(halves(jnp.concatenate(pieces, axis=1)), axis=0)
+            if chunk < CHUNKS - 1:
+                refs[2][n * 4 + m] = both
+            against = [earlier[c][n * 4 + m] for c in range(chunk)] if chunk else []
             product = lax.dot_general(
-                both, both, (((1,), (1,)), ((), ())), preferred_element_type=F32
+                jnp.concatenate([*against, both], axis=0),
+                both,
+                (((1,), (1,)), ((), ())),
+                preferred_element_type=F32,
             )
             total = product if total is None else total + product
-        gram_ref[...] += (
-            total[:bands, :bands]
-            + total[bands:, :bands]
-            + total[:bands, bands:]
-            + total[bands:, bands:]
-        )
+        total = total[:, :per_chunk] + total[:, per_chunk:]
+        for c in range(chunk + 1):
+            first = 2 * c * per_chunk
+            gram_ref[c] += (
+                total[first : first + per_chunk]
+                + total[first + per_chunk : first + 2 * per_chunk]
+            )
         return carry
 
-    lax.fori_loop(0, 8, cells, 0)
+    lax.fori_loop(0, 8, cells, 0, unroll=2)
     gram_ref[...] *= scale
     store.wait()
 
@@ -510,6 +536,7 @@
     meta = jnp.broadcast_to(jnp.pad(meta, (0, LANES - 2 * count))[None], (8, LANES))
     part_rows = 64 + 4 * count + 8
     size = nb * 64
+    tables = part_rows - 64
     core = me % 2
 
     def cross(blocks):
@@ -535,32 +562,25 @@
         potential.reshape(64, LANES),
         meta,
     )
-    packed = []
+    rest = field.reshape(CHUNKS, group // 2, 2, size, LANES)
+    passed = lax.dynamic_slice_in_dim(rest, 1 - core, 1, 2).reshape(-1, LANES)
+    passed = swap(passed, 1)
+    other_parts = swap(parts, 1)
     forward = []
+    joined = []
     for chunk in range(CHUNKS):
-        tables = part_rows if chunk == 0 else 0
-        mine = lax.dynamic_slice_in_dim(field, chunk * group * size, group * size, 0)
-        mine = mine.reshape(group // 2, 2, size, LANES)
-        passed = lax.dynamic_slice_in_dim(mine, 1 - core, 1, 1).reshape(group // 2 * size, LANES)
-        passed = swap(passed, 1)
-        if chunk == 0:
-            extra = [parts, swap(parts, 1)]
-            field, passed = lax.optimization_barrier((field, passed))
-        else:
-            extra = packed[0][:1]
-        packed.append(
-            pl.pallas_call(
-                functools.partial(pack_kernel, group, size, chunk, tables),
-                out_shape=[shape(2 * (size + tables), LANES)] * (group // 2),
-                in_specs=[SMEM, HBM, VMEM] + ([ANY] if chunk else [VMEM] * 2),
-                out_specs=[VMEM] * (group // 2),
-                scratch_shapes=[pltpu.SemaphoreType.DMA((1,))],
-                compiler_params=PARAMS,
-                cost_estimate=cost(1),
-                name="pack",
-            )(me_arr, field, passed, *extra)
-        )
-        forward.append(cross(packed[chunk]))
+        extra = (64, tables) if chunk == 0 else (0, 64 if chunk == CHUNKS - 1 else 0)
+        joined = pl.pallas_call(
+            functools.partial(join_kernel, group, size, chunk, extra),
+            out_shape=[shape(2 * size + 2 * extra[1], LANES)] * (group // 2),
+            in_specs=[SMEM, HBM, ANY] + [VMEM] * 3,
+            out_specs=[VMEM] * (group // 2),
+            scratch_shapes=[pltpu.SemaphoreType.DMA((1,))],
+            compiler_params=PARAMS,
+            cost_estimate=cost(1),
+            name="join",
+        )(me_arr, field, forward[0][1] if chunk else parts, passed, parts, other_parts)
+        forward.append(cross(joined))
 
     tile_shape = shape(rows * SUBS, LANES)
     edge_shape = shape(pairs, SUBS, LANES)
@@ -568,7 +588,7 @@
         tiles, one, two = pl.pallas_call(
             functools.partial(unpack_kernel, gx, gy, nb),
             out_shape=[tile_shape, edge_shape, edge_shape],
-            in_specs=[SMEM, ANY] + [VMEM] * (group // 2),
+            in_specs=[SMEM, ANY] + [VMEM] * len(forward[chunk]),
             out_specs=[VMEM] * 3,
             compiler_params=PARAMS,
             cost_estimate=cost(2),
@@ -576,27 +596,35 @@
         )(me_arr, after, *forward[chunk])
         return None, tiles, one, two
 
-    states = [unpack(0, packed[-1][0])]
+    states = [unpack(0, joined[0])]
     root_tiles = group * count * 8 // (2 * fold)
-    diag, roots, places = pl.pallas_call(
-        functools.partial(setup_kernel, gx, gy, nb, count, fold),
+    roots, places = pl.pallas_call(
+        functools.partial(atoms_kernel, gx, gy, nb, count, fold),
         out_shape=[
-            shape(rows * SUBS, LANES),
             shape(root_tiles, SUBS, LANES),
             shape(2 * group * count, dtype=jnp.int32),
         ],
         in_specs=[SMEM, ANY] + [VMEM] * (group // 2),
-        out_specs=[VMEM, VMEM, SMEM],
+        out_specs=[VMEM, SMEM],
         scratch_shapes=[
             pltpu.SMEM((group * 8, LANES), F32),
             pltpu.SemaphoreType.DMA((1,)),
         ],
         compiler_params=PARAMS,
-        cost_estimate=cost(2),
-        name="setup",
+        cost_estimate=cost(1),
+        name="atoms",
     )(me_arr, states[0][2], *forward[0])
     for chunk in range(1, CHUNKS):
         states.append(unpack(chunk, roots))
+    diag = pl.pallas_call(
+        functools.partial(diagonal_kernel, gx, gy, nb),
+        out_shape=tile_shape,
+        in_specs=[SMEM, ANY] + [VMEM] * (group // 2),
+        out_specs=VMEM,
+        compiler_params=PARAMS,
+        cost_estimate=cost(1),
+        name="diagonal",
+    )(me_arr, states[-1][2], *forward[-1])
 
     own_weights, halo_weights = (jnp.asarray(w) for w in line_weights())
     summing = np.kron(np.eye(2 * fold), np.ones((TILE // fold, TILE // fold)))
@@ -607,48 +635,53 @@
     results = [None] * CHUNKS
     for degree_step in range(DEGREE):
         first, last = degree_step == 0, degree_step == DEGREE - 1
-        outs = None
-        if not first:
-            joint_one = jnp.concatenate([state[2] for state in states], axis=0)
-            joint_two = jnp.concatenate([state[3] for state in states], axis=0)
-            joint_one = lax.ppermute(joint_one, "gz", pair_one)
-            joint_two = lax.ppermute(joint_two, "gz", pair_two)
-        for chunk in range(CHUNKS):
-            prev, tiles, one, two = states[chunk]
+        if first:
+            halos = [
+                (lax.ppermute(state[2], "gz", pair_one), lax.ppermute(state[3], "gz", pair_two))
+                for state in states
+            ]
+        else:
+            one = jnp.concatenate([state[2] for state in states], axis=0)
+            two = jnp.concatenate([state[3] for state in states], axis=0)
+            halos = [(lax.ppermute(one, "gz", pair_one), lax.ppermute(two, "gz", pair_two))] * CHUNKS
+        inner = []
+        for prev, tiles, _, _ in states:
+            operands = [roots, places, tiles]
+            if not first:
+                operands += [prev, diag]
+            operands += [roots, own_weights, summing]
+            inner.append(
+                pl.pallas_call(
+                    functools.partial(inner_kernel, gx, gy, nb, count, fold, first),
+                    out_shape=[tile_shape, tile_shape],
+                    in_specs=[ANY, SMEM] + [VMEM] * (len(operands) - 2),
+                    out_specs=[VMEM] * 2,
+                    scratch_shapes=[pltpu.VMEM((rows * SUBS, LANES), F32)]
+                    + [pltpu.VMEM((root_tiles // 8, SUBS, LANES), F32)] * 2,
+                    compiler_params=PARAMS,
+                    cost_estimate=cost(4),
+                    name="inner",
+                )(*operands)
+            )
+        for chunk, (_, tiles, _, _) in enumerate(states):
             edge = 0 if first else chunk * pairs
+            after = roots if first else inner[chunk - 1][0]
+            operands = [me_arr, after, *inner[chunk], *halos[chunk]]
+            operands.append(halo_weights)
             if first:
-                one = lax.ppermute(one, "gz", pair_one)
-                two = lax.ppermute(two, "gz", pair_two)
-            else:
-                one, two = joint_one, joint_two
-            after = roots if outs is None or not last else outs[0]
-            operands = [after, places, tiles]
-            if not first:
-                operands.append(prev)
-            operands += [diag, roots, own_weights, summing]
-            part, atoms = pl.pallas_call(
-                functools.partial(inner_kernel, gx, gy, nb, count, fold, first),
-                out_shape=[tile_shape, tile_shape],
-                in_specs=[ANY, SMEM] + [VMEM] * (len(operands) - 2),
-                out_specs=[VMEM] * 2,
-                scratch_shapes=[pltpu.VMEM((rows * SUBS, LANES), F32)]
-                + [pltpu.VMEM((root_tiles // 8, SUBS, LANES), F32)] * 2,
-                compiler_params=PARAMS,
-                cost_estimate=cost(4),
-                name="inner",
-            )(*operands)
+                operands += [tiles, diag]
             outs = pl.pallas_call(
                 functools.partial(outer_kernel, gx, gy, nb, first, last, edge),
                 out_shape=[shape(2 * size, LANES)] * (group // 2)
                 if last
                 else [tile_shape, edge_shape, edge_shape],
-                in_specs=[SMEM] + [VMEM] * 5,
+                in_specs=[SMEM, ANY] + [VMEM] * (len(operands) - 2),
                 out_specs=[VMEM] * (group // 2 if last else 3),
                 scratch_shapes=[pltpu.VMEM((rows * SUBS, LANES), F32)] * last,
                 compiler_params=PARAMS,
                 cost_estimate=cost(1),
                 name="outer",
-            )(me_arr, part, atoms, one, two, halo_weights)
+            )(*operands)
             if last:
                 crossed = cross(outs)
                 results[chunk] = crossed + [beside(crossed)]
@@ -656,19 +689,40 @@
                 states[chunk] = (tiles, *outs)
 
     total_cells = size_x * size_y * size_z * group * gz
-    filtered, gram = pl.pallas_call(
-        functools.partial(gather_kernel, group, nb, bands, 1.0 / total_cells),
-        out_shape=[shape(bands * 64, LANES), shape(bands, bands)],
-        in_specs=[SMEM] + [VMEM] * (CHUNKS * (group // 2 + 1)),
-        out_specs=[ANY, VMEM],
-        scratch_shapes=[
-            pltpu.VMEM((bands * 64, LANES), F32),
-            pltpu.SemaphoreType.DMA((1,)),
+    per_chunk = bands // CHUNKS
+    filtered, kept, gram_columns = None, [], []
+    for chunk, blocks in enumerate(results):
+        operands = [me_arr, *blocks, *kept] + ([filtered] if chunk else [])
+        filtered, columns, *own = pl.pallas_call(
+            functools.partial(gather_kernel, group, nb, per_chunk, chunk, 1.0 / total_cells),
+            out_shape=[
+                shape(bands * 64, LANES),
+                shape(chunk + 1, per_chunk, per_chunk),
+            ]
+            + [shape(32, 2 * per_chunk, 2 * LANES, dtype=BF16)] * (chunk < CHUNKS - 1),
+            in_specs=[SMEM] + [VMEM] * (len(operands) - 1 - (chunk > 0)) + [ANY] * (chunk > 0),
+            out_specs=[ANY, VMEM] + [VMEM] * (chunk < CHUNKS - 1),
+            scratch_shapes=[
+                pltpu.VMEM((per_chunk * 64, LANES), F32),
+                pltpu.SemaphoreType.DMA((1,)),
+            ],
+            input_output_aliases={len(operands) - 1: 0} if chunk else {},
+            compiler_params=PARAMS,
+            cost_estimate=cost(2),
+            name="gather",
+        )(*operands)
+        kept += own
+        gram_columns.append(columns)
+    gram = jnp.concatenate(
+        [
+            jnp.concatenate(
+                [gram_columns[d][c] if c <= d else gram_columns[c][d].T for d in range(CHUNKS)],
+                axis=1,
+            )
+            for c in range(CHUNKS)
         ],
-        compiler_params=PARAMS,
-        cost_estimate=cost(5),
-        name="gather",
-    )(me_arr, *[block for chunk in results for block in chunk])
+        axis=0,
+    )
 
     gram = gram + swap(gram, 1)
     d = 2

time: 144 us -> 142 us (0.986)
  waiting for transfers between devices: 42.7 us -> 34.7 us
  Pallas kernels: 57.1 us -> 60.6 us
    ppermute x10, waiting for transfers between devices: 8.43 us -> 2.46 us  [the longest x3 1.77 us: shards(): lax.ppermute(two, 'gz', pair_two)]
    ppermute x10, starting transfers between devices: 11.7 us -> 15.1 us  [the longest x3 5.45 us: shards(): lax.ppermute(two, 'gz', pair_two)]
    pallas_call x4 -> x6, Pallas kernels: 8.64 us -> 11.6 us  [the longest x2 4.2 us: shards(): pl.pallas_call(functools.partial(gather_kernel, group, nb, per_chunk, chu...]
    ppermute x21 -> x20, waiting for transfers between devices: 30.9 us -> 28.1 us  [swap(): return lax.ppermute(block, column, [(s, s ^ d) for s in range(group)])]
    ppermute x21 -> x20, starting transfers between devices: 22.9 us -> 20.7 us  [swap(): return lax.ppermute(block, column, [(s, s ^ d) for s in range(group)])]
    unnamed x19 -> x27, local copies, waits for them, and re-layouts: 0.11 us -> 1.65 us
    dynamic_slice x5 -> x1, local copies, waits for them, and re-layouts: 2.93 us -> 2.28 us  [shards(): passed = lax.dynamic_slice_in_dim(rest, 1 - core, 1, 2).reshape(-1, LANES)]
  transfers between devices with their start and end apart: 34 -> 33, of which waited for: 22 -> 17; matrix products, arithmetic and copies ran while one was open for 0% -> 0% of each run, Pallas kernels for 23% -> 32%
where the time goes in v4:
time: 142 us
  Pallas kernels  60.6 us (43%)
  starting transfers between devices  40.3 us (28%)
  waiting for transfers between devices  34.7 us (24%)
  local copies, waits for them, and re-layouts  4.12 us (3%)
    pallas_call x8, Pallas kernels, shards(): pl.pallas_call(functools.partial(inner_kernel, gx, gy, nb, count, fold, f...  31.2 us
    ppermute x20, waiting for transfers between devices, swap(): return lax.ppermute(block, column, [(s, s ^ d) for s in range(group)])  28.1 us
    ppermute x20, starting transfers between devices, swap(): return lax.ppermute(block, column, [(s, s ^ d) for s in range(group)])  20.7 us
    pallas_call x8, Pallas kernels, shards(): pl.pallas_call(functools.partial(outer_kernel, gx, gy, nb, first, last, e...  13.5 us
    ppermute x3, starting transfers between devices, shards(): lax.ppermute(two, 'gz', pair_two)  5.45 us
    ppermute x2, starting transfers between devices, shards(): lax.ppermute(state[3], 'gz', pair_two)  4.95 us
    ppermute x3, starting transfers between devices, swap_z(): return lax.ppermute(block, 'gz', [(s, s ^ d) for s in range(gz)])  4.45 us
    pallas_call x2, Pallas kernels, shards(): pl.pallas_call(functools.partial(gather_kernel, group, nb, per_chunk, chu...  4.2 us
  transfers between devices with their start and end apart: 33, of which 17 were waited for; matrix products, arithmetic and copies ran while one was open for 0% of the time, Pallas kernels for 32%

profile of v4, /device:TPU:0, one launch (start us, length us, event | category | flops | bytes accessed | tf_op | source)
XLA Modules:
  0.0 142.1 jit_solution(1669578349587960370)
XLA Ops:
  0.7 2.3 %constant_dynamic-slice_fusion.11 = f32[2,4,1,256,128]{4,3,2,1,0:T(8,128)} fusion(f32[2,4,2,256,128]{4,3,2,1,0:T(8,128)} %bitcast.26, s32[]{:T(128)S(6)} %select_n.38), kind=kLoop, calls=%fused_computation.26 | loop fusion | bytes 2097156 | tf_op jit(solution)/shard_map/dynamic_slice | solution.py:566
  5.9 2.2 %join.2 = (f32[592,128]{1,0:T(8,128)S(1)}, f32[592,128]{1,0:T(8,128)}, f32[592,128]{1,0:T(8,128)}, f32[592,128]{1,0:T(8,128)}) custom-call(s32[2]{0:T(128)S(1)} %pad_add_fusion.me_ref, f32[4096,128]{1,0:T(8,128)S(1)} %bitcast.27, f32[104,128]{1,0:T(8,128)S(1)} %parts.1.after_ref.own_ref, f32[2048,128]{1,0:T(8,128)S(1)} %collective-permute-done.passed, ...), custom_call_target="tpu_custom_call" | custom-call | flops 1000000000 | bytes 3000000 | tf_op jit(solution)/shard_map/join/pallas_call | solution.py:573
  8.9 2.9 %collective-permute-start.2 = (f32[592,128]{1,0:T(8,128)}, f32[592,128]{1,0:T(8,128)S(1)}, u32[]{:S(2)}, u32[]{:S(2)}) collective-permute-start(f32[592,128]{1,0:T(8,128)} %get-tuple-element.65), channel_id=1, source_target_pairs={{0,8},{4,12},{8,0},{12,4},{16,24},{20,28},{24,16},{28,20},{1,9},{5... | collective-permute-start | bytes 909320 | tf_op jit(solution)/shard_map/ppermute | solution.py:522
  13.3 6.2 %collective-permute-done.2.after_ref.refs_1_ = f32[592,128]{1,0:T(8,128)S(1)} collective-permute-done((f32[592,128]{1,0:T(8,128)}, f32[592,128]{1,0:T(8,128)S(1)}, u32[]{:S(2)}, u32[]{:S(2)}) %collective-permute-start.2) | collective-permute-done | bytes 303136 | tf_op jit(solution)/shard_map/ppermute | solution.py:522
  25.1 3.0 %collective-permute-done.4.refs_3_ = f32[592,128]{1,0:T(8,128)} collective-permute-done((f32[592,128]{1,0:T(8,128)}, f32[592,128]{1,0:T(8,128)}, u32[]{:S(2)}, u32[]{:S(2)}) %collective-permute-start.4) | collective-permute-done | bytes 303136 | tf_op jit(solution)/shard_map/ppermute | solution.py:522
  28.1 2.1 %unpack.2 = (f32[2048,128]{1,0:T(8,128)S(1)}, f32[16,8,128]{2,1,0:T(8,128)S(1)}, f32[16,8,128]{2,1,0:T(8,128)S(1)}) custom-call(s32[2]{0:T(128)S(1)} %pad_add_fusion.me_ref, f32[640,128]{1,0:T(8,128)S(1)} %get-tuple-element.66.after_ref.refs_0_, f32[592,128]{1,0:T(8,128)S(1)} %copy-done.10, f32[592,128]{1,0:T(8,128)S(1)} %collective-permute-done.2.after_ref.refs_1_, ...), custom_call_target="tpu_custom_call" | custom-call | flops 2000000000 | bytes 6000000 | tf_op jit(solution)/shard_map/unpack/pallas_call | solution.py:588
  30.2 2.2 %collective-permute-start.5 = (f32[16,8,128]{2,1,0:T(8,128)S(1)}, f32[16,8,128]{2,1,0:T(8,128)S(1)}, u32[]{:S(2)}, u32[]{:S(2)}) collective-permute-start(f32[16,8,128]{2,1,0:T(8,128)S(1)} %get-tuple-element.70.after_ref), channel_id=1, source_target_pairs={{0,1},{1,0},{2,3},{3,2},{4,5},{5,4},{6,7},{7,6},{8,9},{9,8},{10,11... | collective-permute-start | bytes 196616 | tf_op jit(solution)/shard_map/ppermute | solution.py:640
  32.4 2.5 %collective-permute-start.6 = (f32[16,8,128]{2,1,0:T(8,128)S(1)}, f32[16,8,128]{2,1,0:T(8,128)S(1)}, u32[]{:S(2)}, u32[]{:S(2)}) collective-permute-start(f32[16,8,128]{2,1,0:T(8,128)S(1)} %get-tuple-element.76), channel_id=1, source_target_pairs={{0,3},{1,2},{2,1},{3,0},{4,7},{5,6},{6,5},{7,4},{8,11},{9,10},{10,... | collective-permute-start | bytes 196616 | tf_op jit(solution)/shard_map/ppermute | solution.py:640
  34.9 3.2 %atoms.1 = (f32[128,8,128]{2,1,0:T(8,128)S(1)}, s32[128]{0:T(128)S(1)}) custom-call(s32[2]{0:T(128)S(1)} %pad_add_fusion.me_ref, f32[16,8,128]{2,1,0:T(8,128)S(1)} %get-tuple-element.70.after_ref, f32[592,128]{1,0:T(8,128)S(1)} %copy-done.10, f32[592,128]{1,0:T(8,128)S(1)} %collective-permute-done.2.after_ref.refs_1_, ...), custom_call_target="tpu_custom_call" | custom-call | flops 1000000000 | bytes 3000000 | tf_op jit(solution)/shard_map/atoms/pallas_call | solution.py:601
  38.1 3.8 %inner.8 = (f32[2048,128]{1,0:T(8,128)S(1)}, f32[2048,128]{1,0:T(8,128)S(1)}) custom-call(f32[128,8,128]{2,1,0:T(8,128)S(1)} %get-tuple-element.71.after_ref.refs_1_.refs_3_, s32[128]{0:T(128)S(1)} %get-tuple-element.72.meta_ref, f32[2048,128]{1,0:T(8,128)S(1)} %get-tuple-element.73.refs_0_.refs_1_, ...), custom_call_target="tpu_custom_call" | custom-call | flops 4000000000 | bytes 12000000 | tf_op jit(solution)/shard_map/inner/pallas_call | solution.py:654
  43.4 3.8 %inner.10 = (f32[2048,128]{1,0:T(8,128)S(1)}, f32[2048,128]{1,0:T(8,128)S(1)}) custom-call(f32[128,8,128]{2,1,0:T(8,128)S(1)} %get-tuple-element.71.after_ref.refs_1_.refs_3_, s32[128]{0:T(128)S(1)} %get-tuple-element.72.meta_ref, f32[2048,128]{1,0:T(8,128)S(1)} %get-tuple-element.83.refs_0_.refs_1_, ...), custom_call_target="tpu_custom_call" | custom-call | flops 4000000000 | bytes 12000000 | tf_op jit(solution)/shard_map/inner/pallas_call | solution.py:654
  48.4 2.5 %collective-permute-start.11 = (f32[16,8,128]{2,1,0:T(8,128)S(1)}, f32[16,8,128]{2,1,0:T(8,128)S(1)}, u32[]{:S(2)}, u32[]{:S(2)}) collective-permute-start(f32[16,8,128]{2,1,0:T(8,128)S(1)} %get-tuple-element.86), channel_id=1, source_target_pairs={{0,3},{1,2},{2,1},{3,0},{4,7},{5,6},{6,5},{7,4},{8,11},{9,10},{10,... | collective-permute-start | bytes 196616 | tf_op jit(solution)/shard_map/ppermute | solution.py:640
  51.7 1.9 %outer.8 = (f32[2048,128]{1,0:T(8,128)S(1)}, f32[16,8,128]{2,1,0:T(8,128)S(1)}, f32[16,8,128]{2,1,0:T(8,128)S(1)}) custom-call(s32[2]{0:T(128)S(1)} %pad_add_fusion.me_ref, f32[128,8,128]{2,1,0:T(8,128)S(1)} %get-tuple-element.71.after_ref.refs_1_.refs_3_, f32[2048,128]{1,0:T(8,128)S(1)} %get-tuple-element.74.part_ref, ...), custom_call_target="tpu_custom_call" | custom-call | flops 1000000000 | bytes 3000000 | tf_op jit(solution)/shard_map/outer/pallas_call | solution.py:673
  53.6 3.9 %inner.9 = (f32[2048,128]{1,0:T(8,128)S(1)}, f32[2048,128]{1,0:T(8,128)S(1)}) custom-call(f32[128,8,128]{2,1,0:T(8,128)S(1)} %get-tuple-element.71.after_ref.refs_1_.refs_3_, s32[128]{0:T(128)S(1)} %get-tuple-element.72.meta_ref, f32[2048,128]{1,0:T(8,128)S(1)} %get-tuple-element.81.refs_0_.refs_1_, f32[2048,128]{1,0:T(8,128)S(1)} %get-tuple-element.73.refs_0_.refs_1_, ...), custom_call_target="tpu_custom_call" | custom-call | flops 4000000000 | bytes 12000000 | tf_op jit(solution)/shard_map/inner/pallas_call | solution.py:654
  57.5 1.9 %outer.9 = (f32[2048,128]{1,0:T(8,128)S(1)}, f32[16,8,128]{2,1,0:T(8,128)S(1)}, f32[16,8,128]{2,1,0:T(8,128)S(1)}) custom-call(s32[2]{0:T(128)S(1)} %pad_add_fusion.me_ref, f32[128,8,128]{2,1,0:T(8,128)S(1)} %get-tuple-element.71.after_ref.refs_1_.refs_3_, f32[2048,128]{1,0:T(8,128)S(1)} %get-tuple-element.84.part_ref, ...), custom_call_target="tpu_custom_call" | custom-call | flops 1000000000 | bytes 3000000 | tf_op jit(solution)/shard_map/outer/pallas_call | solution.py:673
  61.0 3.9 %inner.11 = (f32[2048,128]{1,0:T(8,128)S(1)}, f32[2048,128]{1,0:T(8,128)S(1)}) custom-call(f32[128,8,128]{2,1,0:T(8,128)S(1)} %get-tuple-element.71.after_ref.refs_1_.refs_3_, s32[128]{0:T(128)S(1)} %get-tuple-element.72.meta_ref, f32[2048,128]{1,0:T(8,128)S(1)} %get-tuple-element.87.refs_0_.refs_1_, f32[2048,128]{1,0:T(8,128)S(1)} %get-tuple-element.83.refs_0_.refs_1_, ...), custom_call_target="tpu_custom_call" | custom-call | flops 4000000000 | bytes 12000000 | tf_op jit(solution)/shard_map/inner/pallas_call | solution.py:654
  71.0 2.1 %collective-permute-start.15 = (f32[32,8,128]{2,1,0:T(8,128)S(1)}, f32[32,8,128]{2,1,0:T(8,128)S(1)}, u32[]{:S(2)}, u32[]{:S(2)}) collective-permute-start(f32[32,8,128]{2,1,0:T(8,128)S(1)} %pad_maximum_fusion.5), channel_id=1, source_target_pairs={{0,3},{1,2},{2,1},{3,0},{4,7},{5,6},{6,5},{7,4},{8,11},{9,10},{10,... | collective-permute-start | bytes 393224 | tf_op jit(solution)/shard_map/ppermute | solution.py:646
  73.2 3.9 %inner.13 = (f32[2048,128]{1,0:T(8,128)S(1)}, f32[2048,128]{1,0:T(8,128)S(1)}) custom-call(f32[128,8,128]{2,1,0:T(8,128)S(1)} %get-tuple-element.71.after_ref.refs_1_.refs_3_, s32[128]{0:T(128)S(1)} %get-tuple-element.72.meta_ref, f32[2048,128]{1,0:T(8,128)S(1)} %get-tuple-element.97.refs_0_.refs_1_, f32[2048,128]{1,0:T(8,128)S(1)} %get-tuple-element.81.refs_0_.refs_1_, ...), custom_call_target="tpu_custom_call" | custom-call | flops 4000000000 | bytes 12000000 | tf_op jit(solution)/shard_map/inner/pallas_call | solution.py:654
  77.1 3.9 %inner.12 = (f32[2048,128]{1,0:T(8,128)S(1)}, f32[2048,128]{1,0:T(8,128)S(1)}) custom-call(f32[128,8,128]{2,1,0:T(8,128)S(1)} %get-tuple-element.71.after_ref.refs_1_.refs_3_, s32[128]{0:T(128)S(1)} %get-tuple-element.72.meta_ref, f32[2048,128]{1,0:T(8,128)S(1)} %get-tuple-element.94.refs_0_.refs_1_, f32[2048,128]{1,0:T(8,128)S(1)} %get-tuple-element.87.refs_0_.refs_1_, ...), custom_call_target="tpu_custom_call" | custom-call | flops 4000000000 | bytes 12000000 | tf_op jit(solution)/shard_map/inner/pallas_call | solution.py:654
  84.7 2.0 %collective-permute-start.17 = (f32[32,8,128]{2,1,0:T(8,128)S(1)}, f32[32,8,128]{2,1,0:T(8,128)S(1)}, u32[]{:S(2)}, u32[]{:S(2)}) collective-permute-start(f32[32,8,128]{2,1,0:T(8,128)S(1)} %pad_maximum_fusion.7), channel_id=1, source_target_pairs={{0,3},{1,2},{2,1},{3,0},{4,7},{5,6},{6,5},{7,4},{8,11},{9,10},{10,... | collective-permute-start | bytes 393224 | tf_op jit(solution)/shard_map/ppermute | solution.py:646
  87.8 4.1 %inner.15 = (f32[2048,128]{1,0:T(8,128)S(1)}, f32[2048,128]{1,0:T(8,128)S(1)}) custom-call(f32[128,8,128]{2,1,0:T(8,128)S(1)} %get-tuple-element.71.after_ref.refs_1_.refs_3_, s32[128]{0:T(128)S(1)} %get-tuple-element.72.meta_ref, f32[2048,128]{1,0:T(8,128)S(1)} %get-tuple-element.107.refs_0_, f32[2048,128]{1,0:T(8,128)S(1)} %get-tuple-element.94.refs_0_.refs_1_, ...), custom_call_target="tpu_custom_call" | custom-call | flops 4000000000 | bytes 12000000 | tf_op jit(solution)/shard_map/inner/pallas_call | solution.py:654
  91.9 3.9 %inner.14 = (f32[2048,128]{1,0:T(8,128)S(1)}, f32[2048,128]{1,0:T(8,128)S(1)}) custom-call(f32[128,8,128]{2,1,0:T(8,128)S(1)} %get-tuple-element.71.after_ref.refs_1_.refs_3_, s32[128]{0:T(128)S(1)} %get-tuple-element.72.meta_ref, f32[2048,128]{1,0:T(8,128)S(1)} %get-tuple-element.104.refs_0_, f32[2048,128]{1,0:T(8,128)S(1)} %get-tuple-element.97.refs_0_.refs_1_, ...), custom_call_target="tpu_custom_call" | custom-call | flops 4000000000 | bytes 12000000 | tf_op jit(solution)/shard_map/inner/pallas_call | solution.py:654
  97.1 2.5 %collective-permute-start.24 = (f32[512,128]{1,0:T(8,128)S(1)}, f32[512,128]{1,0:T(8,128)S(1)}, u32[]{:S(2)}, u32[]{:S(2)}) collective-permute-start(f32[512,128]{1,0:T(8,128)S(1)} %get-tuple-element.122), channel_id=1, source_target_pairs={{0,24},{4,28},{8,16},{12,20},{16,8},{20,12},{24,0},{28,4},{1,25},{... | collective-permute-start | bytes 786440 | tf_op jit(solution)/shard_map/ppermute | solution.py:522
  101.9 2.5 %collective-permute-start.20 = (f32[512,128]{1,0:T(8,128)S(1)}, f32[512,128]{1,0:T(8,128)S(1)}, u32[]{:S(2)}, u32[]{:S(2)}) collective-permute-start(f32[512,128]{1,0:T(8,128)S(1)} %get-tuple-element.117), channel_id=1, source_target_pairs={{0,24},{4,28},{8,16},{12,20},{16,8},{20,12},{24,0},{28,4},{1,25},{... | collective-permute-start | bytes 786440 | tf_op jit(solution)/shard_map/ppermute | solution.py:522
  105.0 2.4 %collective-permute-done.24.refs_3_ = f32[512,128]{1,0:T(8,128)S(1)} collective-permute-done((f32[512,128]{1,0:T(8,128)S(1)}, f32[512,128]{1,0:T(8,128)S(1)}, u32[]{:S(2)}, u32[]{:S(2)}) %collective-permute-start.24) | collective-permute-done | bytes 262176 | tf_op jit(solution)/shard_map/ppermute | solution.py:522
  108.9 4.1 %collective-permute-done.23.refs_2_ = f32[512,128]{1,0:T(8,128)S(1)} collective-permute-done((f32[512,128]{1,0:T(8,128)S(1)}, f32[512,128]{1,0:T(8,128)S(1)}, u32[]{:S(2)}, u32[]{:S(2)}) %collective-permute-start.23) | collective-permute-done | bytes 262176 | tf_op jit(solution)/shard_map/ppermute | solution.py:522
  113.9 2.4 %collective-permute-done.20.refs_3_ = f32[512,128]{1,0:T(8,128)S(1)} collective-permute-done((f32[512,128]{1,0:T(8,128)S(1)}, f32[512,128]{1,0:T(8,128)S(1)}, u32[]{:S(2)}, u32[]{:S(2)}) %collective-permute-start.20) | collective-permute-done | bytes 262176 | tf_op jit(solution)/shard_map/ppermute | solution.py:522
  116.3 2.8 %collective-permute-done.19.refs_2_ = f32[512,128]{1,0:T(8,128)S(1)} collective-permute-done((f32[512,128]{1,0:T(8,128)S(1)}, f32[512,128]{1,0:T(8,128)S(1)}, u32[]{:S(2)}, u32[]{:S(2)}) %collective-permute-start.19) | collective-permute-done | bytes 262176 | tf_op jit(solution)/shard_map/ppermute | solution.py:522
  119.4 2.0 %gather.2 = (f32[4096,128]{1,0:T(8,128)}, f32[1,32,32]{2,1,0:T(8,128)S(1)}, bf16[32,64,256]{2,1,0:T(8,128)(2,1)S(1)}) custom-call(s32[2]{0:T(128)S(1)} %pad_add_fusion.me_ref, f32[512,128]{1,0:T(8,128)S(1)} %get-tuple-element.119.refs_0_, f32[512,128]{1,0:T(8,128)S(1)} %collective-permute-done.22.refs_1_, f32[512,128]{1,0:T(8,128)S(1)} %collective-permute-done.23.refs_2_, ...), custom_call_target="tpu_custom_call" | custom-call | flops 2000000000 | bytes 6000000 | tf_op jit(solution)/shard_map/gather/pallas_call | solution.py:696
  121.3 2.2 %gather.3 = (f32[4096,128]{1,0:T(8,128)}, f32[2,32,32]{2,1,0:T(8,128)S(1)}) custom-call(s32[2]{0:T(128)S(1)} %pad_add_fusion.me_ref, f32[512,128]{1,0:T(8,128)S(1)} %get-tuple-element.114.refs_0_, f32[512,128]{1,0:T(8,128)S(1)} %collective-permute-done.18.refs_1_, f32[512,128]{1,0:T(8,128)S(1)} %collective-permute-done.19.refs_2_, ...), custom_call_target="tpu_custom_call", output_to_operand_aliasing={{0}: (7, {})} | custom-call | flops 2000000000 | bytes 6000000 | tf_op jit(solution)/shard_map/gather/pallas_call | solution.py:696
  130.4 2.4 %collective-permute-done.29 = f32[64,64]{1,0:T(8,128)S(1)} collective-permute-done((f32[64,64]{1,0:T(8,128)S(1)}, f32[64,64]{1,0:T(8,128)S(1)}, u32[]{:S(2)}, u32[]{:S(2)}) %collective-permute-start.29) | collective-permute-done | bytes 16416 | tf_op jit(solution)/shard_map/ppermute | solution.py:522
  138.7 2.8 %collective-permute-done.32 = f32[16,64]{1,0:T(8,128)S(1)} collective-permute-done((f32[16,64]{1,0:T(8,128)S(1)}, f32[16,64]{1,0:T(8,128)S(1)}, u32[]{:S(2)}, u32[]{:S(2)}) %collective-permute-start.32) | collective-permute-done | bytes 4128 | tf_op jit(solution)/shard_map/ppermute | solution.py:525
  (118 shorter events, 46.8 us)
Async XLA Ops:
  3.0 3.0 %collective-permute-start = (f32[2048,128]{1,0:T(8,128)}, f32[2048,128]{1,0:T(8,128)S(1)}, u32[]{:S(2)}, u32[]{:S(2)}) collective-permute-start(f32[2048,128]{1,0:T(8,128)} %bitcast.11), channel_id=1, source_target_pairs={{0,4},{4,0},{8,12},{12,8},{16,20},{20,16},{24,28},{28,24},{1,5},{5... | collective-permute-start | bytes 3145736 | tf_op jit(solution)/shard_map/ppermute | solution.py:522
  4.4 1.4 collective-permute-start.1
  8.9 10.6 %collective-permute-start.2 = (f32[592,128]{1,0:T(8,128)}, f32[592,128]{1,0:T(8,128)S(1)}, u32[]{:S(2)}, u32[]{:S(2)}) collective-permute-start(f32[592,128]{1,0:T(8,128)} %get-tuple-element.65), channel_id=1, source_target_pairs={{0,8},{4,12},{8,0},{12,4},{16,24},{20,28},{24,16},{28,20},{1,9},{5... | collective-permute-start | bytes 909320 | tf_op jit(solution)/shard_map/ppermute | solution.py:522
  11.8 13.4 %collective-permute-start.3 = (f32[592,128]{1,0:T(8,128)}, f32[592,128]{1,0:T(8,128)}, u32[]{:S(2)}, u32[]{:S(2)}) collective-permute-start(f32[592,128]{1,0:T(8,128)} %get-tuple-element.68), channel_id=1, source_target_pairs={{0,16},{4,20},{8,24},{12,28},{16,0},{20,4},{24,8},{28,12},{1,17},{... | collective-permute-start | bytes 909320 | tf_op jit(solution)/shard_map/ppermute | solution.py:522
  13.3 14.8 %collective-permute-start.4 = (f32[592,128]{1,0:T(8,128)}, f32[592,128]{1,0:T(8,128)}, u32[]{:S(2)}, u32[]{:S(2)}) collective-permute-start(f32[592,128]{1,0:T(8,128)} %get-tuple-element.69), channel_id=1, source_target_pairs={{0,24},{4,28},{8,16},{12,20},{16,8},{20,12},{24,0},{28,4},{1,25},{... | collective-permute-start | bytes 909320 | tf_op jit(solution)/shard_map/ppermute | solution.py:522
  21.6 20.3 %collective-permute-start.7 = (f32[640,128]{1,0:T(8,128)S(1)}, f32[640,128]{1,0:T(8,128)S(1)}, u32[]{:S(2)}, u32[]{:S(2)}) collective-permute-start(f32[640,128]{1,0:T(8,128)S(1)} %get-tuple-element.77), channel_id=1, source_target_pairs={{0,8},{4,12},{8,0},{12,4},{16,24},{20,28},{24,16},{28,20},{1,9},{5... | collective-permute-start | bytes 983048 | tf_op jit(solution)/shard_map/ppermute | solution.py:522
  23.4 18.5 %collective-permute-start.8 = (f32[640,128]{1,0:T(8,128)S(1)}, f32[640,128]{1,0:T(8,128)S(1)}, u32[]{:S(2)}, u32[]{:S(2)}) collective-permute-start(f32[640,128]{1,0:T(8,128)S(1)} %get-tuple-element.78), channel_id=1, source_target_pairs={{0,16},{4,20},{8,24},{12,28},{16,0},{20,4},{24,8},{28,12},{1,17},{... | collective-permute-start | bytes 983048 | tf_op jit(solution)/shard_map/ppermute | solution.py:522
  24.9 17.0 %collective-permute-start.9 = (f32[640,128]{1,0:T(8,128)S(1)}, f32[640,128]{1,0:T(8,128)S(1)}, u32[]{:S(2)}, u32[]{:S(2)}) collective-permute-start(f32[640,128]{1,0:T(8,128)S(1)} %get-tuple-element.79), channel_id=1, source_target_pairs={{0,24},{4,28},{8,16},{12,20},{16,8},{20,12},{24,0},{28,4},{1,25},{... | collective-permute-start | bytes 983048 | tf_op jit(solution)/shard_map/ppermute | solution.py:522
  30.2 21.5 %collective-permute-start.5 = (f32[16,8,128]{2,1,0:T(8,128)S(1)}, f32[16,8,128]{2,1,0:T(8,128)S(1)}, u32[]{:S(2)}, u32[]{:S(2)}) collective-permute-start(f32[16,8,128]{2,1,0:T(8,128)S(1)} %get-tuple-element.70.after_ref), channel_id=1, source_target_pairs={{0,1},{1,0},{2,3},{3,2},{4,5},{5,4},{6,7},{7,6},{8,9},{9,8},{10,11... | collective-permute-start | bytes 196616 | tf_op jit(solution)/shard_map/ppermute | solution.py:640
  32.4 19.3 %collective-permute-start.6 = (f32[16,8,128]{2,1,0:T(8,128)S(1)}, f32[16,8,128]{2,1,0:T(8,128)S(1)}, u32[]{:S(2)}, u32[]{:S(2)}) collective-permute-start(f32[16,8,128]{2,1,0:T(8,128)S(1)} %get-tuple-element.76), channel_id=1, source_target_pairs={{0,3},{1,2},{2,1},{3,0},{4,7},{5,6},{6,5},{7,4},{8,11},{9,10},{10,... | collective-permute-start | bytes 196616 | tf_op jit(solution)/shard_map/ppermute | solution.py:640
  47.2 10.3 %collective-permute-start.10 = (f32[16,8,128]{2,1,0:T(8,128)S(1)}, f32[16,8,128]{2,1,0:T(8,128)S(1)}, u32[]{:S(2)}, u32[]{:S(2)}) collective-permute-start(f32[16,8,128]{2,1,0:T(8,128)S(1)} %get-tuple-element.80.after_ref), channel_id=1, source_target_pairs={{0,1},{1,0},{2,3},{3,2},{4,5},{5,4},{6,7},{7,6},{8,9},{9,8},{10,11... | collective-permute-start | bytes 196616 | tf_op jit(solution)/shard_map/ppermute | solution.py:640
  48.4 9.1 %collective-permute-start.11 = (f32[16,8,128]{2,1,0:T(8,128)S(1)}, f32[16,8,128]{2,1,0:T(8,128)S(1)}, u32[]{:S(2)}, u32[]{:S(2)}) collective-permute-start(f32[16,8,128]{2,1,0:T(8,128)S(1)} %get-tuple-element.86), channel_id=1, source_target_pairs={{0,3},{1,2},{2,1},{3,0},{4,7},{5,6},{6,5},{7,4},{8,11},{9,10},{10,... | collective-permute-start | bytes 196616 | tf_op jit(solution)/shard_map/ppermute | solution.py:640
  59.4 7.2 %collective-permute-start.13 = (f32[32,8,128]{2,1,0:T(8,128)S(1)}, f32[32,8,128]{2,1,0:T(8,128)S(1)}, u32[]{:S(2)}, u32[]{:S(2)}) collective-permute-start(f32[32,8,128]{2,1,0:T(8,128)S(1)} %pad_maximum_fusion.3), channel_id=1, source_target_pairs={{0,3},{1,2},{2,1},{3,0},{4,7},{5,6},{6,5},{7,4},{8,11},{9,10},{10,... | collective-permute-start | bytes 393224 | tf_op jit(solution)/shard_map/ppermute | solution.py:646
  60.9 6.4 %collective-permute-start.12 = (f32[32,8,128]{2,1,0:T(8,128)S(1)}, f32[32,8,128]{2,1,0:T(8,128)S(1)}, u32[]{:S(2)}, u32[]{:S(2)}) collective-permute-start(f32[32,8,128]{2,1,0:T(8,128)S(1)} %pad_maximum_fusion.2), channel_id=1, source_target_pairs={{0,1},{1,0},{2,3},{3,2},{4,5},{5,4},{6,7},{7,6},{8,9},{9,8},{10,11... | collective-permute-start | bytes 393224 | tf_op jit(solution)/shard_map/ppermute | solution.py:646
  71.0 10.0 %collective-permute-start.15 = (f32[32,8,128]{2,1,0:T(8,128)S(1)}, f32[32,8,128]{2,1,0:T(8,128)S(1)}, u32[]{:S(2)}, u32[]{:S(2)}) collective-permute-start(f32[32,8,128]{2,1,0:T(8,128)S(1)} %pad_maximum_fusion.5), channel_id=1, source_target_pairs={{0,3},{1,2},{2,1},{3,0},{4,7},{5,6},{6,5},{7,4},{8,11},{9,10},{10,... | collective-permute-start | bytes 393224 | tf_op jit(solution)/shard_map/ppermute | solution.py:646
  73.1 7.9 %collective-permute-start.14 = (f32[32,8,128]{2,1,0:T(8,128)S(1)}, f32[32,8,128]{2,1,0:T(8,128)S(1)}, u32[]{:S(2)}, u32[]{:S(2)}) collective-permute-start(f32[32,8,128]{2,1,0:T(8,128)S(1)} %pad_maximum_fusion.4), channel_id=1, source_target_pairs={{0,1},{1,0},{2,3},{3,2},{4,5},{5,4},{6,7},{7,6},{8,9},{9,8},{10,11... | collective-permute-start | bytes 393224 | tf_op jit(solution)/shard_map/ppermute | solution.py:646
  84.7 11.1 %collective-permute-start.17 = (f32[32,8,128]{2,1,0:T(8,128)S(1)}, f32[32,8,128]{2,1,0:T(8,128)S(1)}, u32[]{:S(2)}, u32[]{:S(2)}) collective-permute-start(f32[32,8,128]{2,1,0:T(8,128)S(1)} %pad_maximum_fusion.7), channel_id=1, source_target_pairs={{0,3},{1,2},{2,1},{3,0},{4,7},{5,6},{6,5},{7,4},{8,11},{9,10},{10,... | collective-permute-start | bytes 393224 | tf_op jit(solution)/shard_map/ppermute | solution.py:646
  86.7 9.2 %collective-permute-start.16 = (f32[32,8,128]{2,1,0:T(8,128)S(1)}, f32[32,8,128]{2,1,0:T(8,128)S(1)}, u32[]{:S(2)}, u32[]{:S(2)}) collective-permute-start(f32[32,8,128]{2,1,0:T(8,128)S(1)} %pad_maximum_fusion.6), channel_id=1, source_target_pairs={{0,1},{1,0},{2,3},{3,2},{4,5},{5,4},{6,7},{7,6},{8,9},{9,8},{10,11... | collective-permute-start | bytes 393224 | tf_op jit(solution)/shard_map/ppermute | solution.py:646
  97.1 10.3 %collective-permute-start.24 = (f32[512,128]{1,0:T(8,128)S(1)}, f32[512,128]{1,0:T(8,128)S(1)}, u32[]{:S(2)}, u32[]{:S(2)}) collective-permute-start(f32[512,128]{1,0:T(8,128)S(1)} %get-tuple-element.122), channel_id=1, source_target_pairs={{0,24},{4,28},{8,16},{12,20},{16,8},{20,12},{24,0},{28,4},{1,25},{... | collective-permute-start | bytes 786440 | tf_op jit(solution)/shard_map/ppermute | solution.py:522
  99.6 13.4 %collective-permute-start.23 = (f32[512,128]{1,0:T(8,128)S(1)}, f32[512,128]{1,0:T(8,128)S(1)}, u32[]{:S(2)}, u32[]{:S(2)}) collective-permute-start(f32[512,128]{1,0:T(8,128)S(1)} %get-tuple-element.121), channel_id=1, source_target_pairs={{0,16},{4,20},{8,24},{12,28},{16,0},{20,4},{24,8},{28,12},{1,17},{... | collective-permute-start | bytes 786440 | tf_op jit(solution)/shard_map/ppermute | solution.py:522
  100.1 13.7 %collective-permute-start.22 = (f32[512,128]{1,0:T(8,128)S(1)}, f32[512,128]{1,0:T(8,128)S(1)}, u32[]{:S(2)}, u32[]{:S(2)}) collective-permute-start(f32[512,128]{1,0:T(8,128)S(1)} %get-tuple-element.120), channel_id=1, source_target_pairs={{0,8},{4,12},{8,0},{12,4},{16,24},{20,28},{24,16},{28,20},{1,9},{5... | collective-permute-start | bytes 786440 | tf_op jit(solution)/shard_map/ppermute | solution.py:522
  101.9 14.5 %collective-permute-start.20 = (f32[512,128]{1,0:T(8,128)S(1)}, f32[512,128]{1,0:T(8,128)S(1)}, u32[]{:S(2)}, u32[]{:S(2)}) collective-permute-start(f32[512,128]{1,0:T(8,128)S(1)} %get-tuple-element.117), channel_id=1, source_target_pairs={{0,24},{4,28},{8,16},{12,20},{16,8},{20,12},{24,0},{28,4},{1,25},{... | collective-permute-start | bytes 786440 | tf_op jit(solution)/shard_map/ppermute | solution.py:522
  104.4 14.8 %collective-permute-start.19 = (f32[512,128]{1,0:T(8,128)S(1)}, f32[512,128]{1,0:T(8,128)S(1)}, u32[]{:S(2)}, u32[]{:S(2)}) collective-permute-start(f32[512,128]{1,0:T(8,128)S(1)} %get-tuple-element.116), channel_id=1, source_target_pairs={{0,16},{4,20},{8,24},{12,28},{16,0},{20,4},{24,8},{28,12},{1,17},{... | collective-permute-start | bytes 786440 | tf_op jit(solution)/shard_map/ppermute | solution.py:522
  107.4 11.8 %collective-permute-start.18 = (f32[512,128]{1,0:T(8,128)S(1)}, f32[512,128]{1,0:T(8,128)S(1)}, u32[]{:S(2)}, u32[]{:S(2)}) collective-permute-start(f32[512,128]{1,0:T(8,128)S(1)} %get-tuple-element.115), channel_id=1, source_target_pairs={{0,8},{4,12},{8,0},{12,4},{16,24},{20,28},{24,16},{28,20},{1,9},{5... | collective-permute-start | bytes 786440 | tf_op jit(solution)/shard_map/ppermute | solution.py:522
  113.8 5.5 %collective-permute-start.25 = (f32[1024,128]{1,0:T(8,128)S(1)}, f32[1024,128]{1,0:T(8,128)S(1)}, u32[]{:S(2)}, u32[]{:S(2)}) collective-permute-start(f32[1024,128]{1,0:T(8,128)S(1)} %pad_maximum_fusion.1), channel_id=1, source_target_pairs={{0,4},{4,0},{8,12},{12,8},{16,20},{20,16},{24,28},{28,24},{1,5},{5... | collective-permute-start | bytes 1572872 | tf_op jit(solution)/shard_map/ppermute | solution.py:522
  119.3 2.1 %collective-permute-start.21 = (f32[1024,128]{1,0:T(8,128)S(1)}, f32[1024,128]{1,0:T(8,128)S(1)}, u32[]{:S(2)}, u32[]{:S(2)}) collective-permute-start(f32[1024,128]{1,0:T(8,128)S(1)} %pad_maximum_fusion), channel_id=1, source_target_pairs={{0,4},{4,0},{8,12},{12,8},{16,20},{20,16},{24,28},{28,24},{1,5},{5... | collective-permute-start | bytes 1572872 | tf_op jit(solution)/shard_map/ppermute | solution.py:522
  125.2 3.9 %collective-permute-start.27 = (f32[64,64]{1,0:T(8,128)S(1)}, f32[64,64]{1,0:T(8,128)S(1)}, u32[]{:S(2)}, u32[]{:S(2)}) collective-permute-start(f32[64,64]{1,0:T(8,128)S(1)} %fusion), channel_id=1, source_target_pairs={{0,8},{4,12},{8,0},{12,4},{16,24},{20,28},{24,16},{28,20},{1,9},{5... | collective-permute-start | bytes 49160 | tf_op jit(solution)/shard_map/ppermute | solution.py:522
  126.5 3.9 %collective-permute-start.28 = (f32[64,64]{1,0:T(8,128)S(1)}, f32[64,64]{1,0:T(8,128)S(1)}, u32[]{:S(2)}, u32[]{:S(2)}) collective-permute-start(f32[64,64]{1,0:T(8,128)S(1)} %fusion), channel_id=1, source_target_pairs={{0,16},{4,20},{8,24},{12,28},{16,0},{20,4},{24,8},{28,12},{1,17},{... | collective-permute-start | bytes 49160 | tf_op jit(solution)/shard_map/ppermute | solution.py:522
  128.0 4.8 %collective-permute-start.29 = (f32[64,64]{1,0:T(8,128)S(1)}, f32[64,64]{1,0:T(8,128)S(1)}, u32[]{:S(2)}, u32[]{:S(2)}) collective-permute-start(f32[64,64]{1,0:T(8,128)S(1)} %fusion), channel_id=1, source_target_pairs={{0,24},{4,28},{8,16},{12,20},{16,8},{20,12},{24,0},{28,4},{1,25},{... | collective-permute-start | bytes 49160 | tf_op jit(solution)/shard_map/ppermute | solution.py:522
  132.8 4.5 %collective-permute-start.30 = (f32[16,64]{1,0:T(8,128)S(1)}, f32[16,64]{1,0:T(8,128)S(1)}, u32[]{:S(2)}, u32[]{:S(2)}) collective-permute-start(f32[16,64]{1,0:T(8,128)S(1)} %get-tuple-element.128), channel_id=1, source_target_pairs={{0,1},{1,0},{2,3},{3,2},{4,5},{5,4},{6,7},{7,6},{8,9},{9,8},{10,11... | collective-permute-start | bytes 12296 | tf_op jit(solution)/shard_map/ppermute | solution.py:525
  134.2 4.5 %collective-permute-start.31 = (f32[16,64]{1,0:T(8,128)S(1)}, f32[16,64]{1,0:T(8,128)S(1)}, u32[]{:S(2)}, u32[]{:S(2)}) collective-permute-start(f32[16,64]{1,0:T(8,128)S(1)} %get-tuple-element.130), channel_id=1, source_target_pairs={{0,2},{1,3},{2,0},{3,1},{4,6},{5,7},{6,4},{7,5},{8,10},{9,11},{10,... | collective-permute-start | bytes 12296 | tf_op jit(solution)/shard_map/ppermute | solution.py:525
  136.0 5.4 %collective-permute-start.32 = (f32[16,64]{1,0:T(8,128)S(1)}, f32[16,64]{1,0:T(8,128)S(1)}, u32[]{:S(2)}, u32[]{:S(2)}) collective-permute-start(f32[16,64]{1,0:T(8,128)S(1)} %get-tuple-element.129), channel_id=1, source_target_pairs={{0,3},{1,2},{2,1},{3,0},{4,7},{5,6},{6,5},{7,4},{8,11},{9,10},{10,... | collective-permute-start | bytes 12296 | tf_op jit(solution)/shard_map/ppermute | solution.py:525
  (14 other events, 51.4 us)

commit v5 on v4

--- a/solution.py
+++ b/solution.py
@@ -119,23 +119,17 @@
 
 def atoms_kernel(gx, gy, nb, count, fold, me_ref, after_ref, *refs):
     half = gx * gy // 2
-    roots_ref, meta_ref, raw, sem = refs[half:]
+    roots_ref, meta_ref, whole, raw, sem = refs[half:]
     rows = 4 * count + 8
     sources = []
     for n in range(half):
         for other in range(2):
             at = 2 * nb * 64 + other * rows
             sources.append((me_ref[0] ^ (2 * n + other), refs[n].at[pl.ds(at, rows)]))
-    copies = [
-        pltpu.make_async_copy(
-            source.at[pl.ds(rows - 8, 8)],
-            raw.at[pl.ds(pl.multiple_of(slot * 8, 8), 8)],
-            sem.at[0],
-        )
-        for slot, source in sources
-    ]
-    for copy in copies:
-        copy.start()
+    for slot, source in sources:
+        whole[pl.ds(slot, 1)] = source[rows - 8 : rows - 7].astype(jnp.int32)
+    copy = pltpu.make_async_copy(whole, raw, sem.at[0])
+    copy.start()
     sub = lax.broadcasted_iota(jnp.int32, (SUBS, LANES), 0)
     per_slot = count // (2 * fold)
     for slot, source in sources:
@@ -147,15 +141,12 @@
                     parts.append(jnp.broadcast_to(source[at : at + 1, :], (SUBS, LANES)))
                 value = parts[0] if fold == 1 else jnp.where(sub < SUBS // 2, parts[0], parts[1])
                 roots_ref[(slot * per_slot + m) * 8 + k] = value
-    for copy in copies:
-        copy.wait()
+    copy.wait()
 
     def corners(slot, carry):
         for atom in range(count):
-            n = slot * count + atom
-            first = (raw[slot * 8, atom].astype(jnp.int32) + (slot % gy) * 64) * SUBS
-            meta_ref[2 * n] = first + (slot // gy * nb if fold == 2 else 0)
-            meta_ref[2 * n + 1] = raw[slot * 8, count + atom].astype(jnp.int32)
+            meta_ref[2 * (slot * count + atom)] = raw[slot, atom]
+            meta_ref[2 * (slot * count + atom) + 1] = raw[slot, count + atom]
         return carry
 
     lax.fori_loop(0, gx * gy, corners, 0)
@@ -195,11 +186,11 @@
 
 
 def join_kernel(
-    group, size, chunk, extra, me_ref, field, after_ref, passed, own_ref, other_ref, *refs
+    group, size, chunk, extra, chips, me_ref, field, after_ref, passed, own_ref, other_ref, *refs
 ):
     blocks, sem = refs[:-1], refs[-1]
     copies = []
-    for n, block in enumerate(blocks):
+    for n, block in zip(chips, blocks):
         chip = me_ref[0] // 2 ^ n
         row = (chunk * group + chip * 2 + me_ref[0] % 2) * size
         copies.append(
@@ -212,7 +203,7 @@
     for copy in copies:
         copy.start()
     first, rows = extra
-    for n, block in enumerate(blocks):
+    for n, block in zip(chips, blocks):
         chip = me_ref[0] // 2 ^ n
         row = (chunk * group // 2 + chip) * size
         block[pl.ds(size, size)] = passed[pl.ds(pl.multiple_of(row, 64), size)]
@@ -258,7 +249,7 @@
         z_ref, roots_ref, w_ref, sum_ref = refs[:4]
     else:
         z_ref, prev_ref, diag_ref, roots_ref, w_ref, sum_ref = refs[:6]
-    out_ref, atoms_ref, acc, tile_ref, spread_ref = refs[-5:]
+    out_ref, atoms_ref, tile_ref, spread_ref = refs[-4:]
     group = gx * gy
     ny = gy * 8
     width = TILE // fold
@@ -307,24 +298,17 @@
                 for here, value in sums:
                     atoms_ref[here] = value
 
-    def second_dim(x, carry):
+    def third_dim(n, carry):
         for c in range(group // 8):
-            gather(x * (group // 8) + c)
-        block = pl.ds(pl.multiple_of(x * 32 * SUBS, 32 * SUBS), 32 * SUBS)
+            gather(n * (group // 8) + c)
+        block = pl.ds(pl.multiple_of(n * 32 * SUBS, 32 * SUBS), 32 * SUBS)
         operand = jnp.concatenate(halves(z_ref[block]), axis=1)
         product = jnp.dot(operand, w_ref[...], preferred_element_type=F32)
         out_ref[block] = product[:, :LANES] + product[:, LANES:]
-        values = [z_ref[tile_rows(y * 8 + x)] for y in range(ny)]
-        for y in range(ny):
-            total = None
-            for k in range(1, REACH + 1):
-                term = TAPS[k] * (values[(y + k) % ny] + values[(y - k) % ny])
-                total = term if total is None else total + term
-            acc[tile_rows(y * 8 + x)] = total
-            atoms_ref[tile_rows(y * 8 + x)] = jnp.zeros((SUBS, LANES), F32)
+        atoms_ref[block] = jnp.zeros((32 * SUBS, LANES), F32)
         return carry
 
-    lax.fori_loop(0, 8, second_dim, 0, unroll=2)
+    lax.fori_loop(0, 8, third_dim, 0, unroll=8 if group <= 8 else 1)
 
     def contract(eight, carry):
         products = []
@@ -353,17 +337,21 @@
 
     def rest(four):
         for q in range(4):
-            values = [z_ref[tile_rows(four * 32 + 8 * q + x)] for x in range(8)]
+            y = four * 4 + q
+            values = [z_ref[tile_rows(y * 8 + x)] for x in range(8)]
             after = [pltpu.roll(value, SUBS - nb, 0) for value in values]
             before = after if gx == 2 else [pltpu.roll(value, nb, 0) for value in values]
             wide = before + values + after
+            up = [(y + k) % ny * 8 for k in range(REACH + 1)]
+            down = [(y + ny - k) % ny * 8 for k in range(REACH + 1)]
             for x in range(8):
-                here = tile_rows(four * 32 + 8 * q + x)
-                total = acc[here] + out_ref[here]
+                here = tile_rows(y * 8 + x)
+                total = out_ref[here]
                 if not first:
                     total = total + diag_ref[here] * values[x]
                 for k in range(1, REACH + 1):
-                    total = total + TAPS[k] * (wide[8 + x + k] + wide[8 + x - k])
+                    beside = z_ref[tile_rows(up[k] + x)] + z_ref[tile_rows(down[k] + x)]
+                    total = total + TAPS[k] * (wide[8 + x + k] + wide[8 + x - k] + beside)
                 if not first:
                     total = 2.0 * total - prev_ref[here]
                 out_ref[here] = total
@@ -375,7 +363,7 @@
             rest(2 * j + half)
         return carry
 
-    lax.fori_loop(0, gy, block, 0)
+    lax.fori_loop(0, gy, block, 0, unroll=gy if group <= 8 else 1)
 
 
 def outer_kernel(
@@ -532,7 +520,10 @@
         ]
     )
     local = atom_corner - anchor[None, :]
-    meta = jnp.concatenate([local[:, 1] * 8 + local[:, 0], local[:, 2]]).astype(F32)
+    start = (me % gy * 64 + local[:, 1] * 8 + local[:, 0]) * SUBS
+    if fold == 2:
+        start = start + me // gy * nb
+    meta = jnp.concatenate([start, local[:, 2]]).astype(F32)
     meta = jnp.broadcast_to(jnp.pad(meta, (0, LANES - 2 * count))[None], (8, LANES))
     part_rows = 64 + 4 * count + 8
     size = nb * 64
@@ -567,20 +558,24 @@
     passed = swap(passed, 1)
     other_parts = swap(parts, 1)
     forward = []
-    joined = []
     for chunk in range(CHUNKS):
         extra = (64, tables) if chunk == 0 else (0, 64 if chunk == CHUNKS - 1 else 0)
-        joined = pl.pallas_call(
-            functools.partial(join_kernel, group, size, chunk, extra),
-            out_shape=[shape(2 * size + 2 * extra[1], LANES)] * (group // 2),
-            in_specs=[SMEM, HBM, ANY] + [VMEM] * 3,
-            out_specs=[VMEM] * (group // 2),
-            scratch_shapes=[pltpu.SemaphoreType.DMA((1,))],
-            compiler_params=PARAMS,
-            cost_estimate=cost(1),
-            name="join",
-        )(me_arr, field, forward[0][1] if chunk else parts, passed, parts, other_parts)
-        forward.append(cross(joined))
+
+        def join(chips, after):
+            return pl.pallas_call(
+                functools.partial(join_kernel, group, size, chunk, extra, chips),
+                out_shape=[shape(2 * size + 2 * extra[1], LANES)] * len(chips),
+                in_specs=[SMEM, HBM, ANY] + [VMEM] * 3,
+                out_specs=[VMEM] * len(chips),
+                scratch_shapes=[pltpu.SemaphoreType.DMA((1,))],
+                compiler_params=PARAMS,
+                cost_estimate=cost(1),
+                name="join",
+            )(me_arr, field, after, passed, parts, other_parts)
+
+        sent = join(range(1, group // 2), forward[0][1] if chunk else parts)
+        came = [swap(block, 2 * n) for n, block in enumerate(sent, 1)]
+        forward.append([*join(range(1), came[0]), *came])
 
     tile_shape = shape(rows * SUBS, LANES)
     edge_shape = shape(pairs, SUBS, LANES)
@@ -596,7 +591,7 @@
         )(me_arr, after, *forward[chunk])
         return None, tiles, one, two
 
-    states = [unpack(0, joined[0])]
+    states = [unpack(0, sent[0])]
     root_tiles = group * count * 8 // (2 * fold)
     roots, places = pl.pallas_call(
         functools.partial(atoms_kernel, gx, gy, nb, count, fold),
@@ -607,7 +602,8 @@
         in_specs=[SMEM, ANY] + [VMEM] * (group // 2),
         out_specs=[VMEM, SMEM],
         scratch_shapes=[
-            pltpu.SMEM((group * 8, LANES), F32),
+            pltpu.VMEM((group, LANES), jnp.int32),
+            pltpu.SMEM((group, LANES), jnp.int32),
             pltpu.SemaphoreType.DMA((1,)),
         ],
         compiler_params=PARAMS,
@@ -656,8 +652,7 @@
                     out_shape=[tile_shape, tile_shape],
                     in_specs=[ANY, SMEM] + [VMEM] * (len(operands) - 2),
                     out_specs=[VMEM] * 2,
-                    scratch_shapes=[pltpu.VMEM((rows * SUBS, LANES), F32)]
-                    + [pltpu.VMEM((root_tiles // 8, SUBS, LANES), F32)] * 2,
+                    scratch_shapes=[pltpu.VMEM((root_tiles // 8, SUBS, LANES), F32)] * 2,
                     compiler_params=PARAMS,
                     cost_estimate=cost(4),
                     name="inner",

time: 142 us -> 138 us (0.972)
  Pallas kernels: 60.6 us -> 57.2 us
    pallas_call x8, Pallas kernels: 31.2 us -> 27 us  [shards(): pl.pallas_call(functools.partial(inner_kernel, gx, gy, nb, count, fold, f...]
    pallas_call x2 -> x4, Pallas kernels: 3.5 us -> 4.63 us  [join(): pl.pallas_call(functools.partial(join_kernel, group, size, chunk, extra,...]
  transfers between devices with their start and end apart: 33 -> 33, of which waited for: 17 -> 17; matrix products, arithmetic and copies ran while one was open for 0% -> 0% of each run, Pallas kernels for 32% -> 31%
where the time goes in v5:
time: 138 us
  Pallas kernels  57.2 us (41%)
  starting transfers between devices  40.6 us (29%)
  waiting for transfers between devices  34.7 us (25%)
  local copies, waits for them, and re-layouts  3.25 us (2%)
    ppermute x20, waiting for transfers between devices, swap(): return lax.ppermute(block, column, [(s, s ^ d) for s in range(group)])  27.7 us
    pallas_call x8, Pallas kernels, shards(): pl.pallas_call(functools.partial(inner_kernel, gx, gy, nb, count, fold, f...  27 us
    ppermute x20, starting transfers between devices, swap(): return lax.ppermute(block, column, [(s, s ^ d) for s in range(group)])  20.8 us
    pallas_call x8, Pallas kernels, shards(): pl.pallas_call(functools.partial(outer_kernel, gx, gy, nb, first, last, e...  13.8 us
    ppermute x3, starting transfers between devices, shards(): lax.ppermute(two, 'gz', pair_two)  5.33 us
    ppermute x2, starting transfers between devices, shards(): lax.ppermute(state[3], 'gz', pair_two)  4.98 us
    pallas_call x4, Pallas kernels, join(): pl.pallas_call(functools.partial(join_kernel, group, size, chunk, extra,...  4.63 us
    ppermute x3, starting transfers between devices, swap_z(): return lax.ppermute(block, 'gz', [(s, s ^ d) for s in range(gz)])  4.45 us
  transfers between devices with their start and end apart: 33, of which 17 were waited for; matrix products, arithmetic and copies ran while one was open for 0% of the time, Pallas kernels for 31%

profile of v5, /device:TPU:0, one launch (start us, length us, event | category | flops | bytes accessed | tf_op | source)
XLA Modules:
  0.0 138.2 jit_solution(5191896555348264846)
XLA Ops:
  0.7 2.3 %constant_dynamic-slice_fusion.11 = f32[2,4,1,256,128]{4,3,2,1,0:T(8,128)} fusion(f32[2,4,2,256,128]{4,3,2,1,0:T(8,128)} %bitcast.26, s32[]{:T(128)S(6)} %select_n.48), kind=kLoop, calls=%fused_computation.26 | loop fusion | bytes 2097156 | tf_op jit(solution)/shard_map/dynamic_slice | solution.py:557
  5.9 2.0 %join.4 = (f32[592,128]{1,0:T(8,128)}, f32[592,128]{1,0:T(8,128)}, f32[592,128]{1,0:T(8,128)}) custom-call(s32[2]{0:T(128)S(1)} %pad_add_fusion.me_ref, f32[4096,128]{1,0:T(8,128)S(1)} %bitcast.27, f32[104,128]{1,0:T(8,128)S(1)} %parts.1.after_ref.own_ref, f32[2048,128]{1,0:T(8,128)S(1)} %collective-permute-done.passed, ...), custom_call_target="tpu_custom_call" | custom-call | flops 1000000000 | bytes 3000000 | tf_op jit(solution)/shard_map/join/pallas_call | solution.py:565
  8.0 3.0 %collective-permute-start.2 = (f32[592,128]{1,0:T(8,128)}, f32[592,128]{1,0:T(8,128)S(1)}, u32[]{:S(2)}, u32[]{:S(2)}) collective-permute-start(f32[592,128]{1,0:T(8,128)} %get-tuple-element.63), channel_id=1, source_target_pairs={{0,8},{4,12},{8,0},{12,4},{16,24},{20,28},{24,16},{28,20},{1,9},{5... | collective-permute-start | bytes 909320 | tf_op jit(solution)/shard_map/ppermute | solution.py:510
  12.5 6.2 %collective-permute-done.2.after_ref.refs_1_ = f32[592,128]{1,0:T(8,128)S(1)} collective-permute-done((f32[592,128]{1,0:T(8,128)}, f32[592,128]{1,0:T(8,128)S(1)}, u32[]{:S(2)}, u32[]{:S(2)}) %collective-permute-start.2) | collective-permute-done | bytes 303136 | tf_op jit(solution)/shard_map/ppermute | solution.py:510
  24.7 2.6 %collective-permute-done.4.refs_3_ = f32[592,128]{1,0:T(8,128)} collective-permute-done((f32[592,128]{1,0:T(8,128)}, f32[592,128]{1,0:T(8,128)}, u32[]{:S(2)}, u32[]{:S(2)}) %collective-permute-start.4) | collective-permute-done | bytes 303136 | tf_op jit(solution)/shard_map/ppermute | solution.py:510
  27.3 2.1 %unpack.2 = (f32[2048,128]{1,0:T(8,128)S(1)}, f32[16,8,128]{2,1,0:T(8,128)S(1)}, f32[16,8,128]{2,1,0:T(8,128)S(1)}) custom-call(s32[2]{0:T(128)S(1)} %copy-done.3, f32[640,128]{1,0:T(8,128)S(1)} %get-tuple-element.64.after_ref, f32[592,128]{1,0:T(8,128)S(1)} %join.6.refs_0_, f32[592,128]{1,0:T(8,128)S(1)} %collective-permute-done.2.after_ref.refs_1_, ...), custom_call_target="tpu_custom_call" | custom-call | flops 2000000000 | bytes 6000000 | tf_op jit(solution)/shard_map/unpack/pallas_call | solution.py:583
  29.4 2.1 %collective-permute-start.5 = (f32[16,8,128]{2,1,0:T(8,128)S(1)}, f32[16,8,128]{2,1,0:T(8,128)S(1)}, u32[]{:S(2)}, u32[]{:S(2)}) collective-permute-start(f32[16,8,128]{2,1,0:T(8,128)S(1)} %get-tuple-element.67.after_ref), channel_id=1, source_target_pairs={{0,1},{1,0},{2,3},{3,2},{4,5},{5,4},{6,7},{7,6},{8,9},{9,8},{10,11... | collective-permute-start | bytes 196616 | tf_op jit(solution)/shard_map/ppermute | solution.py:636
  31.5 2.5 %collective-permute-start.6 = (f32[16,8,128]{2,1,0:T(8,128)S(1)}, f32[16,8,128]{2,1,0:T(8,128)S(1)}, u32[]{:S(2)}, u32[]{:S(2)}) collective-permute-start(f32[16,8,128]{2,1,0:T(8,128)S(1)} %get-tuple-element.73), channel_id=1, source_target_pairs={{0,3},{1,2},{2,1},{3,0},{4,7},{5,6},{6,5},{7,4},{8,11},{9,10},{10,... | collective-permute-start | bytes 196616 | tf_op jit(solution)/shard_map/ppermute | solution.py:636
  34.0 2.5 %atoms.1 = (f32[128,8,128]{2,1,0:T(8,128)S(1)}, s32[128]{0:T(128)S(1)}) custom-call(s32[2]{0:T(128)S(1)} %copy-done.3, f32[16,8,128]{2,1,0:T(8,128)S(1)} %get-tuple-element.67.after_ref, f32[592,128]{1,0:T(8,128)S(1)} %join.6.refs_0_, f32[592,128]{1,0:T(8,128)S(1)} %collective-permute-done.2.after_ref.refs_1_, f32[592,128]{1,0:T(8,128)} %collective-permute-done.3.refs_2_, ...), custom_call_target="tpu_custom_call" | custom-call | flops 1000000000 | bytes 3000000 | tf_op jit(solution)/shard_map/atoms/pallas_call | solution.py:596
  36.5 3.3 %inner.8 = (f32[2048,128]{1,0:T(8,128)S(1)}, f32[2048,128]{1,0:T(8,128)S(1)}) custom-call(f32[128,8,128]{2,1,0:T(8,128)S(1)} %get-tuple-element.68.after_ref.refs_1_.refs_3_, s32[128]{0:T(128)S(1)} %get-tuple-element.69.meta_ref, f32[2048,128]{1,0:T(8,128)S(1)} %get-tuple-element.70.refs_0_.refs_1_, ...), custom_call_target="tpu_custom_call" | custom-call | flops 4000000000 | bytes 12000000 | tf_op jit(solution)/shard_map/inner/pallas_call | solution.py:650
  42.2 3.3 %inner.10 = (f32[2048,128]{1,0:T(8,128)S(1)}, f32[2048,128]{1,0:T(8,128)S(1)}) custom-call(f32[128,8,128]{2,1,0:T(8,128)S(1)} %get-tuple-element.68.after_ref.refs_1_.refs_3_, s32[128]{0:T(128)S(1)} %get-tuple-element.69.meta_ref, f32[2048,128]{1,0:T(8,128)S(1)} %get-tuple-element.79.refs_0_.refs_1_, ...), custom_call_target="tpu_custom_call" | custom-call | flops 4000000000 | bytes 12000000 | tf_op jit(solution)/shard_map/inner/pallas_call | solution.py:650
  47.1 2.5 %collective-permute-start.11 = (f32[16,8,128]{2,1,0:T(8,128)S(1)}, f32[16,8,128]{2,1,0:T(8,128)S(1)}, u32[]{:S(2)}, u32[]{:S(2)}) collective-permute-start(f32[16,8,128]{2,1,0:T(8,128)S(1)} %get-tuple-element.82), channel_id=1, source_target_pairs={{0,3},{1,2},{2,1},{3,0},{4,7},{5,6},{6,5},{7,4},{8,11},{9,10},{10,... | collective-permute-start | bytes 196616 | tf_op jit(solution)/shard_map/ppermute | solution.py:636
  52.3 3.4 %inner.9 = (f32[2048,128]{1,0:T(8,128)S(1)}, f32[2048,128]{1,0:T(8,128)S(1)}) custom-call(f32[128,8,128]{2,1,0:T(8,128)S(1)} %get-tuple-element.68.after_ref.refs_1_.refs_3_, s32[128]{0:T(128)S(1)} %get-tuple-element.69.meta_ref, f32[2048,128]{1,0:T(8,128)S(1)} %get-tuple-element.77.refs_0_.refs_1_, f32[2048,128]{1,0:T(8,128)S(1)} %get-tuple-element.70.refs_0_.refs_1_, ...), custom_call_target="tpu_custom_call" | custom-call | flops 4000000000 | bytes 12000000 | tf_op jit(solution)/shard_map/inner/pallas_call | solution.py:650
  55.7 2.0 %outer.9 = (f32[2048,128]{1,0:T(8,128)S(1)}, f32[16,8,128]{2,1,0:T(8,128)S(1)}, f32[16,8,128]{2,1,0:T(8,128)S(1)}) custom-call(s32[2]{0:T(128)S(1)} %copy-done.3, f32[128,8,128]{2,1,0:T(8,128)S(1)} %get-tuple-element.68.after_ref.refs_1_.refs_3_, f32[2048,128]{1,0:T(8,128)S(1)} %get-tuple-element.80.part_ref, f32[2048,128]{1,0:T(8,128)S(1)} %get-tuple-element.81.atoms_ref, ...), custom_call_target="tpu_custom_call" | custom-call | flops 1000000000 | bytes 3000000 | tf_op jit(solution)/shard_map/outer/pallas_call | solution.py:668
  59.2 3.4 %inner.11 = (f32[2048,128]{1,0:T(8,128)S(1)}, f32[2048,128]{1,0:T(8,128)S(1)}) custom-call(f32[128,8,128]{2,1,0:T(8,128)S(1)} %get-tuple-element.68.after_ref.refs_1_.refs_3_, s32[128]{0:T(128)S(1)} %get-tuple-element.69.meta_ref, f32[2048,128]{1,0:T(8,128)S(1)} %get-tuple-element.83.refs_0_.refs_1_, f32[2048,128]{1,0:T(8,128)S(1)} %get-tuple-element.79.refs_0_.refs_1_, ...), custom_call_target="tpu_custom_call" | custom-call | flops 4000000000 | bytes 12000000 | tf_op jit(solution)/shard_map/inner/pallas_call | solution.py:650
  62.6 2.3 %collective-permute-done.13.two_in = f32[32,8,128]{2,1,0:T(8,128)S(1)} collective-permute-done((f32[32,8,128]{2,1,0:T(8,128)S(1)}, f32[32,8,128]{2,1,0:T(8,128)S(1)}, u32[]{:S(2)}, u32[]{:S(2)}) %collective-permute-start.13) | collective-permute-done | bytes 131104 | tf_op jit(solution)/shard_map/ppermute | solution.py:642
  69.3 2.1 %collective-permute-start.15 = (f32[32,8,128]{2,1,0:T(8,128)S(1)}, f32[32,8,128]{2,1,0:T(8,128)S(1)}, u32[]{:S(2)}, u32[]{:S(2)}) collective-permute-start(f32[32,8,128]{2,1,0:T(8,128)S(1)} %pad_maximum_fusion.5), channel_id=1, source_target_pairs={{0,3},{1,2},{2,1},{3,0},{4,7},{5,6},{6,5},{7,4},{8,11},{9,10},{10,... | collective-permute-start | bytes 393224 | tf_op jit(solution)/shard_map/ppermute | solution.py:642
  71.4 3.4 %inner.13 = (f32[2048,128]{1,0:T(8,128)S(1)}, f32[2048,128]{1,0:T(8,128)S(1)}) custom-call(f32[128,8,128]{2,1,0:T(8,128)S(1)} %get-tuple-element.68.after_ref.refs_1_.refs_3_, s32[128]{0:T(128)S(1)} %get-tuple-element.69.meta_ref, f32[2048,128]{1,0:T(8,128)S(1)} %get-tuple-element.93.refs_0_.refs_1_, f32[2048,128]{1,0:T(8,128)S(1)} %get-tuple-element.77.refs_0_.refs_1_, ...), custom_call_target="tpu_custom_call" | custom-call | flops 4000000000 | bytes 12000000 | tf_op jit(solution)/shard_map/inner/pallas_call | solution.py:650
  74.8 3.4 %inner.12 = (f32[2048,128]{1,0:T(8,128)S(1)}, f32[2048,128]{1,0:T(8,128)S(1)}) custom-call(f32[128,8,128]{2,1,0:T(8,128)S(1)} %get-tuple-element.68.after_ref.refs_1_.refs_3_, s32[128]{0:T(128)S(1)} %get-tuple-element.69.meta_ref, f32[2048,128]{1,0:T(8,128)S(1)} %get-tuple-element.90.refs_0_.refs_1_, f32[2048,128]{1,0:T(8,128)S(1)} %get-tuple-element.83.refs_0_.refs_1_, ...), custom_call_target="tpu_custom_call" | custom-call | flops 4000000000 | bytes 12000000 | tf_op jit(solution)/shard_map/inner/pallas_call | solution.py:650
  80.1 2.0 %outer.12 = (f32[2048,128]{1,0:T(8,128)S(1)}, f32[16,8,128]{2,1,0:T(8,128)S(1)}, f32[16,8,128]{2,1,0:T(8,128)S(1)}) custom-call(s32[2]{0:T(128)S(1)} %copy-done.3, f32[2048,128]{1,0:T(8,128)S(1)} %get-tuple-element.91.after_ref.part_ref, f32[2048,128]{1,0:T(8,128)S(1)} %get-tuple-element.94.part_ref.after_ref, f32[2048,128]{1,0:T(8,128)S(1)} %get-tuple-element.95.atoms_ref, ...), custom_call_target="tpu_custom_call" | custom-call | flops 1000000000 | bytes 3000000 | tf_op jit(solution)/shard_map/outer/pallas_call | solution.py:668
  85.2 3.4 %inner.15 = (f32[2048,128]{1,0:T(8,128)S(1)}, f32[2048,128]{1,0:T(8,128)S(1)}) custom-call(f32[128,8,128]{2,1,0:T(8,128)S(1)} %get-tuple-element.68.after_ref.refs_1_.refs_3_, s32[128]{0:T(128)S(1)} %get-tuple-element.69.meta_ref, f32[2048,128]{1,0:T(8,128)S(1)} %get-tuple-element.103.refs_0_, f32[2048,128]{1,0:T(8,128)S(1)} %get-tuple-element.90.refs_0_.refs_1_, ...), custom_call_target="tpu_custom_call" | custom-call | flops 4000000000 | bytes 12000000 | tf_op jit(solution)/shard_map/inner/pallas_call | solution.py:650
  88.7 3.4 %inner.14 = (f32[2048,128]{1,0:T(8,128)S(1)}, f32[2048,128]{1,0:T(8,128)S(1)}) custom-call(f32[128,8,128]{2,1,0:T(8,128)S(1)} %get-tuple-element.68.after_ref.refs_1_.refs_3_, s32[128]{0:T(128)S(1)} %get-tuple-element.69.meta_ref, f32[2048,128]{1,0:T(8,128)S(1)} %get-tuple-element.100.refs_0_, f32[2048,128]{1,0:T(8,128)S(1)} %get-tuple-element.93.refs_0_.refs_1_, ...), custom_call_target="tpu_custom_call" | custom-call | flops 4000000000 | bytes 12000000 | tf_op jit(solution)/shard_map/inner/pallas_call | solution.py:650
  93.3 2.5 %collective-permute-start.24 = (f32[512,128]{1,0:T(8,128)S(1)}, f32[512,128]{1,0:T(8,128)S(1)}, u32[]{:S(2)}, u32[]{:S(2)}) collective-permute-start(f32[512,128]{1,0:T(8,128)S(1)} %get-tuple-element.118), channel_id=1, source_target_pairs={{0,24},{4,28},{8,16},{12,20},{16,8},{20,12},{24,0},{28,4},{1,25},{... | collective-permute-start | bytes 786440 | tf_op jit(solution)/shard_map/ppermute | solution.py:510
  98.1 2.5 %collective-permute-start.20 = (f32[512,128]{1,0:T(8,128)S(1)}, f32[512,128]{1,0:T(8,128)S(1)}, u32[]{:S(2)}, u32[]{:S(2)}) collective-permute-start(f32[512,128]{1,0:T(8,128)S(1)} %get-tuple-element.113), channel_id=1, source_target_pairs={{0,24},{4,28},{8,16},{12,20},{16,8},{20,12},{24,0},{28,4},{1,25},{... | collective-permute-start | bytes 786440 | tf_op jit(solution)/shard_map/ppermute | solution.py:510
  101.2 2.4 %collective-permute-done.24.refs_3_ = f32[512,128]{1,0:T(8,128)S(1)} collective-permute-done((f32[512,128]{1,0:T(8,128)S(1)}, f32[512,128]{1,0:T(8,128)S(1)}, u32[]{:S(2)}, u32[]{:S(2)}) %collective-permute-start.24) | collective-permute-done | bytes 262176 | tf_op jit(solution)/shard_map/ppermute | solution.py:510
  105.2 4.1 %collective-permute-done.23.refs_2_ = f32[512,128]{1,0:T(8,128)S(1)} collective-permute-done((f32[512,128]{1,0:T(8,128)S(1)}, f32[512,128]{1,0:T(8,128)S(1)}, u32[]{:S(2)}, u32[]{:S(2)}) %collective-permute-start.23) | collective-permute-done | bytes 262176 | tf_op jit(solution)/shard_map/ppermute | solution.py:510
  110.2 2.4 %collective-permute-done.20.refs_3_ = f32[512,128]{1,0:T(8,128)S(1)} collective-permute-done((f32[512,128]{1,0:T(8,128)S(1)}, f32[512,128]{1,0:T(8,128)S(1)}, u32[]{:S(2)}, u32[]{:S(2)}) %collective-permute-start.20) | collective-permute-done | bytes 262176 | tf_op jit(solution)/shard_map/ppermute | solution.py:510
  112.6 2.8 %collective-permute-done.19.refs_2_ = f32[512,128]{1,0:T(8,128)S(1)} collective-permute-done((f32[512,128]{1,0:T(8,128)S(1)}, f32[512,128]{1,0:T(8,128)S(1)}, u32[]{:S(2)}, u32[]{:S(2)}) %collective-permute-start.19) | collective-permute-done | bytes 262176 | tf_op jit(solution)/shard_map/ppermute | solution.py:510
  115.6 2.0 %gather.2 = (f32[4096,128]{1,0:T(8,128)}, f32[1,32,32]{2,1,0:T(8,128)S(1)}, bf16[32,64,256]{2,1,0:T(8,128)(2,1)S(1)}) custom-call(s32[2]{0:T(128)S(1)} %copy-done.3, f32[512,128]{1,0:T(8,128)S(1)} %get-tuple-element.115.refs_0_, f32[512,128]{1,0:T(8,128)S(1)} %collective-permute-done.22.refs_1_, f32[512,128]{1,0:T(8,128)S(1)} %collective-permute-done.23.refs_2_, ...), custom_call_target="tpu_custom_call" | custom-call | flops 2000000000 | bytes 6000000 | tf_op jit(solution)/shard_map/gather/pallas_call | solution.py:691
  117.6 2.2 %gather.3 = (f32[4096,128]{1,0:T(8,128)}, f32[2,32,32]{2,1,0:T(8,128)S(1)}) custom-call(s32[2]{0:T(128)S(1)} %copy-done.3, f32[512,128]{1,0:T(8,128)S(1)} %get-tuple-element.110.refs_0_, f32[512,128]{1,0:T(8,128)S(1)} %collective-permute-done.18.refs_1_, f32[512,128]{1,0:T(8,128)S(1)} %collective-permute-done.19.refs_2_, ...), custom_call_target="tpu_custom_call", output_to_operand_aliasing={{0}: (7, {})} | custom-call | flops 2000000000 | bytes 6000000 | tf_op jit(solution)/shard_map/gather/pallas_call | solution.py:691
  126.7 2.4 %collective-permute-done.29 = f32[64,64]{1,0:T(8,128)S(1)} collective-permute-done((f32[64,64]{1,0:T(8,128)S(1)}, f32[64,64]{1,0:T(8,128)S(1)}, u32[]{:S(2)}, u32[]{:S(2)}) %collective-permute-start.29) | collective-permute-done | bytes 16416 | tf_op jit(solution)/shard_map/ppermute | solution.py:510
  134.9 2.8 %collective-permute-done.32 = f32[16,64]{1,0:T(8,128)S(1)} collective-permute-done((f32[16,64]{1,0:T(8,128)S(1)}, f32[16,64]{1,0:T(8,128)S(1)}, u32[]{:S(2)}, u32[]{:S(2)}) %collective-permute-start.32) | collective-permute-done | bytes 4128 | tf_op jit(solution)/shard_map/ppermute | solution.py:513
  (116 shorter events, 47.8 us)
Async XLA Ops:
  3.0 3.0 %collective-permute-start = (f32[2048,128]{1,0:T(8,128)}, f32[2048,128]{1,0:T(8,128)S(1)}, u32[]{:S(2)}, u32[]{:S(2)}) collective-permute-start(f32[2048,128]{1,0:T(8,128)} %bitcast.11), channel_id=1, source_target_pairs={{0,4},{4,0},{8,12},{12,8},{16,20},{20,16},{24,28},{28,24},{1,5},{5... | collective-permute-start | bytes 3145736 | tf_op jit(solution)/shard_map/ppermute | solution.py:510
  4.4 1.4 %collective-permute-start.1 = (f32[104,128]{1,0:T(8,128)S(1)}, f32[104,128]{1,0:T(8,128)S(1)}, u32[]{:S(2)}, u32[]{:S(2)}) collective-permute-start(f32[104,128]{1,0:T(8,128)S(1)} %parts.1.after_ref.own_ref), channel_id=1, source_target_pairs={{0,4},{4,0},{8,12},{12,8},{16,20},{20,16},{24,28},{28,24},{1,5},{5... | collective-permute-start | bytes 159752 | tf_op jit(solution)/shard_map/ppermute | solution.py:510
  8.0 10.6 %collective-permute-start.2 = (f32[592,128]{1,0:T(8,128)}, f32[592,128]{1,0:T(8,128)S(1)}, u32[]{:S(2)}, u32[]{:S(2)}) collective-permute-start(f32[592,128]{1,0:T(8,128)} %get-tuple-element.63), channel_id=1, source_target_pairs={{0,8},{4,12},{8,0},{12,4},{16,24},{20,28},{24,16},{28,20},{1,9},{5... | collective-permute-start | bytes 909320 | tf_op jit(solution)/shard_map/ppermute | solution.py:510
  10.9 13.8 %collective-permute-start.3 = (f32[592,128]{1,0:T(8,128)}, f32[592,128]{1,0:T(8,128)}, u32[]{:S(2)}, u32[]{:S(2)}) collective-permute-start(f32[592,128]{1,0:T(8,128)} %get-tuple-element.65), channel_id=1, source_target_pairs={{0,16},{4,20},{8,24},{12,28},{16,0},{20,4},{24,8},{28,12},{1,17},{... | collective-permute-start | bytes 909320 | tf_op jit(solution)/shard_map/ppermute | solution.py:510
  12.4 14.9 %collective-permute-start.4 = (f32[592,128]{1,0:T(8,128)}, f32[592,128]{1,0:T(8,128)}, u32[]{:S(2)}, u32[]{:S(2)}) collective-permute-start(f32[592,128]{1,0:T(8,128)} %get-tuple-element.66), channel_id=1, source_target_pairs={{0,24},{4,28},{8,16},{12,20},{16,8},{20,12},{24,0},{28,4},{1,25},{... | collective-permute-start | bytes 909320 | tf_op jit(solution)/shard_map/ppermute | solution.py:510
  20.4 19.4 %collective-permute-start.7 = (f32[640,128]{1,0:T(8,128)S(1)}, f32[640,128]{1,0:T(8,128)S(1)}, u32[]{:S(2)}, u32[]{:S(2)}) collective-permute-start(f32[640,128]{1,0:T(8,128)S(1)} %get-tuple-element.64.after_ref), channel_id=1, source_target_pairs={{0,8},{4,12},{8,0},{12,4},{16,24},{20,28},{24,16},{28,20},{1,9},{5... | collective-permute-start | bytes 983048 | tf_op jit(solution)/shard_map/ppermute | solution.py:510
  22.2 18.4 %collective-permute-start.8 = (f32[640,128]{1,0:T(8,128)S(1)}, f32[640,128]{1,0:T(8,128)S(1)}, u32[]{:S(2)}, u32[]{:S(2)}) collective-permute-start(f32[640,128]{1,0:T(8,128)S(1)} %get-tuple-element.74), channel_id=1, source_target_pairs={{0,16},{4,20},{8,24},{12,28},{16,0},{20,4},{24,8},{28,12},{1,17},{... | collective-permute-start | bytes 983048 | tf_op jit(solution)/shard_map/ppermute | solution.py:510
  23.7 16.9 %collective-permute-start.9 = (f32[640,128]{1,0:T(8,128)S(1)}, f32[640,128]{1,0:T(8,128)S(1)}, u32[]{:S(2)}, u32[]{:S(2)}) collective-permute-start(f32[640,128]{1,0:T(8,128)S(1)} %get-tuple-element.75), channel_id=1, source_target_pairs={{0,24},{4,28},{8,16},{12,20},{16,8},{20,12},{24,0},{28,4},{1,25},{... | collective-permute-start | bytes 983048 | tf_op jit(solution)/shard_map/ppermute | solution.py:510
  29.4 20.9 %collective-permute-start.5 = (f32[16,8,128]{2,1,0:T(8,128)S(1)}, f32[16,8,128]{2,1,0:T(8,128)S(1)}, u32[]{:S(2)}, u32[]{:S(2)}) collective-permute-start(f32[16,8,128]{2,1,0:T(8,128)S(1)} %get-tuple-element.67.after_ref), channel_id=1, source_target_pairs={{0,1},{1,0},{2,3},{3,2},{4,5},{5,4},{6,7},{7,6},{8,9},{9,8},{10,11... | collective-permute-start | bytes 196616 | tf_op jit(solution)/shard_map/ppermute | solution.py:636
  31.5 18.8 %collective-permute-start.6 = (f32[16,8,128]{2,1,0:T(8,128)S(1)}, f32[16,8,128]{2,1,0:T(8,128)S(1)}, u32[]{:S(2)}, u32[]{:S(2)}) collective-permute-start(f32[16,8,128]{2,1,0:T(8,128)S(1)} %get-tuple-element.73), channel_id=1, source_target_pairs={{0,3},{1,2},{2,1},{3,0},{4,7},{5,6},{6,5},{7,4},{8,11},{9,10},{10,... | collective-permute-start | bytes 196616 | tf_op jit(solution)/shard_map/ppermute | solution.py:636
  45.5 10.2 %collective-permute-start.10 = (f32[16,8,128]{2,1,0:T(8,128)S(1)}, f32[16,8,128]{2,1,0:T(8,128)S(1)}, u32[]{:S(2)}, u32[]{:S(2)}) collective-permute-start(f32[16,8,128]{2,1,0:T(8,128)S(1)} %get-tuple-element.76.after_ref), channel_id=1, source_target_pairs={{0,1},{1,0},{2,3},{3,2},{4,5},{5,4},{6,7},{7,6},{8,9},{9,8},{10,11... | collective-permute-start | bytes 196616 | tf_op jit(solution)/shard_map/ppermute | solution.py:636
  47.1 8.6 %collective-permute-start.11 = (f32[16,8,128]{2,1,0:T(8,128)S(1)}, f32[16,8,128]{2,1,0:T(8,128)S(1)}, u32[]{:S(2)}, u32[]{:S(2)}) collective-permute-start(f32[16,8,128]{2,1,0:T(8,128)S(1)} %get-tuple-element.82), channel_id=1, source_target_pairs={{0,3},{1,2},{2,1},{3,0},{4,7},{5,6},{6,5},{7,4},{8,11},{9,10},{10,... | collective-permute-start | bytes 196616 | tf_op jit(solution)/shard_map/ppermute | solution.py:636
  57.7 7.2 %collective-permute-start.13 = (f32[32,8,128]{2,1,0:T(8,128)S(1)}, f32[32,8,128]{2,1,0:T(8,128)S(1)}, u32[]{:S(2)}, u32[]{:S(2)}) collective-permute-start(f32[32,8,128]{2,1,0:T(8,128)S(1)} %pad_maximum_fusion.3), channel_id=1, source_target_pairs={{0,3},{1,2},{2,1},{3,0},{4,7},{5,6},{6,5},{7,4},{8,11},{9,10},{10,... | collective-permute-start | bytes 393224 | tf_op jit(solution)/shard_map/ppermute | solution.py:642
  59.1 6.4 %collective-permute-start.12 = (f32[32,8,128]{2,1,0:T(8,128)S(1)}, f32[32,8,128]{2,1,0:T(8,128)S(1)}, u32[]{:S(2)}, u32[]{:S(2)}) collective-permute-start(f32[32,8,128]{2,1,0:T(8,128)S(1)} %pad_maximum_fusion.2), channel_id=1, source_target_pairs={{0,1},{1,0},{2,3},{3,2},{4,5},{5,4},{6,7},{7,6},{8,9},{9,8},{10,11... | collective-permute-start | bytes 393224 | tf_op jit(solution)/shard_map/ppermute | solution.py:642
  69.3 9.0 %collective-permute-start.15 = (f32[32,8,128]{2,1,0:T(8,128)S(1)}, f32[32,8,128]{2,1,0:T(8,128)S(1)}, u32[]{:S(2)}, u32[]{:S(2)}) collective-permute-start(f32[32,8,128]{2,1,0:T(8,128)S(1)} %pad_maximum_fusion.5), channel_id=1, source_target_pairs={{0,3},{1,2},{2,1},{3,0},{4,7},{5,6},{6,5},{7,4},{8,11},{9,10},{10,... | collective-permute-start | bytes 393224 | tf_op jit(solution)/shard_map/ppermute | solution.py:642
  71.3 6.9 %collective-permute-start.14 = (f32[32,8,128]{2,1,0:T(8,128)S(1)}, f32[32,8,128]{2,1,0:T(8,128)S(1)}, u32[]{:S(2)}, u32[]{:S(2)}) collective-permute-start(f32[32,8,128]{2,1,0:T(8,128)S(1)} %pad_maximum_fusion.4), channel_id=1, source_target_pairs={{0,1},{1,0},{2,3},{3,2},{4,5},{5,4},{6,7},{7,6},{8,9},{9,8},{10,11... | collective-permute-start | bytes 393224 | tf_op jit(solution)/shard_map/ppermute | solution.py:642
  82.1 9.9 %collective-permute-start.17 = (f32[32,8,128]{2,1,0:T(8,128)S(1)}, f32[32,8,128]{2,1,0:T(8,128)S(1)}, u32[]{:S(2)}, u32[]{:S(2)}) collective-permute-start(f32[32,8,128]{2,1,0:T(8,128)S(1)} %pad_maximum_fusion.7), channel_id=1, source_target_pairs={{0,3},{1,2},{2,1},{3,0},{4,7},{5,6},{6,5},{7,4},{8,11},{9,10},{10,... | collective-permute-start | bytes 393224 | tf_op jit(solution)/shard_map/ppermute | solution.py:642
  84.0 8.0 %collective-permute-start.16 = (f32[32,8,128]{2,1,0:T(8,128)S(1)}, f32[32,8,128]{2,1,0:T(8,128)S(1)}, u32[]{:S(2)}, u32[]{:S(2)}) collective-permute-start(f32[32,8,128]{2,1,0:T(8,128)S(1)} %pad_maximum_fusion.6), channel_id=1, source_target_pairs={{0,1},{1,0},{2,3},{3,2},{4,5},{5,4},{6,7},{7,6},{8,9},{9,8},{10,11... | collective-permute-start | bytes 393224 | tf_op jit(solution)/shard_map/ppermute | solution.py:642
  93.3 10.3 %collective-permute-start.24 = (f32[512,128]{1,0:T(8,128)S(1)}, f32[512,128]{1,0:T(8,128)S(1)}, u32[]{:S(2)}, u32[]{:S(2)}) collective-permute-start(f32[512,128]{1,0:T(8,128)S(1)} %get-tuple-element.118), channel_id=1, source_target_pairs={{0,24},{4,28},{8,16},{12,20},{16,8},{20,12},{24,0},{28,4},{1,25},{... | collective-permute-start | bytes 786440 | tf_op jit(solution)/shard_map/ppermute | solution.py:510
  95.8 13.4 %collective-permute-start.23 = (f32[512,128]{1,0:T(8,128)S(1)}, f32[512,128]{1,0:T(8,128)S(1)}, u32[]{:S(2)}, u32[]{:S(2)}) collective-permute-start(f32[512,128]{1,0:T(8,128)S(1)} %get-tuple-element.117), channel_id=1, source_target_pairs={{0,16},{4,20},{8,24},{12,28},{16,0},{20,4},{24,8},{28,12},{1,17},{... | collective-permute-start | bytes 786440 | tf_op jit(solution)/shard_map/ppermute | solution.py:510
  96.4 13.7 %collective-permute-start.22 = (f32[512,128]{1,0:T(8,128)S(1)}, f32[512,128]{1,0:T(8,128)S(1)}, u32[]{:S(2)}, u32[]{:S(2)}) collective-permute-start(f32[512,128]{1,0:T(8,128)S(1)} %get-tuple-element.116), channel_id=1, source_target_pairs={{0,8},{4,12},{8,0},{12,4},{16,24},{20,28},{24,16},{28,20},{1,9},{5... | collective-permute-start | bytes 786440 | tf_op jit(solution)/shard_map/ppermute | solution.py:510
  98.1 14.5 %collective-permute-start.20 = (f32[512,128]{1,0:T(8,128)S(1)}, f32[512,128]{1,0:T(8,128)S(1)}, u32[]{:S(2)}, u32[]{:S(2)}) collective-permute-start(f32[512,128]{1,0:T(8,128)S(1)} %get-tuple-element.113), channel_id=1, source_target_pairs={{0,24},{4,28},{8,16},{12,20},{16,8},{20,12},{24,0},{28,4},{1,25},{... | collective-permute-start | bytes 786440 | tf_op jit(solution)/shard_map/ppermute | solution.py:510
  100.6 14.8 %collective-permute-start.19 = (f32[512,128]{1,0:T(8,128)S(1)}, f32[512,128]{1,0:T(8,128)S(1)}, u32[]{:S(2)}, u32[]{:S(2)}) collective-permute-start(f32[512,128]{1,0:T(8,128)S(1)} %get-tuple-element.112), channel_id=1, source_target_pairs={{0,16},{4,20},{8,24},{12,28},{16,0},{20,4},{24,8},{28,12},{1,17},{... | collective-permute-start | bytes 786440 | tf_op jit(solution)/shard_map/ppermute | solution.py:510
  103.6 11.8 %collective-permute-start.18 = (f32[512,128]{1,0:T(8,128)S(1)}, f32[512,128]{1,0:T(8,128)S(1)}, u32[]{:S(2)}, u32[]{:S(2)}) collective-permute-start(f32[512,128]{1,0:T(8,128)S(1)} %get-tuple-element.111), channel_id=1, source_target_pairs={{0,8},{4,12},{8,0},{12,4},{16,24},{20,28},{24,16},{28,20},{1,9},{5... | collective-permute-start | bytes 786440 | tf_op jit(solution)/shard_map/ppermute | solution.py:510
  110.1 5.5 %collective-permute-start.25 = (f32[1024,128]{1,0:T(8,128)S(1)}, f32[1024,128]{1,0:T(8,128)S(1)}, u32[]{:S(2)}, u32[]{:S(2)}) collective-permute-start(f32[1024,128]{1,0:T(8,128)S(1)} %pad_maximum_fusion.1), channel_id=1, source_target_pairs={{0,4},{4,0},{8,12},{12,8},{16,20},{20,16},{24,28},{28,24},{1,5},{5... | collective-permute-start | bytes 1572872 | tf_op jit(solution)/shard_map/ppermute | solution.py:510
  115.5 2.1 %collective-permute-start.21 = (f32[1024,128]{1,0:T(8,128)S(1)}, f32[1024,128]{1,0:T(8,128)S(1)}, u32[]{:S(2)}, u32[]{:S(2)}) collective-permute-start(f32[1024,128]{1,0:T(8,128)S(1)} %pad_maximum_fusion), channel_id=1, source_target_pairs={{0,4},{4,0},{8,12},{12,8},{16,20},{20,16},{24,28},{28,24},{1,5},{5... | collective-permute-start | bytes 1572872 | tf_op jit(solution)/shard_map/ppermute | solution.py:510
  121.4 3.9 %collective-permute-start.27 = (f32[64,64]{1,0:T(8,128)S(1)}, f32[64,64]{1,0:T(8,128)S(1)}, u32[]{:S(2)}, u32[]{:S(2)}) collective-permute-start(f32[64,64]{1,0:T(8,128)S(1)} %fusion), channel_id=1, source_target_pairs={{0,8},{4,12},{8,0},{12,4},{16,24},{20,28},{24,16},{28,20},{1,9},{5... | collective-permute-start | bytes 49160 | tf_op jit(solution)/shard_map/ppermute | solution.py:510
  122.7 3.9 %collective-permute-start.28 = (f32[64,64]{1,0:T(8,128)S(1)}, f32[64,64]{1,0:T(8,128)S(1)}, u32[]{:S(2)}, u32[]{:S(2)}) collective-permute-start(f32[64,64]{1,0:T(8,128)S(1)} %fusion), channel_id=1, source_target_pairs={{0,16},{4,20},{8,24},{12,28},{16,0},{20,4},{24,8},{28,12},{1,17},{... | collective-permute-start | bytes 49160 | tf_op jit(solution)/shard_map/ppermute | solution.py:510
  124.2 4.8 %collective-permute-start.29 = (f32[64,64]{1,0:T(8,128)S(1)}, f32[64,64]{1,0:T(8,128)S(1)}, u32[]{:S(2)}, u32[]{:S(2)}) collective-permute-start(f32[64,64]{1,0:T(8,128)S(1)} %fusion), channel_id=1, source_target_pairs={{0,24},{4,28},{8,16},{12,20},{16,8},{20,12},{24,0},{28,4},{1,25},{... | collective-permute-start | bytes 49160 | tf_op jit(solution)/shard_map/ppermute | solution.py:510
  129.1 4.5 %collective-permute-start.30 = (f32[16,64]{1,0:T(8,128)S(1)}, f32[16,64]{1,0:T(8,128)S(1)}, u32[]{:S(2)}, u32[]{:S(2)}) collective-permute-start(f32[16,64]{1,0:T(8,128)S(1)} %get-tuple-element.124), channel_id=1, source_target_pairs={{0,1},{1,0},{2,3},{3,2},{4,5},{5,4},{6,7},{7,6},{8,9},{9,8},{10,11... | collective-permute-start | bytes 12296 | tf_op jit(solution)/shard_map/ppermute | solution.py:513
  130.3 4.5 %collective-permute-start.31 = (f32[16,64]{1,0:T(8,128)S(1)}, f32[16,64]{1,0:T(8,128)S(1)}, u32[]{:S(2)}, u32[]{:S(2)}) collective-permute-start(f32[16,64]{1,0:T(8,128)S(1)} %get-tuple-element.126), channel_id=1, source_target_pairs={{0,2},{1,3},{2,0},{3,1},{4,6},{5,7},{6,4},{7,5},{8,10},{9,11},{10,... | collective-permute-start | bytes 12296 | tf_op jit(solution)/shard_map/ppermute | solution.py:513
  132.2 5.4 %collective-permute-start.32 = (f32[16,64]{1,0:T(8,128)S(1)}, f32[16,64]{1,0:T(8,128)S(1)}, u32[]{:S(2)}, u32[]{:S(2)}) collective-permute-start(f32[16,64]{1,0:T(8,128)S(1)} %get-tuple-element.125), channel_id=1, source_target_pairs={{0,3},{1,2},{2,1},{3,0},{4,7},{5,6},{6,5},{7,4},{8,11},{9,10},{10,... | collective-permute-start | bytes 12296 | tf_op jit(solution)/shard_map/ppermute | solution.py:513
  (12 other events, 42.7 us)
